TPU v7x, 32 devices: a whole 2x2x4 slice. The times are simulated.
32 devices in a mesh: ctx: 16 (over z, y, x), head: 2 (over core).
Axes of the slice: x: 2, y: 2, z: 4, core: 2. Of those that a mesh axis runs over, the one named last changes fastest.
Arguments:
- window_queries: bfloat16 [4096, 4096], P('ctx', 'head'), may hold values from -260 to 260
- window_keys: bfloat16 [4096, 512], P('ctx', 'head'), may hold values from -7 to 7
- window_values: bfloat16 [4096, 512], P('ctx', 'head'), may hold values from -6 to 6
- out_weight: bfloat16 [4096, 2880], P('head'), may hold values from -0.09375 to 0.09375
- norm_gain: float32 [2880], replicated, may hold values from 0.5 to 1.5
- query_weight: bfloat16 [2880, 4096], P(None, 'head'), may hold values from -4.5280377 to 4.5280377
- key_weight: bfloat16 [2880, 512], P(None, 'head'), may hold values from -0.1118034 to 0.1118034
- value_weight: bfloat16 [2880, 512], P(None, 'head'), may hold values from -0.109375 to 0.109375
- doc_lengths: int32 [32], replicated, may hold values from 1 to 256, as said below
Outputs:
- first_branch: bfloat16 [4096, 2880], P(('ctx', 'head'))
- causal_out: bfloat16 [4096, 4096], P('ctx', 'head')
Inputs may be any that keep to these rules, and one draw needn't show every extreme that they name: `doc_lengths`: the first two documents cover 256 / 2 positions together; each following pair of documents except the last two covers exactly 256 positions; the second-to-last document has exactly 256 positions and the last 128.
All inputs are finite; a program needn't handle non-finite values.
Results may differ from a plain program's by a relative error of at most 0.025.
Values may be sent and summed in bfloat16 or wider, within the bound.
No kernel may reach another device: no remote copies, remote signals or barrier semaphores. Data moves between devices by JAX's collectives and lax.ppermute only.
A program may use at most 128 MiB of HBM per device.

v0:
```python
import jax
import jax.numpy as jnp
from jax import lax
from jax.sharding import PartitionSpec as P

HD = 64
WIN = 128


def shifted(block, axis, distance):
    devices = range(lax.axis_size(axis))
    route = [(i - distance, i) for i in devices if i - distance in devices]
    return lax.ppermute(block, axis, route)


def doc_index(positions, doc_lengths):
    starts = jnp.cumsum(doc_lengths) - doc_lengths
    return jnp.sum((positions[:, None] >= starts[None, :]).astype(jnp.int32), axis=1) - 1


def head_scores(queries, key_part, kv_heads, groups):
    row_count = queries.shape[0]
    query_four = queries.reshape(row_count, kv_heads, groups, HD)
    key_three = key_part.reshape(key_part.shape[0], kv_heads, HD)
    return jnp.einsum(
        "rkgd,lkd->kgrl", query_four, key_three, preferred_element_type=jnp.float32
    ) * HD ** (-0.5)


def window_attend(queries, key_part, value_part, allowed, kv_heads, groups):
    row_count = queries.shape[0]
    scores = jnp.where(allowed[None, None], head_scores(queries, key_part, kv_heads, groups), -1e30)
    highest = jnp.max(scores, axis=-1, keepdims=True)
    exponent = jnp.where(allowed[None, None], jnp.exp(scores - highest), 0.0)
    denominator = jnp.sum(exponent, axis=-1)
    value_three = value_part.reshape(value_part.shape[0], kv_heads, HD)
    weighted = jnp.einsum(
        "kgrl,lkd->rkgd",
        exponent.astype(jnp.bfloat16),
        value_three,
        preferred_element_type=jnp.float32,
    )
    result = weighted / jnp.transpose(denominator, (2, 0, 1))[..., None]
    return result.reshape(row_count, -1).astype(jnp.bfloat16)


def normalize(branch, norm_gain):
    return (
        branch * lax.rsqrt(jnp.mean(branch * branch, axis=-1, keepdims=True) + 1e-05) * norm_gain
    ).astype(jnp.bfloat16)


def local(
    window_queries,
    window_keys,
    window_values,
    out_weight,
    norm_gain,
    query_weight,
    key_weight,
    value_weight,
    doc_lengths,
):
    row_count = window_queries.shape[0]
    kv_width = window_keys.shape[1]
    kv_heads = kv_width // HD
    groups = window_queries.shape[1] // kv_width
    anchor = lax.axis_index("ctx") * row_count
    own_pos = anchor + jnp.arange(row_count, dtype=jnp.int32)
    own_doc = doc_index(own_pos, doc_lengths)
    key_values = jnp.concatenate([window_keys, window_values], axis=1)
    before = shifted(key_values[row_count - WIN :], "ctx", 1)
    window = jnp.concatenate([before, key_values], axis=0)

    def window_piece(block_index):
        first = block_index * row_count
        query_pos = anchor + first + jnp.arange(row_count, dtype=jnp.int32)
        key_pos = anchor + first - WIN + jnp.arange(row_count + WIN, dtype=jnp.int32)
        query_doc = doc_index(query_pos, doc_lengths)
        key_doc = doc_index(key_pos, doc_lengths)
        allowed = (
            (key_doc[None, :] == query_doc[:, None])
            & (key_pos[None, :] <= query_pos[:, None])
            & (key_pos[None, :] > query_pos[:, None] - WIN)
        )
        return window_attend(
            window_queries, window[:, :kv_width], window[:, kv_width:], allowed, kv_heads, groups
        )

    window_out = lax.map(window_piece, jnp.arange(row_count // row_count, dtype=jnp.int32)).reshape(
        row_count, -1
    )
    branch = lax.psum_scatter(
        jnp.dot(window_out, out_weight, preferred_element_type=jnp.float32).astype(jnp.bfloat16),
        "head",
        scatter_dimension=0,
        tiled=True,
    ).astype(jnp.float32)
    normed = normalize(branch, norm_gain)
    normed_part = lax.all_gather(normed, "head", axis=0, tiled=True)
    projected = jnp.concatenate(
        [
            jnp.dot(normed_part, query_weight, preferred_element_type=jnp.float32),
            jnp.dot(normed_part, key_weight, preferred_element_type=jnp.float32),
            jnp.dot(normed_part, value_weight, preferred_element_type=jnp.float32),
        ],
        axis=1,
    ).astype(jnp.bfloat16)
    query_width = window_queries.shape[1]
    causal_queries = projected[:, :query_width]
    causal_pairs = projected[:, query_width:]

    def fold_keys(fold_state, kv_piece, first_row):
        row_total = kv_piece.shape[0]
        block_total = row_total // row_total
        tiles = kv_piece.reshape(block_total, row_total, kv_piece.shape[1])

        def advance(inner_state, block_item):
            block_index, key_tile = block_item
            first_key = first_row + block_index * row_total
            tile_pos = first_key + jnp.arange(row_total, dtype=jnp.int32)
            tile_doc = doc_index(tile_pos, doc_lengths)
            skipped = (first_key > own_pos[-1]) | (tile_doc[-1] < own_doc[0])

            def update(state_now):
                running_max, denominator, weighted = state_now
                permitted = (tile_doc[None, :] == own_doc[:, None]) & (
                    tile_pos[None, :] <= own_pos[:, None]
                )
                scores = jnp.where(
                    permitted[None, None],
                    head_scores(causal_queries, key_tile[:, :kv_width], kv_heads, groups),
                    -1e30,
                )
                new_max = jnp.maximum(running_max, jnp.max(scores, axis=-1))
                rescale = jnp.exp(running_max - new_max)
                exponent = jnp.where(
                    permitted[None, None], jnp.exp(scores - new_max[..., None]), 0.0
                )
                value_three = key_tile[:, kv_width:].reshape(row_total, kv_heads, HD)
                added = jnp.einsum(
                    "kgrl,lkd->kgrd",
                    exponent.astype(jnp.bfloat16),
                    value_three,
                    preferred_element_type=jnp.float32,
                )
                return (
                    new_max,
                    denominator * rescale + jnp.sum(exponent, axis=-1),
                    weighted * rescale[..., None] + added,
                )

            return (lax.cond(skipped, lambda state_now: state_now, update, inner_state), None)

        fold_state, _ = lax.scan(
            advance, fold_state, (jnp.arange(block_total, dtype=jnp.int32), tiles)
        )
        return fold_state

    initial = (
        jnp.full((kv_heads, groups, row_count), -1e30, jnp.float32),
        jnp.zeros((kv_heads, groups, row_count), jnp.float32),
        jnp.zeros((kv_heads, groups, row_count, HD), jnp.float32),
    )
    fold_state = fold_keys(initial, causal_pairs, anchor)
    earlier = shifted(causal_pairs, "ctx", 1)
    fold_state = fold_keys(fold_state, earlier, anchor - row_count)
    running_max, denominator, weighted = fold_state
    causal_out = (
        jnp.transpose(weighted / denominator[..., None], (2, 0, 1, 3))
        .reshape(row_count, -1)
        .astype(jnp.bfloat16)
    )
    return (branch.astype(jnp.bfloat16), causal_out)


def solution(mesh):
    placed = (
        P("ctx", "head"),
        P("ctx", "head"),
        P("ctx", "head"),
        P("head", None),
        P(),
        P(None, "head"),
        P(None, "head"),
        P(None, "head"),
        P(),
    )
    return jax.shard_map(
        local,
        mesh=mesh,
        in_specs=placed,
        out_specs=(P(("ctx", "head"), None), P("ctx", "head")),
        check_vma=False,
    )
```

profile of v0, /device:TPU:3, one launch (start us, length us, event | category | flops | bytes accessed | tf_op | source)
XLA Modules:
  0.0 104.8 jit_solution(6019318090620048537)
XLA Ops:
  7.2 1.0 constant_dynamic-update-slice_fusion.1
  8.2 0.9 constant_dynamic-update-slice_fusion
  9.2 3.1 %collective-permute-start = (bf16[128,512]{1,0:T(8,128)(2,1)S(1)}, bf16[128,512]{1,0:T(8,128)(2,1)S(1)}, u32[]{:S(2)}, u32[]{:S(2)}) collective-permute-start(bf16[128,512]{1,0:T(8,128)(2,1)S(1)} %slice.58), channel_id=1, source_target_pairs={{0,2},{2,4},{4,6},{6,8},{8,10},{10,12},{12,14},{14,16},{16,18},{18... | collective-permute-start | bytes 393224 | tf_op jit(solution)/shard_map/ppermute | solution.py:13
  12.3 0.7 copy.44
  14.1 1.5 %copy.46 = bf16[256,2048]{0,1:T(8,128)(2,1)S(1)} copy(bf16[256,2048]{1,0:T(8,128)(2,1)} %param.13) | data formatting | bytes 2097152 | tf_op args[0]
  16.2 7.2 %fusion.43 = (f32[4,8,256]{2,1,0:T(8,128)S(1)}, bf16[4,8,256,384]{2,3,1,0:T(8,128)(2,1)}) fusion(pred[256,384]{0,1:T(8,128)(4,1)S(1)} %compare_and_fusion.2, bf16[384,4,64,1]{0,2,3,1:T(8,128)(2,1)S(1)} %bitcast.110, bf16[256,4,8,64]{0,3,2,1:T(8,128)(2,1)S(1)} %bitcast.107), kind=kOutput, calls=%fused_computation.76 | convolution fusion | flops 421527936 | bytes 7667712 | tf_op jit(solution)/shard_map/while/body/eval_jaxpr/sub | solution.py:34
  23.3 4.0 %fusion.29 = bf16[256,4,8,64]{0,3,2,1:T(8,128)(2,1)S(1)} fusion(bf16[384,4,64,1]{0,2,3,1:T(8,128)(2,1)S(1)} %bitcast.111, bf16[4,8,256,384]{2,3,1,0:T(8,128)(2,1)} %get-tuple-element.281, f32[256,4,8]{0,2,1:T(8,128)S(1)} %bitcast.116), kind=kOutput, calls=%fused_computation.42 | convolution fusion | flops 403701760 | bytes 7569408 | tf_op jit(solution)/shard_map/while/body/eval_jaxpr/kgrl,lkd->rkgd/dot_general | solution.py:37
  27.4 7.6 %convolution_convert_fusion = bf16[256,2880]{0,1:T(8,128)(2,1)S(1)} fusion(bf16[2048,2880]{0,1:T(8,128)(2,1)} %param.16, bf16[256,2048]{0,1:T(8,128)(2,1)S(1)} %bitcast.115), kind=kOutput, calls=%fused_computation.39 | convolution fusion | flops 3020636160 | bytes 14319616 | tf_op jit(solution)/shard_map/dot_general | solution.py:94
  35.0 1.7 %copy.60 = bf16[256,2880]{1,0:T(8,128)(2,1)} copy(bf16[256,2880]{0,1:T(8,128)(2,1)S(1)} %convolution_convert_fusion) | data formatting | bytes 2949120
  36.8 11.5 %reduce-scatter.4.cloned.1.call-done = bf16[128,2880]{1,0:T(8,128)(2,1)} async-done(((bf16[256,2880]{1,0:T(8,128)(2,1)}), bf16[128,2880]{1,0:T(8,128)(2,1)}) %reduce-scatter.4.cloned.1.call-update) | async-done | bytes 737296
  48.3 1.5 %copy.61 = bf16[128,2880]{0,1:T(8,128)(2,1)S(1)} copy(bf16[128,2880]{1,0:T(8,128)(2,1)} %reduce-scatter.4.cloned.1.call-done) | data formatting | bytes 1474560
  50.2 1.3 %fusion.34 = bf16[128,2880]{0,1:T(8,128)(2,1)} fusion(bf16[128,2880]{0,1:T(8,128)(2,1)S(1)} %copy.61, f32[2880]{0:T(1024)S(1)} %copy-done.8, f32[128]{0:T(128)S(1)} %add_rsqrt_fusion), kind=kLoop, calls=%fused_computation.48 | loop fusion | flops 1474560 | bytes 1486592 | tf_op jit(solution)/shard_map/convert_element_type | solution.py:50
  57.5 1.6 %broadcast_in_dim.129 = f32[4,8,256,64]{2,3,1,0:T(8,128)} broadcast(f32[]{:T(128)} %constant.107.clone.1), dimensions={} | broadcast | bytes 2097156 | tf_op jit(solution)/shard_map/broadcast_in_dim | solution.py:163
  59.1 3.4 %all-gather.2.cloned.1.call-done = bf16[256,2880]{0,1:T(8,128)(2,1)} async-done(((bf16[128,2880]{0,1:T(8,128)(2,1)}), bf16[256,2880]{0,1:T(8,128)(2,1)}) %all-gather.2.cloned.1.call-update) | async-done | bytes 1474576 | tf_op jit(solution)/shard_map/all_gather | solution.py:100
  62.5 2.2 %convolution_convert_fusion.2 = bf16[256,256]{0,1:T(8,128)(2,1)S(1)} fusion(bf16[256,2880]{0,1:T(8,128)(2,1)} %all-gather.2.cloned.1.call-done, bf16[2880,256]{1,0:T(8,128)(2,1)S(1)} %copy-done), kind=kOutput, calls=%fused_computation.50 | convolution fusion | flops 377552896 | bytes 3080192 | tf_op jit(solution)/shard_map/dot_general | solution.py:105
  64.7 2.5 %convolution_convert_fusion.3 = bf16[256,256]{0,1:T(8,128)(2,1)S(1)} fusion(bf16[256,2880]{0,1:T(8,128)(2,1)} %all-gather.2.cloned.1.call-done, bf16[2880,256]{1,0:T(8,128)(2,1)} %param.19), kind=kOutput, calls=%fused_computation.51 | convolution fusion | flops 377552896 | bytes 3080192 | tf_op jit(solution)/shard_map/dot_general | solution.py:104
  67.2 0.7 pad_maximum_fusion
  67.9 3.3 %collective-permute-start.1 = (bf16[256,512]{0,1:T(8,128)(2,1)}, bf16[256,512]{0,1:T(8,128)(2,1)S(1)}, u32[]{:S(2)}, u32[]{:S(2)}) collective-permute-start(bf16[256,512]{0,1:T(8,128)(2,1)} %pad_maximum_fusion), channel_id=1, source_target_pairs={{0,2},{2,4},{4,6},{6,8},{8,10},{10,12},{12,14},{14,16},{16,18},{18... | collective-permute-start | bytes 786440 | tf_op jit(solution)/shard_map/ppermute | solution.py:13
  71.2 6.5 %convolution_convert_fusion.1 = bf16[256,2048]{1,0:T(8,128)(2,1)S(1)} fusion(bf16[256,2880]{0,1:T(8,128)(2,1)S(1)} %copy-done.7, bf16[2880,2048]{1,0:T(8,128)(2,1)} %param.18), kind=kOutput, calls=%fused_computation.40 | convolution fusion | flops 3020423168 | bytes 14319616 | tf_op jit(solution)/shard_map/dot_general | solution.py:103
  77.7 8.9 %conditional.2 = (f32[4,8,256]{2,1,0:T(8,128)S(1)}, f32[4,8,256]{2,1,0:T(8,128)S(1)}, f32[4,8,256,64]{2,3,1,0:T(8,128)}) conditional(s32[]{:T(128)} %convert_element_type.72, (s32[256]{0:T(256)S(1)}, s32[]{:T(128)}, s32[256]{0:T(256)S(1)}, s32[256]{0:T(256)S(1)}, bf16[256,512]{0,1:T(8,128)(2,1)}, /*index=5*/bf16[256,2048]{1,0:T(8,128)(2,1)S(1)}, ...), branch_computations={%region_8.11_spmd, %region_11.12_spmd} | conditional | flops 565395712 | bytes 50795604 | solution.py:153
  77.9 1.0 fusion.40
  79.4 1.4 %fusion = (f32[4,8,256]{2,1,0:T(8,128)S(1)}, f32[4,256,256,8]{2,1,3,0:T(8,128)S(1)}) fusion(pred[256,256]{0,1:T(8,128)(4,1)S(1)} %compare_and_fusion, bf16[256,4,64,1]{0,2,3,1:T(8,128)(2,1)S(1)} %bitcast.108, bf16[256,4,8,64]{0,3,2,1:T(8,128)(2,1)S(1)} %bitcast.104), kind=kOutput, calls=%fused_computation.2 | convolution fusion | flops 274718720 | bytes 9666560 | tf_op jit(solution)/shard_map/while/body/eval_jaxpr/cond/branch_0_fun/rkgd,lkd->kgrl/dot_general | solution.py:25
  80.8 2.1 %fusion.2 = f32[4,8,256]{2,1,0:T(8,128)S(1)} fusion(f32[4,256,256,8]{2,1,3,0:T(8,128)S(1)} %get-tuple-element.271, f32[4,8,256]{2,1,0:T(8,128)S(1)} %max.5, pred[256,256]{0,1:T(8,128)(4,1)S(1)} %compare_and_fusion), kind=kLoop, calls=%fused_computation.4 | loop fusion | flops 10477568 | bytes 8519680 | tf_op jit(solution)/shard_map/while/body/eval_jaxpr/cond/branch_0_fun/reduce_sum | solution.py:149
  83.0 2.3 %multiply_add_fusion = f32[4,8,256,64]{2,3,1,0:T(8,128)S(1)} fusion(f32[4,8,256,64]{2,3,1,0:T(8,128)S(1)} %copy-done.2, bf16[256,4,64,1]{0,2,3,1:T(8,128)(2,1)S(1)} %bitcast.112, f32[4,256,256,8]{2,1,3,0:T(8,128)S(1)} %get-tuple-element.271, f32[4,8,256]{2,1,0:T(8,128)S(1)} %max.5, pred[256,256]{0,1:T(8,128)(4,1)S(1)} %compare_and_fusion, ...), kind=kOutput, calls=%fused_computation.7 | convolution fusion | flops 279969792 | bytes 12845056 | tf_op jit(solution)/shard_map/while/body/eval_jaxpr/cond/branch_0_fun/kgrl,lkd->kgrd/dot_general | solution.py:141
  85.3 1.3 %copy-done.3 = f32[4,8,256,64]{2,3,1,0:T(8,128)} copy-done((f32[4,8,256,64]{2,3,1,0:T(8,128)}, f32[4,8,256,64]{2,3,1,0:T(8,128)S(1)}, u32[]{:S(2)}) %copy-start.3) | copy-done | bytes 2097176 | tf_op jit(solution)/shard_map/while/body/eval_jaxpr/cond
  86.6 7.9 %conditional.3 = ((f32[4,8,256]{2,1,0:T(8,128)S(1)}, f32[4,8,256,64]{2,3,1,0:T(8,128)})) conditional(s32[]{:T(128)} %convert_element_type.69, (s32[256]{0:T(256)S(1)}, s32[256]{0:T(256)S(1)}, s32[]{:T(128)}, s32[256]{0:T(256)S(1)}, s32[256]{0:T(256)S(1)}, /*index=5*/bf16[256,512]{0,1:T(8,128)(2,1)S(1)}, bf16[256,2048]{1,0:T(8,128)(2,1)S(1)}, ...), branch_computations={%region_12.15_spmd, %region_15.16_spmd} | conditional | flops 565395712 | bytes 50796628 | solution.py:153
  87.4 1.4 %fusion.11 = (f32[4,8,256]{2,1,0:T(8,128)S(1)}, f32[4,256,256,8]{2,1,3,0:T(8,128)S(1)}) fusion(pred[256,256]{0,1:T(8,128)(4,1)S(1)} %compare_and_fusion.1, bf16[256,4,64,1]{0,2,3,1:T(8,128)(2,1)S(1)} %bitcast.109, bf16[256,4,8,64]{0,3,2,1:T(8,128)(2,1)S(1)} %bitcast.105), kind=kOutput, calls=%fused_computation.17 | convolution fusion | flops 274718720 | bytes 9666560 | tf_op jit(solution)/shard_map/while/body/eval_jaxpr/cond/branch_0_fun/rkgd,lkd->kgrl/dot_general | solution.py:25
  88.7 2.1 %fusion.13 = f32[4,8,256]{2,1,0:T(8,128)S(1)} fusion(f32[4,256,256,8]{2,1,3,0:T(8,128)S(1)} %get-tuple-element.275, f32[4,8,256]{2,1,0:T(8,128)S(1)} %max.6, pred[256,256]{0,1:T(8,128)(4,1)S(1)} %compare_and_fusion.1), kind=kLoop, calls=%fused_computation.19 | loop fusion | flops 10477568 | bytes 8519680 | tf_op jit(solution)/shard_map/while/body/eval_jaxpr/cond/branch_0_fun/reduce_sum | solution.py:149
  90.9 2.3 %multiply_add_fusion.2 = f32[4,8,256,64]{2,3,1,0:T(8,128)S(1)} fusion(f32[4,8,256,64]{2,3,1,0:T(8,128)S(1)} %copy-done.4, bf16[256,4,64,1]{0,2,3,1:T(8,128)(2,1)S(1)} %bitcast.113, f32[4,256,256,8]{2,1,3,0:T(8,128)S(1)} %get-tuple-element.275, f32[4,8,256]{2,1,0:T(8,128)S(1)} %max.6, pred[256,256]{0,1:T(8,128)(4,1)S(1)} %compare_and_fusion.1, ...), kind=kOutput, calls=%fused_computation.22 | convolution fusion | flops 279969792 | bytes 12845056 | tf_op jit(solution)/shard_map/while/body/eval_jaxpr/cond/branch_0_fun/kgrl,lkd->kgrd/dot_general | solution.py:141
  93.2 1.3 %copy-done.5 = f32[4,8,256,64]{2,3,1,0:T(8,128)} copy-done((f32[4,8,256,64]{2,3,1,0:T(8,128)}, f32[4,8,256,64]{2,3,1,0:T(8,128)S(1)}, u32[]{:S(2)}) %copy-start.5) | copy-done | bytes 2097176 | tf_op jit(solution)/shard_map/while/body/eval_jaxpr/cond
  94.5 2.0 %divide_convert_fusion = bf16[4,8,256,64]{2,3,1,0:T(8,128)(2,1)S(1)} fusion(f32[4,8,256,64]{2,3,1,0:T(8,128)} %get-tuple-element.178, f32[4,8,256]{2,1,0:T(8,128)S(1)} %get-tuple-element.179), kind=kLoop, calls=%fused_computation.43 | loop fusion | flops 1048576 | bytes 3178496 | tf_op jit(solution)/shard_map/convert_element_type | solution.py:172
  96.5 1.4 %copy.50 = bf16[256,2048]{1,0:T(8,128)(2,1)} copy(bf16[256,2048]{0,1:T(8,128)(2,1)S(1)} %bitcast.106) | data formatting | bytes 2097152
  (58 shorter events, 5.6 us)
Async XLA Ops:
  7.2 55.3 %copy-start = (bf16[2880,256]{1,0:T(8,128)(2,1)S(1)}, bf16[2880,256]{1,0:T(8,128)(2,1)}, u32[]{:S(2)}) copy-start(bf16[2880,256]{1,0:T(8,128)(2,1)} %param.20) | copy-start | bytes 4423684
  7.2 41.1 %reduce-scatter.4.cloned.1.call-start = ((), (), s32[]{:S(2)}) async-start(), calls=%async_computation.2 | async-start | bytes 2260992
  9.2 6.6 %collective-permute-start = (bf16[128,512]{1,0:T(8,128)(2,1)S(1)}, bf16[128,512]{1,0:T(8,128)(2,1)S(1)}, u32[]{:S(2)}, u32[]{:S(2)}) collective-permute-start(bf16[128,512]{1,0:T(8,128)(2,1)S(1)} %slice.58), channel_id=1, source_target_pairs={{0,2},{2,4},{4,6},{6,8},{8,10},{10,12},{12,14},{14,16},{16,18},{18... | collective-permute-start | bytes 393224 | tf_op jit(solution)/shard_map/ppermute | solution.py:13
  27.4 22.9 %copy-start.8 = (f32[2880]{0:T(1024)S(1)}, f32[2880]{0:T(1024)}, u32[]{:S(2)}) copy-start(f32[2880]{0:T(1024)} %param.17) | copy-start | bytes 34564
  36.7 25.7 %all-gather.2.cloned.1.call-start = ((), (), s32[]{:S(2)}) async-start(), calls=%async_computation.1 | async-start | bytes 2211840 | tf_op jit(solution)/shard_map/all_gather | solution.py:100
  49.8 27.9 %copy-start.6 = (bf16[128,2880]{0,1:T(8,128)(2,1)}, bf16[128,2880]{0,1:T(8,128)(2,1)S(1)}, u32[]{:S(2)}) copy-start(bf16[128,2880]{0,1:T(8,128)(2,1)S(1)} %copy.61) | copy-start | bytes 2211844
  62.5 8.7 %copy-start.7 = (bf16[256,2880]{0,1:T(8,128)(2,1)S(1)}, bf16[256,2880]{0,1:T(8,128)(2,1)}, u32[]{:S(2)}) copy-start(bf16[256,2880]{0,1:T(8,128)(2,1)} %all-gather.2.cloned.1.call-done) | copy-start | bytes 4423684
  67.9 18.7 %collective-permute-start.1 = (bf16[256,512]{0,1:T(8,128)(2,1)}, bf16[256,512]{0,1:T(8,128)(2,1)S(1)}, u32[]{:S(2)}, u32[]{:S(2)}) collective-permute-start(bf16[256,512]{0,1:T(8,128)(2,1)} %pad_maximum_fusion), channel_id=1, source_target_pairs={{0,2},{2,4},{4,6},{6,8},{8,10},{10,12},{12,14},{14,16},{16,18},{18... | collective-permute-start | bytes 786440 | tf_op jit(solution)/shard_map/ppermute | solution.py:13
  79.4 3.5 %copy-start.2 = (f32[4,8,256,64]{2,3,1,0:T(8,128)S(1)}, f32[4,8,256,64]{2,3,1,0:T(8,128)}, u32[]{:S(2)}) copy-start(f32[4,8,256,64]{2,3,1,0:T(8,128)} %get-tuple-element.157) | copy-start | bytes 6291460 | tf_op jit(solution)/shard_map/while/body/eval_jaxpr/cond
  85.3 1.4 %copy-start.3 = (f32[4,8,256,64]{2,3,1,0:T(8,128)}, f32[4,8,256,64]{2,3,1,0:T(8,128)S(1)}, u32[]{:S(2)}) copy-start(f32[4,8,256,64]{2,3,1,0:T(8,128)S(1)} %multiply_add_fusion) | copy-start | bytes 6291460 | tf_op jit(solution)/shard_map/while/body/eval_jaxpr/cond
  87.3 3.5 %copy-start.4 = (f32[4,8,256,64]{2,3,1,0:T(8,128)S(1)}, f32[4,8,256,64]{2,3,1,0:T(8,128)}, u32[]{:S(2)}) copy-start(f32[4,8,256,64]{2,3,1,0:T(8,128)} %get-tuple-element.167) | copy-start | bytes 6291460 | tf_op jit(solution)/shard_map/while/body/eval_jaxpr/cond
  93.2 1.4 %copy-start.5 = (f32[4,8,256,64]{2,3,1,0:T(8,128)}, f32[4,8,256,64]{2,3,1,0:T(8,128)S(1)}, u32[]{:S(2)}) copy-start(f32[4,8,256,64]{2,3,1,0:T(8,128)S(1)} %multiply_add_fusion.2) | copy-start | bytes 6291460 | tf_op jit(solution)/shard_map/while/body/eval_jaxpr/cond
  94.5 3.4 %copy-start.1 = (bf16[2880,256]{1,0:T(8,128)(2,1)S(1)}, bf16[2880,256]{1,0:T(8,128)(2,1)}, u32[]{:S(2)}) copy-start(bf16[2880,256]{1,0:T(8,128)(2,1)} %param.20) | copy-start | bytes 4423684
Sparse Core Ops, SparseCore 0:
  36.9 11.4 reduce-scatter.3
  51.7 10.7 all-gather.1
where the time goes:
time: 105 us
  matrix products  37.3 us (36%)
  between operations  18.1 us (17%)
  local copies, waits for them, and re-layouts  17.5 us (17%)
  waiting for transfers between devices  15 us (14%)
  other arithmetic  10.2 us (10%)
  starting transfers between devices  6.46 us (6%)
    unnamed x3, waiting for transfers between devices  11.6 us
    dot_general x1, matrix products, local(): jnp.dot(window_out, out_weight, preferred_element_type=jnp.float32)  7.6 us
    unnamed x15, local copies, waits for them, and re-layouts  7.16 us
    sub x1, matrix products, window_attend(): exponent = jnp.where(allowed[None, None], jnp.exp(scores - highest), 0.0)  7.16 us
    dot_general x1, matrix products, local(): jnp.dot(normed_part, query_weight, preferred_element_type=jnp.float32)  6.53 us
    ppermute x2, starting transfers between devices, shifted(): return lax.ppermute(block, axis, route)  6.38 us
    dot_general x2, matrix products, update(): jnp.einsum('kgrl,lkd->kgrd', exponent.astype(jnp.bfloat16), value_three,...  4.57 us
    reduce_sum x2, other arithmetic, update(): jnp.sum(exponent, axis=-1)  4.24 us
  transfers between devices with their start and end apart: 4, of which 2 were waited for; matrix products, arithmetic and copies ran while one was open for 20% of the time, Pallas kernels for 0%

commit v1 on v0

v1 whole, which is shorter than its diff:
```python
import functools

import jax
import jax.numpy as jnp
from jax import lax
from jax.experimental import pallas as pl
from jax.experimental.pallas import tpu as pltpu
from jax.sharding import PartitionSpec as P

HD = 64
WIN = 128
LANES = 128
NEG = -1e30
TAIL = 16

F32 = jnp.float32
BF16 = jnp.bfloat16
MIB = 1024 * 1024


def params(mib):
    return pltpu.CompilerParams(vmem_limit_bytes=mib * MIB)


def in_vmem(array):
    return pltpu.with_memory_space_constraint(array, pltpu.VMEM)


def vmem_specs(count):
    return [pl.BlockSpec(memory_space=pltpu.VMEM)] * count


SMEM_SPEC = pl.BlockSpec(memory_space=pltpu.SMEM)


def dot(a, b, dims):
    return lax.dot_general(a, b, (dims, ((), ())), preferred_element_type=F32)


def shifted(block, axis):
    size = lax.axis_size(axis)
    return lax.ppermute(block, axis, [(i, i + 1) for i in range(size - 1)])


def swapped(block, axis):
    size = lax.axis_size(axis)
    return lax.ppermute(block, axis, [(i, size - 1 - i) for i in range(size)])


def lower_bias(lengths_ref, half, width):
    ctx = lax.axis_index("ctx")
    first = jnp.where(ctx == 0, half, 0)
    split = first + lengths_ref[2 * ctx]
    return bias_of(2 * half, half, half, first, split, width)


def upper_bias(lengths_ref, half, width):
    ctx = lax.axis_index("ctx")
    last = lengths_ref.shape[0] - 1
    split = lengths_ref[jnp.minimum(2 * ctx + 2, last)]
    split = jnp.where(ctx == lax.axis_size("ctx") - 1, 2 * half, split)
    return bias_of(half, half, 0, 0, split, width)


def bias_of(keys, rows, row_offset, first, split, width):
    key = lax.broadcasted_iota(jnp.int32, (keys, rows), 0)
    row = lax.broadcasted_iota(jnp.int32, (keys, rows), 1) + row_offset
    lowest = jnp.where(row >= split, split, first)
    if width is not None:
        lowest = jnp.maximum(lowest, row - (width - 1))
    return jnp.where((key >= lowest) & (key <= row), 0.0, NEG).astype(F32)


def stage_keys(keys, keys_ref):
    scaled = (keys.astype(F32) * HD ** (-0.5)).astype(BF16)
    lane = lax.broadcasted_iota(jnp.int32, (keys.shape[0], LANES), 1)
    zero = jnp.zeros((keys.shape[0], LANES), BF16)
    for pair in range(keys.shape[1] // LANES):
        tile = scaled[:, pair * LANES : (pair + 1) * LANES]
        turned = jnp.concatenate([tile[:, HD:], tile[:, :HD]], axis=1)
        keys_ref[2 * pair, 0] = jnp.where(lane < HD, tile, zero)
        keys_ref[2 * pair, 1] = jnp.where(lane < HD, zero, turned)
        keys_ref[2 * pair + 1, 0] = jnp.where(lane < HD, turned, zero)
        keys_ref[2 * pair + 1, 1] = jnp.where(lane < HD, zero, tile)


def stage_values(values, values_ref):
    count = values.shape[0]
    turned = jnp.transpose(values.astype(F32)).astype(BF16)
    for head in range(values.shape[1] // HD):
        values_ref[head, :HD, :] = turned[head * HD : (head + 1) * HD]
        values_ref[head, HD:, :] = jnp.ones((TAIL, count), BF16)


def attend_head(key_tile, value_tile, query_pair, bias):
    scores = dot(key_tile, query_pair, ((1,), (1,))) + bias
    highest = jnp.max(scores, axis=0, keepdims=True)
    pattern = jnp.exp(scores - highest).astype(BF16)
    weighted = dot(value_tile, pattern, ((1,), (0,)))
    return weighted[:HD] * (1.0 / weighted[HD : HD + 1])


def window_heads(q_ref, rows, keys_ref, values_ref, bias_ref, out_ref, columns):
    kv_heads = keys_ref.shape[0]
    pairs = q_ref.shape[1] // kv_heads // LANES

    def one(g, carry):
        for t in range(pairs):
            lane = pl.multiple_of((g * pairs + t) * LANES, LANES)
            query_pair = q_ref[rows, pl.ds(lane, LANES)]
            for side in range(2):
                part = attend_head(keys_ref[g, side], values_ref[g], query_pair, bias_ref[...])
                start = pl.multiple_of(lane + side * HD, HD)
                out_ref[pl.ds(start, HD), columns] = part.astype(BF16)
        return carry

    lax.fori_loop(0, kv_heads, one, 0)


def causal_heads(q_ref, rows, keys_ref, values_ref, bias_ref, out_ref, out_rows):
    kv_heads = keys_ref.shape[0]
    pairs = q_ref.shape[1] // kv_heads // LANES

    def one(g, carry):
        for t in range(pairs):
            lane = pl.multiple_of((g * pairs + t) * LANES, LANES)
            query_pair = q_ref[rows, pl.ds(lane, LANES)]
            both = [
                attend_head(keys_ref[g, side], values_ref[g], query_pair, bias_ref[...])
                for side in range(2)
            ]
            turned = jnp.transpose(jnp.concatenate(both, axis=0))
            out_ref[out_rows, pl.ds(lane, LANES)] = turned.astype(BF16)
        return carry

    lax.fori_loop(0, kv_heads, one, 0)


def window_upper_kernel(lengths_ref, q_ref, k_ref, v_ref, out_ref, keys_s, values_s, bias_s):
    half = q_ref.shape[0] // 2
    bias_s[...] = upper_bias(lengths_ref, half, WIN)
    stage_keys(k_ref[half:], keys_s)
    stage_values(v_ref[half:], values_s)
    window_heads(q_ref, pl.ds(half, half), keys_s, values_s, bias_s, out_ref, slice(None))


def window_lower_kernel(
    lengths_ref, q_ref, k_ref, v_ref, halo_ref, upper_ref, weight_ref, out_ref,
    attn_s, keys_s, values_s, bias_s, *, chunk
):
    half = q_ref.shape[0] // 2
    kv_width = k_ref.shape[1]
    bias_s[...] = lower_bias(lengths_ref, half, WIN)
    stage_keys(jnp.concatenate([halo_ref[:, :kv_width], k_ref[:half]], axis=0), keys_s)
    stage_values(jnp.concatenate([halo_ref[:, kv_width:], v_ref[:half]], axis=0), values_s)
    attn_s[:, half:] = upper_ref[...]
    window_heads(q_ref, pl.ds(0, half), keys_s, values_s, bias_s, attn_s, pl.ds(0, half))

    def project(c, carry):
        rows = pl.ds(pl.multiple_of(c * chunk, 16), chunk)
        out_ref[rows, :] = dot(weight_ref[rows, :], attn_s[...], ((1,), (0,))).astype(BF16)
        return carry

    lax.fori_loop(0, out_ref.shape[0] // chunk, project, 0)


def norm_kernel(
    own_ref, other_ref, gain_ref, kw_ref, vw_ref, branch_ref, normed_ref, kv_ref, sum_s, *, chunk
):
    width, rows = own_ref.shape
    half = rows // 2
    head = lax.axis_index("head")

    def add(c, squares):
        part = pl.ds(pl.multiple_of(c * chunk, 16), chunk)
        total = own_ref[part, :].astype(F32) + other_ref[part, :].astype(F32)
        sum_s[part, :] = total
        branch_ref[part, :] = jnp.where(head == 0, total[:, :half], total[:, half:]).astype(BF16)
        return squares + jnp.sum(total * total, axis=0, keepdims=True)

    squares = lax.fori_loop(0, width // chunk, add, jnp.zeros((1, rows), F32))
    factor = lax.rsqrt(squares * (1.0 / width) + 1e-05)
    for first in range(0, width, LANES):
        last = min(first + LANES, width)
        piece = jnp.transpose(sum_s[first:last, :] * factor) * gain_ref[:, first:last]
        normed_ref[:, first:last] = piece.astype(BF16)
    kv_width = kw_ref.shape[1]
    kv_ref[:, :kv_width] = dot(normed_ref[...], kw_ref[...], ((1,), (0,))).astype(BF16)
    kv_ref[:, kv_width:] = dot(normed_ref[...], vw_ref[...], ((1,), (0,))).astype(BF16)


def query_kernel(
    lengths_ref, normed_ref, qw_ref, kv_ref, q_ref, out_ref, keys_s, values_s, bias_s, *, chunk
):
    half = normed_ref.shape[0] // 2
    kv_width = kv_ref.shape[1] // 2
    for first in range(0, qw_ref.shape[1], chunk):
        columns = slice(first, first + chunk)
        q_ref[:, columns] = dot(normed_ref[...], qw_ref[:, columns], ((1,), (0,))).astype(BF16)
    bias_s[...] = upper_bias(lengths_ref, half, None)
    stage_keys(kv_ref[half:, :kv_width], keys_s)
    stage_values(kv_ref[half:, kv_width:], values_s)
    causal_heads(q_ref, pl.ds(half, half), keys_s, values_s, bias_s, out_ref, slice(None))


def causal_lower_kernel(
    lengths_ref, q_ref, kv_ref, halo_ref, upper_ref, out_ref, keys_s, values_s, bias_s
):
    half = q_ref.shape[0] // 2
    kv_width = kv_ref.shape[1] // 2
    bias_s[...] = lower_bias(lengths_ref, half, None)
    stage_keys(
        jnp.concatenate([halo_ref[:, :kv_width], kv_ref[:half, :kv_width]], axis=0), keys_s
    )
    stage_values(
        jnp.concatenate([halo_ref[:, kv_width:], kv_ref[:half, kv_width:]], axis=0), values_s
    )
    out_ref[half:, :] = upper_ref[...]
    causal_heads(q_ref, pl.ds(0, half), keys_s, values_s, bias_s, out_ref, pl.ds(0, half))


def attention_scratch(kv_heads, keys, rows):
    return [
        pltpu.VMEM((kv_heads, 2, keys, LANES), BF16),
        pltpu.VMEM((kv_heads, HD + TAIL, keys), BF16),
        pltpu.VMEM((keys, rows), F32),
    ]


def local(
    window_queries,
    window_keys,
    window_values,
    out_weight,
    norm_gain,
    query_weight,
    key_weight,
    value_weight,
    doc_lengths,
):
    rows, q_width = window_queries.shape
    kv_width = window_keys.shape[1]
    kv_heads = kv_width // HD
    width = out_weight.shape[1]
    half = rows // 2

    halo = shifted(jnp.concatenate([window_keys[half:], window_values[half:]], axis=1), "ctx")
    upper = pl.pallas_call(
        window_upper_kernel,
        out_shape=jax.ShapeDtypeStruct((q_width, half), BF16),
        in_specs=[SMEM_SPEC] + vmem_specs(3),
        out_specs=vmem_specs(1)[0],
        scratch_shapes=attention_scratch(kv_heads, half, half),
        compiler_params=params(16),
        name="window_upper",
    )(doc_lengths, window_queries, window_keys, window_values)
    partial = pl.pallas_call(
        functools.partial(window_lower_kernel, chunk=576),
        out_shape=jax.ShapeDtypeStruct((width, rows), BF16),
        in_specs=[SMEM_SPEC] + vmem_specs(6),
        out_specs=vmem_specs(1)[0],
        scratch_shapes=[pltpu.VMEM((q_width, rows), BF16)]
        + attention_scratch(kv_heads, 2 * half, half),
        compiler_params=params(16),
        name="window_lower",
    )(
        doc_lengths, window_queries, window_keys, window_values, halo, upper,
        in_vmem(jnp.transpose(out_weight)),
    )
    other = swapped(partial, "head")
    branch, normed, pairs = pl.pallas_call(
        functools.partial(norm_kernel, chunk=192),
        out_shape=(
            jax.ShapeDtypeStruct((width, half), BF16),
            jax.ShapeDtypeStruct((rows, width), BF16),
            jax.ShapeDtypeStruct((rows, 2 * kv_width), BF16),
        ),
        in_specs=vmem_specs(5),
        out_specs=tuple(vmem_specs(3)),
        scratch_shapes=[pltpu.VMEM((width, rows), F32)],
        compiler_params=params(16),
        name="norm_and_pairs",
    )(
        partial, other, norm_gain.reshape(1, width),
        in_vmem(key_weight), in_vmem(value_weight),
    )
    earlier = shifted(pairs[half:], "ctx")
    queries, causal_upper = pl.pallas_call(
        functools.partial(query_kernel, chunk=512),
        out_shape=(
            jax.ShapeDtypeStruct((rows, q_width), BF16),
            jax.ShapeDtypeStruct((half, q_width), BF16),
        ),
        in_specs=[SMEM_SPEC] + vmem_specs(3),
        out_specs=tuple(vmem_specs(2)),
        scratch_shapes=attention_scratch(kv_heads, half, half),
        compiler_params=params(16),
        name="queries_and_upper",
    )(doc_lengths, normed, in_vmem(query_weight), pairs)
    causal_out = pl.pallas_call(
        causal_lower_kernel,
        out_shape=jax.ShapeDtypeStruct((rows, q_width), BF16),
        in_specs=[SMEM_SPEC] + vmem_specs(4),
        out_specs=vmem_specs(1)[0],
        scratch_shapes=attention_scratch(kv_heads, 2 * half, half),
        compiler_params=params(16),
        name="causal_lower",
    )(doc_lengths, queries, pairs, earlier, causal_upper)
    return (jnp.transpose(branch), causal_out)


def solution(mesh):
    placed = (
        P("ctx", "head"),
        P("ctx", "head"),
        P("ctx", "head"),
        P("head", None),
        P(),
        P(None, "head"),
        P(None, "head"),
        P(None, "head"),
        P(),
    )
    return jax.shard_map(
        local,
        mesh=mesh,
        in_specs=placed,
        out_specs=(P(("ctx", "head"), None), P("ctx", "head")),
        check_vma=False,
    )
```

time: 105 us -> 60.2 us (0.57)
  the two profiles are of different devices: /device:TPU:3 before, /device:TPU:0 now
where the time goes in v1:
time: 60.2 us; the launch traced here: 59.9 us
  Pallas kernels  37.8 us (63%)
  local copies, waits for them, and re-layouts  9.76 us (16%)
  starting transfers between devices  8.31 us (14%)
  waiting for transfers between devices  3.22 us (5%)
  between operations  0.78 us (1%)
    pallas_call x1, Pallas kernels, local(): pl.pallas_call(functools.partial(query_kernel, chunk=512), out_shape=(jax...  11.5 us
    pallas_call x1, Pallas kernels, local(): pl.pallas_call(functools.partial(window_lower_kernel, chunk=576), out_sha...  9.58 us
    ppermute x2, starting transfers between devices, shifted(): return lax.ppermute(block, axis, [(i, i + 1) for i in range(size - 1)])  8.24 us
    unnamed x20, local copies, waits for them, and re-layouts  8.05 us
    pallas_call x1, Pallas kernels, local(): pl.pallas_call(window_upper_kernel, out_shape=jax.ShapeDtypeStruct((q_wid...  7.71 us
    pallas_call x1, Pallas kernels, local(): pl.pallas_call(causal_lower_kernel, out_shape=jax.ShapeDtypeStruct((rows,...  6.97 us
    ppermute x1, waiting for transfers between devices, swapped(): return lax.ppermute(block, axis, [(i, size - 1 - i) for i in range(size)])  3.22 us
    pallas_call x1, Pallas kernels, local(): pl.pallas_call(functools.partial(norm_kernel, chunk=192), out_shape=(jax....  2.03 us
  transfers between devices with their start and end apart: 3, of which 1 were waited for; matrix products, arithmetic and copies ran while one was open for 0% of the time, Pallas kernels for 32%

profile of v1, /device:TPU:0, one launch (start us, length us, event | category | flops | bytes accessed | tf_op | source)
XLA Modules:
  0.0 59.9 jit_solution(9733263546253223815)
XLA Ops:
  0.6 0.8 %slice.9 = bf16[128,256]{1,0:T(8,128)(2,1)S(1)} slice(bf16[256,256]{1,0:T(8,128)(2,1)} %k_ref.3), slice={[128:256], [0:256]} | slice | bytes 131072 | tf_op jit(solution)/shard_map/slice | solution.py:247
  1.5 0.8 %slice.10 = bf16[128,256]{1,0:T(8,128)(2,1)S(1)} slice(bf16[256,256]{1,0:T(8,128)(2,1)} %v_ref.3), slice={[128:256], [0:256]} | slice | bytes 131072 | tf_op jit(solution)/shard_map/slice | solution.py:247
  2.3 4.8 %collective-permute-start = (bf16[128,512]{1,0:T(8,128)(2,1)S(1)}, bf16[128,512]{1,0:T(8,128)(2,1)S(1)}, u32[]{:S(2)}, u32[]{:S(2)}) collective-permute-start(bf16[128,512]{1,0:T(8,128)(2,1)S(1)} %pad_maximum_fusion), channel_id=1, source_target_pairs={{0,2},{2,4},{4,6},{6,8},{8,10},{10,12},{12,14},{14,16},{16,18},{18... | collective-permute-start | bytes 393224 | tf_op jit(solution)/shard_map/ppermute | solution.py:42
  7.2 0.0 copy-start.2
  7.2 1.2 %copy-done.2 = bf16[256,2048]{1,0:T(8,128)(2,1)S(1)} copy-done((bf16[256,2048]{1,0:T(8,128)(2,1)S(1)}, bf16[256,2048]{1,0:T(8,128)(2,1)}, u32[]{:S(2)}) %copy-start.2) | copy-done | bytes 1048600
  8.4 0.0 copy-start.5
  8.4 0.9 %copy-done.5 = bf16[256,256]{1,0:T(8,128)(2,1)S(1)} copy-done((bf16[256,256]{1,0:T(8,128)(2,1)S(1)}, bf16[256,256]{1,0:T(8,128)(2,1)}, u32[]{:S(2)}) %copy-start.5) | copy-done | bytes 131096
  9.3 0.0 copy-start.6
  9.3 0.9 %copy-done.6 = bf16[256,256]{1,0:T(8,128)(2,1)S(1)} copy-done((bf16[256,256]{1,0:T(8,128)(2,1)S(1)}, bf16[256,256]{1,0:T(8,128)(2,1)}, u32[]{:S(2)}) %copy-start.6) | copy-done | bytes 131096
  10.2 0.0 copy-start.7
  10.2 0.7 %copy-done.7 = s32[32]{0:T(128)S(1)} copy-done((s32[32]{0:T(128)S(1)}, s32[32]{0:T(128)}, u32[]{:S(2)}) %copy-start.7) | copy-done | bytes 152
  10.9 7.7 %window_upper.1.upper_ref = bf16[2048,128]{1,0:T(8,128)(2,1)S(1)} custom-call(s32[32]{0:T(128)S(1)} %copy-done.7, bf16[256,2048]{1,0:T(8,128)(2,1)S(1)} %copy-done.2, bf16[256,256]{1,0:T(8,128)(2,1)S(1)} %copy-done.5, bf16[256,256]{1,0:T(8,128)(2,1)S(1)} %copy-done.6), custom_call_target="tpu_custom_call" | custom-call | tf_op jit(solution)/shard_map/window_upper/pallas_call | solution.py:248
  18.6 0.0 collective-permute-done.halo_ref
  18.6 0.0 copy-start
  18.6 4.3 %copy-done = bf16[2048,2880]{0,1:T(8,128)(2,1)S(1)} copy-done((bf16[2048,2880]{0,1:T(8,128)(2,1)S(1)}, bf16[2048,2880]{0,1:T(8,128)(2,1)}, u32[]{:S(2)}) %copy-start) | copy-done | bytes 11796504
  23.0 0.0 copy-start.9
  23.0 0.0 copy-start.3
  23.0 0.0 copy-start.4
  23.0 9.6 %window_lower.1.own_ref = bf16[2880,256]{1,0:T(8,128)(2,1)S(1)} custom-call(s32[32]{0:T(128)S(1)} %copy-done.7, bf16[256,2048]{1,0:T(8,128)(2,1)S(1)} %copy-done.2, bf16[256,256]{1,0:T(8,128)(2,1)S(1)} %copy-done.5, bf16[256,256]{1,0:T(8,128)(2,1)S(1)} %copy-done.6, bf16[128,512]{1,0:T(8,128)(2,1)S(1)} %collective-permute-done.halo_ref, ...), custom_call_target="tpu_custom_call" | custom-call | tf_op jit(solution)/shard_map/window_lower/pallas_call | solution.py:257
  32.6 0.1 collective-permute-start.1
  32.6 0.0 copy-done.9
  32.7 0.0 copy-start.8
  32.7 3.2 %collective-permute-done.1.other_ref = bf16[2880,256]{1,0:T(8,128)(2,1)S(1)} collective-permute-done((bf16[2880,256]{1,0:T(8,128)(2,1)S(1)}, bf16[2880,256]{1,0:T(8,128)(2,1)S(1)}, u32[]{:S(2)}, u32[]{:S(2)}) %collective-permute-start.1) | collective-permute-done | bytes 1474592 | tf_op jit(solution)/shard_map/ppermute | solution.py:47
  35.9 0.0 copy-done.3
  35.9 0.0 copy-done.4
  35.9 2.0 %norm_and_pairs.1 = (bf16[2880,128]{1,0:T(8,128)(2,1)}, bf16[256,2880]{1,0:T(8,128)(2,1)S(1)}, bf16[256,512]{1,0:T(8,128)(2,1)S(1)}) custom-call(bf16[2880,256]{1,0:T(8,128)(2,1)S(1)} %window_lower.1.own_ref, bf16[2880,256]{1,0:T(8,128)(2,1)S(1)} %collective-permute-done.1.other_ref, f32[1,2880]{1,0:T(1,128)S(1)} %reshape.7.gain_ref, ...), custom_call_target="tpu_custom_call" | custom-call | tf_op jit(solution)/shard_map/norm_and_pairs/pallas_call | solution.py:271
  38.0 3.4 %collective-permute-start.2 = (bf16[128,512]{1,0:T(8,128)(2,1)S(1)}, bf16[128,512]{1,0:T(8,128)(2,1)S(1)}, u32[]{:S(2)}, u32[]{:S(2)}) collective-permute-start(bf16[128,512]{1,0:T(8,128)(2,1)S(1)} %slice.11), channel_id=1, source_target_pairs={{0,2},{2,4},{4,6},{6,8},{8,10},{10,12},{12,14},{14,16},{16,18},{18... | collective-permute-start | bytes 393224 | tf_op jit(solution)/shard_map/ppermute | solution.py:42
  41.4 0.0 copy-done.1
  41.4 0.0 copy-done.8
  41.4 11.5 %queries_and_upper.1 = (bf16[256,2048]{1,0:T(8,128)(2,1)S(1)}, bf16[128,2048]{1,0:T(8,128)(2,1)S(1)}) custom-call(s32[32]{0:T(128)S(1)} %copy-done.8, bf16[256,2880]{1,0:T(8,128)(2,1)S(1)} %get-tuple-element.8.normed_ref, bf16[2880,2048]{1,0:T(8,128)(2,1)S(1)} %copy-done.1, bf16[256,512]{1,0:T(8,128)(2,1)S(1)} %get-tuple-element.9.kv_ref), custom_call_target="tpu_custom_call" | custom-call | tf_op jit(solution)/shard_map/queries_and_upper/pallas_call | solution.py:288
  52.9 0.0 collective-permute-done.2.halo_ref
  52.9 7.0 %causal_lower.1 = bf16[256,2048]{1,0:T(8,128)(2,1)} custom-call(s32[32]{0:T(128)S(1)} %copy-done.8, bf16[256,2048]{1,0:T(8,128)(2,1)S(1)} %get-tuple-element.10.q_ref, bf16[256,512]{1,0:T(8,128)(2,1)S(1)} %get-tuple-element.9.kv_ref, bf16[128,512]{1,0:T(8,128)(2,1)S(1)} %collective-permute-done.2.halo_ref, bf16[128,2048]{1,0:T(8,128)(2,1)S(1)} %get-tuple-element.11.upper_ref), custom_call_target="tpu_custom_call" | custom-call | tf_op jit(solution)/shard_map/causal_lower/pallas_call | solution.py:300
  (4 shorter events, 0.0 us)
Async XLA Ops:
  2.3 16.3 %collective-permute-start = (bf16[128,512]{1,0:T(8,128)(2,1)S(1)}, bf16[128,512]{1,0:T(8,128)(2,1)S(1)}, u32[]{:S(2)}, u32[]{:S(2)}) collective-permute-start(bf16[128,512]{1,0:T(8,128)(2,1)S(1)} %pad_maximum_fusion), channel_id=1, source_target_pairs={{0,2},{2,4},{4,6},{6,8},{8,10},{10,12},{12,14},{14,16},{16,18},{18... | collective-permute-start | bytes 393224 | tf_op jit(solution)/shard_map/ppermute | solution.py:42
  7.2 1.2 %copy-start.2 = (bf16[256,2048]{1,0:T(8,128)(2,1)S(1)}, bf16[256,2048]{1,0:T(8,128)(2,1)}, u32[]{:S(2)}) copy-start(bf16[256,2048]{1,0:T(8,128)(2,1)} %q_ref.3) | copy-start | bytes 3145732
  8.4 0.9 %copy-start.5 = (bf16[256,256]{1,0:T(8,128)(2,1)S(1)}, bf16[256,256]{1,0:T(8,128)(2,1)}, u32[]{:S(2)}) copy-start(bf16[256,256]{1,0:T(8,128)(2,1)} %k_ref.3) | copy-start | bytes 393220
  9.3 0.9 %copy-start.6 = (bf16[256,256]{1,0:T(8,128)(2,1)S(1)}, bf16[256,256]{1,0:T(8,128)(2,1)}, u32[]{:S(2)}) copy-start(bf16[256,256]{1,0:T(8,128)(2,1)} %v_ref.3) | copy-start | bytes 393220
  10.2 0.7 %copy-start.7 = (s32[32]{0:T(128)S(1)}, s32[32]{0:T(128)}, u32[]{:S(2)}) copy-start(s32[32]{0:T(128)} %lengths_ref.7) | copy-start | bytes 388
  18.6 4.4 %copy-start = (bf16[2048,2880]{0,1:T(8,128)(2,1)S(1)}, bf16[2048,2880]{0,1:T(8,128)(2,1)}, u32[]{:S(2)}) copy-start(bf16[2048,2880]{0,1:T(8,128)(2,1)} %param.12) | copy-start | bytes 35389444
  23.0 9.7 %copy-start.9 = (f32[2880]{0:T(1024)S(1)}, f32[2880]{0:T(1024)}, u32[]{:S(2)}) copy-start(f32[2880]{0:T(1024)} %param.13) | copy-start | bytes 34564
  23.0 12.9 %copy-start.3 = (bf16[2880,256]{1,0:T(8,128)(2,1)S(1)}, bf16[2880,256]{1,0:T(8,128)(2,1)}, u32[]{:S(2)}) copy-start(bf16[2880,256]{1,0:T(8,128)(2,1)} %kw_ref.1) | copy-start | bytes 4423684
  23.0 12.9 %copy-start.4 = (bf16[2880,256]{1,0:T(8,128)(2,1)S(1)}, bf16[2880,256]{1,0:T(8,128)(2,1)}, u32[]{:S(2)}) copy-start(bf16[2880,256]{1,0:T(8,128)(2,1)} %vw_ref.1) | copy-start | bytes 4423684
  23.0 18.4 %copy-start.1 = (bf16[2880,2048]{1,0:T(8,128)(2,1)S(1)}, bf16[2880,2048]{1,0:T(8,128)(2,1)}, u32[]{:S(2)}) copy-start(bf16[2880,2048]{1,0:T(8,128)(2,1)} %qw_ref.1) | copy-start | bytes 35389444
  32.6 3.3 %collective-permute-start.1 = (bf16[2880,256]{1,0:T(8,128)(2,1)S(1)}, bf16[2880,256]{1,0:T(8,128)(2,1)S(1)}, u32[]{:S(2)}, u32[]{:S(2)}) collective-permute-start(bf16[2880,256]{1,0:T(8,128)(2,1)S(1)} %window_lower.1.own_ref), channel_id=1, source_target_pairs={{0,1},{1,0},{2,3},{3,2},{4,5},{5,4},{6,7},{7,6},{8,9},{9,8},{10,11... | collective-permute-start | bytes 4423688 | tf_op jit(solution)/shard_map/ppermute | solution.py:47
  32.7 8.7 %copy-start.8 = (s32[32]{0:T(128)S(1)}, s32[32]{0:T(128)}, u32[]{:S(2)}) copy-start(s32[32]{0:T(128)} %lengths_ref.7) | copy-start | bytes 388
  38.0 14.9 %collective-permute-start.2 = (bf16[128,512]{1,0:T(8,128)(2,1)S(1)}, bf16[128,512]{1,0:T(8,128)(2,1)S(1)}, u32[]{:S(2)}, u32[]{:S(2)}) collective-permute-start(bf16[128,512]{1,0:T(8,128)(2,1)S(1)} %slice.11), channel_id=1, source_target_pairs={{0,2},{2,4},{4,6},{6,8},{8,10},{10,12},{12,14},{14,16},{16,18},{18... | collective-permute-start | bytes 393224 | tf_op jit(solution)/shard_map/ppermute | solution.py:42

commit v2 on v1

v2 whole, which is shorter than its diff:
```python
import functools

import jax
import jax.numpy as jnp
from jax import lax
from jax.experimental import pallas as pl
from jax.experimental.pallas import tpu as pltpu
from jax.sharding import PartitionSpec as P

HD = 64
WIN = 128
LANES = 128
NEG = -1e30
TAIL = 16

F32 = jnp.float32
BF16 = jnp.bfloat16
MIB = 1024 * 1024


def params(mib):
    return pltpu.CompilerParams(vmem_limit_bytes=mib * MIB)


def in_vmem(array):
    return pltpu.with_memory_space_constraint(array, pltpu.VMEM)


def in_hbm(array):
    return pltpu.with_memory_space_constraint(array, pltpu.HBM)


def hbm_specs(count):
    return [pl.BlockSpec(memory_space=pltpu.HBM)] * count


def vmem_specs(count):
    return [pl.BlockSpec(memory_space=pltpu.VMEM)] * count


def dot(a, b, dims):
    return lax.dot_general(a, b, (dims, ((), ())), preferred_element_type=F32)


def shifted(block, axis):
    size = lax.axis_size(axis)
    return lax.ppermute(block, axis, [(i, (i + 1) % size) for i in range(size)])


def swapped(block, axis):
    size = lax.axis_size(axis)
    return lax.ppermute(block, axis, [(i, size - 1 - i) for i in range(size)])


def lower_bias(lengths_ref, half, width):
    ctx = lax.axis_index("ctx")
    first = jnp.where(ctx == 0, half, 0)
    split = first + lengths_ref[2 * ctx]
    return bias_of(2 * half, half, half, first, split, width)


def upper_bias(lengths_ref, half, width):
    ctx = lax.axis_index("ctx")
    last = lengths_ref.shape[0] - 1
    split = lengths_ref[jnp.minimum(2 * ctx + 2, last)]
    split = jnp.where(ctx == lax.axis_size("ctx") - 1, 2 * half, split)
    return bias_of(half, half, 0, 0, split, width)


def bias_of(keys, rows, row_offset, first, split, width):
    key = lax.broadcasted_iota(jnp.int32, (keys, rows), 0)
    row = lax.broadcasted_iota(jnp.int32, (keys, rows), 1) + row_offset
    lowest = jnp.where(row >= split, split, first)
    if width is not None:
        lowest = jnp.maximum(lowest, row - (width - 1))
    return jnp.where((key >= lowest) & (key <= row), 0.0, NEG).astype(F32)


def stage_keys(keys, keys_ref):
    scaled = (keys.astype(F32) * HD ** (-0.5)).astype(BF16)
    lane = lax.broadcasted_iota(jnp.int32, (keys.shape[0], LANES), 1)
    zero = jnp.zeros((keys.shape[0], LANES), BF16)
    for pair in range(keys.shape[1] // LANES):
        tile = scaled[:, pair * LANES : (pair + 1) * LANES]
        turned = jnp.concatenate([tile[:, HD:], tile[:, :HD]], axis=1)
        keys_ref[2 * pair, 0] = jnp.where(lane < HD, tile, zero)
        keys_ref[2 * pair, 1] = jnp.where(lane < HD, zero, turned)
        keys_ref[2 * pair + 1, 0] = jnp.where(lane < HD, turned, zero)
        keys_ref[2 * pair + 1, 1] = jnp.where(lane < HD, zero, tile)


def stage_values(values, values_ref):
    count = values.shape[0]
    turned = jnp.transpose(values.astype(F32)).astype(BF16)
    for head in range(values.shape[1] // HD):
        values_ref[head, :HD, :] = turned[head * HD : (head + 1) * HD]
        values_ref[head, HD:, :] = jnp.ones((TAIL, count), BF16)


def heads_of(g, query_tiles, keys_ref, values_ref, bias):
    count = bias.shape[0]
    queries = jnp.concatenate(query_tiles, axis=0)
    keys = jnp.concatenate([keys_ref[g, 0], keys_ref[g, 1]], axis=0)
    scores = dot(keys, queries, ((1,), (1,)))
    wide = jnp.concatenate([bias] * len(query_tiles), axis=1)
    patterns = []
    for side in range(2):
        masked = scores[side * count : (side + 1) * count] + wide
        highest = jnp.max(masked, axis=0, keepdims=True)
        patterns.append(jnp.exp(masked - highest).astype(BF16))
    pattern = jnp.concatenate(patterns, axis=1)
    weighted = dot(values_ref[g], pattern, ((1,), (0,)))
    return weighted[:HD] * (1.0 / weighted[HD : HD + 1])


def window_heads(q_ref, keys_ref, values_ref, bias_ref, out_ref):
    kv_heads = keys_ref.shape[0]
    rows = q_ref.shape[0]
    tiles = q_ref.shape[1] // kv_heads // LANES
    for g in range(kv_heads):
        lanes = [(g * tiles + t) * LANES for t in range(tiles)]
        part = heads_of(
            g, [q_ref[:, lane : lane + LANES] for lane in lanes], keys_ref, values_ref, bias_ref[...]
        ).astype(BF16)
        for side in range(2):
            for t, lane in enumerate(lanes):
                at = (side * tiles + t) * rows
                start = lane + side * HD
                out_ref[start : start + HD, :] = part[:, at : at + rows]


def causal_heads(g, query_tiles, keys_ref, values_ref, bias_ref, out_ref, first_row):
    tiles = len(query_tiles)
    rows = query_tiles[0].shape[0]
    part = heads_of(g, query_tiles, keys_ref, values_ref, bias_ref[...])
    for t in range(tiles):
        low = part[:, t * rows : (t + 1) * rows]
        high = part[:, (tiles + t) * rows : (tiles + t + 1) * rows]
        turned = jnp.transpose(jnp.concatenate([low, high], axis=0)).astype(BF16)
        lane = (g * tiles + t) * LANES
        out_ref[first_row : first_row + rows, lane : lane + LANES] = turned


def pack_kernel(k_ref, v_ref, out_ref, sems):
    half = out_ref.shape[0]
    kv_width = k_ref.shape[1]
    copies = [
        pltpu.make_async_copy(k_ref.at[pl.ds(half, half)], out_ref.at[:, pl.ds(0, kv_width)], sems.at[0]),
        pltpu.make_async_copy(
            v_ref.at[pl.ds(half, half)], out_ref.at[:, pl.ds(kv_width, kv_width)], sems.at[1]
        ),
    ]
    for copy in copies:
        copy.start()
    for copy in copies:
        copy.wait()


def window_upper_kernel(
    lengths_ref, q_ref, k_ref, v_ref, weight_ref, out_ref, held_ref,
    lengths_s, q_s, k_s, v_s, attn_s, keys_s, values_s, bias_s, sems, weight_sems, *, chunk
):
    half = q_s.shape[0]
    upper = pl.ds(half, half)
    copies = [
        pltpu.make_async_copy(lengths_ref, lengths_s, sems.at[0]),
        pltpu.make_async_copy(k_ref.at[upper], k_s, sems.at[1]),
        pltpu.make_async_copy(v_ref.at[upper], v_s, sems.at[2]),
        pltpu.make_async_copy(q_ref.at[upper], q_s, sems.at[3]),
    ]
    count = held_ref.shape[0] // chunk
    weights = [
        pltpu.make_async_copy(
            weight_ref.at[pl.ds(c * chunk, chunk)], held_ref.at[pl.ds(c * chunk, chunk)], weight_sems.at[c]
        )
        for c in range(count)
    ]
    for copy in copies + weights:
        copy.start()
    copies[0].wait()
    bias_s[...] = upper_bias(lengths_s, half, WIN)
    copies[1].wait()
    stage_keys(k_s[...], keys_s)
    copies[2].wait()
    stage_values(v_s[...], values_s)
    copies[3].wait()
    window_heads(q_s, keys_s, values_s, bias_s, attn_s)
    for c in range(count):
        weights[c].wait()
        part = slice(c * chunk, (c + 1) * chunk)
        out_ref[part, :] = dot(held_ref[part, :], attn_s[...], ((1,), (0,))).astype(BF16)


def window_lower_kernel(
    lengths_ref, q_ref, k_ref, v_ref, halo_ref, held_ref, out_ref,
    lengths_s, q_s, k_s, v_s, attn_s, keys_s, values_s, bias_s, sems, *, chunk
):
    half = q_s.shape[0]
    kv_width = k_s.shape[1]
    lower = pl.ds(0, half)
    copies = [
        pltpu.make_async_copy(lengths_ref, lengths_s, sems.at[0]),
        pltpu.make_async_copy(k_ref.at[lower], k_s, sems.at[1]),
        pltpu.make_async_copy(v_ref.at[lower], v_s, sems.at[2]),
        pltpu.make_async_copy(q_ref.at[lower], q_s, sems.at[3]),
    ]
    for copy in copies:
        copy.start()
    copies[0].wait()
    bias_s[...] = lower_bias(lengths_s, half, WIN)
    copies[1].wait()
    stage_keys(jnp.concatenate([halo_ref[:, :kv_width], k_s[...]], axis=0), keys_s)
    copies[2].wait()
    stage_values(jnp.concatenate([halo_ref[:, kv_width:], v_s[...]], axis=0), values_s)
    copies[3].wait()
    window_heads(q_s, keys_s, values_s, bias_s, attn_s)
    for first in range(0, out_ref.shape[0], chunk):
        part = slice(first, first + chunk)
        out_ref[part, :] = dot(held_ref[part, :], attn_s[...], ((1,), (0,))).astype(BF16)


def add_and_norm(own_ref, other_ref, gain_ref, branch_ref, normed_ref, first_row, sum_s, keep_ref, chunk):
    width, rows = own_ref.shape
    head = lax.axis_index("head")

    def add(c, squares):
        part = pl.ds(pl.multiple_of(c * chunk, 16), chunk)
        total = own_ref[part, :].astype(F32) + other_ref[part, :].astype(F32)
        sum_s[part, :] = total
        rounded = total.astype(BF16)
        if keep_ref is not None:
            rounded = jnp.where(head == 0, rounded, keep_ref[part, :])
        branch_ref[part, :] = rounded
        return squares + jnp.sum(total * total, axis=0, keepdims=True)

    squares = lax.fori_loop(0, width // chunk, add, jnp.zeros((1, rows), F32))
    factor = lax.rsqrt(squares * (1.0 / width) + 1e-05)
    for first in range(0, width, LANES):
        last = min(first + LANES, width)
        piece = jnp.transpose(sum_s[first:last, :] * factor) * gain_ref[:, first:last]
        normed_ref[first_row : first_row + rows, first:last] = piece.astype(BF16)


def norm_upper_kernel(
    own_ref, other_ref, gain_ref, kw_ref, vw_ref, branch_ref, normed_ref, kv_ref, sum_s, *, chunk
):
    add_and_norm(own_ref, other_ref, gain_ref, branch_ref, normed_ref, 0, sum_s, None, chunk)
    kv_width = kw_ref.shape[1]
    kv_ref[:, :kv_width] = dot(normed_ref[...], kw_ref[...], ((1,), (0,))).astype(BF16)
    kv_ref[:, kv_width:] = dot(normed_ref[...], vw_ref[...], ((1,), (0,))).astype(BF16)


def causal_upper_kernel(
    lengths_ref, own_ref, other_ref, gain_ref, kw_ref, vw_ref, qw_ref, kept_ref, normed_ref, kv_up_ref,
    branch_ref, q_ref, kv_ref, out_ref, lengths_s, normed_s, sum_s, keys_s, values_s, bias_s, sem, *, chunk
):
    half = own_ref.shape[1]
    kv_width = kw_ref.shape[1]
    copy = pltpu.make_async_copy(lengths_ref, lengths_s, sem)
    copy.start()
    normed_s[half:, :] = normed_ref[...]
    add_and_norm(own_ref, other_ref, gain_ref, branch_ref, normed_s, 0, sum_s, kept_ref, chunk)
    copy.wait()
    bias_s[...] = upper_bias(lengths_s, half, None)
    stage_keys(kv_up_ref[:, :kv_width], keys_s)
    stage_values(kv_up_ref[:, kv_width:], values_s)
    kv_heads = keys_s.shape[0]
    group = qw_ref.shape[1] // kv_heads
    for g in range(kv_heads):
        columns = slice(g * group, (g + 1) * group)
        queries = dot(normed_s[...], qw_ref[:, columns], ((1,), (0,))).astype(BF16)
        q_ref[:, columns] = queries[:half]
        tiles = [queries[half:, at : at + LANES] for at in range(0, group, LANES)]
        causal_heads(g, tiles, keys_s, values_s, bias_s, out_ref, 0)
    kv_ref[:, :kv_width] = dot(normed_s[:half, :], kw_ref[...], ((1,), (0,))).astype(BF16)
    kv_ref[:, kv_width:] = dot(normed_s[:half, :], vw_ref[...], ((1,), (0,))).astype(BF16)


def causal_lower_kernel(
    lengths_ref, q_ref, kv_ref, halo_ref, upper_ref, out_ref, lengths_s, keys_s, values_s, bias_s, sem
):
    half = q_ref.shape[0]
    kv_width = kv_ref.shape[1] // 2
    copy = pltpu.make_async_copy(lengths_ref, lengths_s, sem)
    copy.start()
    stage_keys(jnp.concatenate([halo_ref[:, :kv_width], kv_ref[:, :kv_width]], axis=0), keys_s)
    stage_values(jnp.concatenate([halo_ref[:, kv_width:], kv_ref[:, kv_width:]], axis=0), values_s)
    out_ref[half:, :] = upper_ref[...]
    copy.wait()
    bias_s[...] = lower_bias(lengths_s, half, None)
    kv_heads = keys_s.shape[0]
    group = q_ref.shape[1] // kv_heads
    for g in range(kv_heads):
        tiles = [q_ref[:, at : at + LANES] for at in range(g * group, (g + 1) * group, LANES)]
        causal_heads(g, tiles, keys_s, values_s, bias_s, out_ref, 0)


def attention_scratch(kv_heads, keys, rows):
    return [
        pltpu.VMEM((kv_heads, 2, keys, LANES), BF16),
        pltpu.VMEM((kv_heads, HD + TAIL, keys), BF16),
        pltpu.VMEM((keys, rows), F32),
    ]


def local(
    window_queries,
    window_keys,
    window_values,
    out_weight,
    norm_gain,
    query_weight,
    key_weight,
    value_weight,
    doc_lengths,
):
    rows, q_width = window_queries.shape
    kv_width = window_keys.shape[1]
    kv_heads = kv_width // HD
    width = out_weight.shape[1]
    half = rows // 2
    chunk = 576
    dma = pltpu.SemaphoreType.DMA
    lengths_s = pltpu.SMEM(doc_lengths.shape, jnp.int32)
    lengths, queries, keys, values = [
        in_hbm(x) for x in (doc_lengths, window_queries, window_keys, window_values)
    ]

    packed = pl.pallas_call(
        pack_kernel,
        out_shape=jax.ShapeDtypeStruct((half, 2 * kv_width), BF16),
        in_specs=hbm_specs(2),
        out_specs=vmem_specs(1)[0],
        scratch_shapes=[dma((2,))],
        compiler_params=params(16),
        name="pack",
    )(keys, values)
    halo = shifted(packed, "ctx")
    inputs_s = [
        lengths_s,
        pltpu.VMEM((half, q_width), BF16),
        pltpu.VMEM((half, kv_width), BF16),
        pltpu.VMEM((half, kv_width), BF16),
        pltpu.VMEM((q_width, half), BF16),
    ]
    own_upper, held = pl.pallas_call(
        functools.partial(window_upper_kernel, chunk=chunk),
        out_shape=(pltpu.VMEM((width, half), BF16), pltpu.VMEM((width, q_width), BF16)),
        in_specs=hbm_specs(5),
        out_specs=tuple(vmem_specs(2)),
        scratch_shapes=inputs_s + attention_scratch(kv_heads, half, half) + [dma((4,)), dma((width // chunk,))],
        compiler_params=params(16),
        name="window_upper",
    )(lengths, queries, keys, values, in_hbm(jnp.transpose(out_weight)))
    other_upper = swapped(own_upper, "head")
    own_lower = pl.pallas_call(
        functools.partial(window_lower_kernel, chunk=chunk),
        out_shape=pltpu.VMEM((width, half), BF16),
        in_specs=hbm_specs(4) + vmem_specs(2),
        out_specs=vmem_specs(1)[0],
        scratch_shapes=inputs_s + attention_scratch(kv_heads, 2 * half, half) + [dma((4,))],
        compiler_params=params(16),
        name="window_lower",
    )(lengths, queries, keys, values, in_vmem(halo), held)
    other_lower = swapped(own_lower, "head")
    gain = norm_gain.reshape(1, width)
    key_held, value_held, query_held = [in_vmem(x) for x in (key_weight, value_weight, query_weight)]
    branch_upper, normed_upper, pairs_upper = pl.pallas_call(
        functools.partial(norm_upper_kernel, chunk=192),
        out_shape=(
            pltpu.VMEM((width, half), BF16),
            pltpu.VMEM((half, width), BF16),
            pltpu.VMEM((half, 2 * kv_width), BF16),
        ),
        in_specs=vmem_specs(5),
        out_specs=tuple(vmem_specs(3)),
        scratch_shapes=[pltpu.VMEM((width, half), F32)],
        compiler_params=params(16),
        name="norm_upper",
    )(own_upper, other_upper, gain, key_held, value_held)
    earlier = shifted(pairs_upper, "ctx")
    branch, causal_queries, pairs_lower, causal_upper = pl.pallas_call(
        functools.partial(causal_upper_kernel, chunk=192),
        out_shape=(
            jax.ShapeDtypeStruct((width, half), BF16),
            pltpu.VMEM((half, q_width), BF16),
            pltpu.VMEM((half, 2 * kv_width), BF16),
            pltpu.VMEM((half, q_width), BF16),
        ),
        in_specs=hbm_specs(1) + vmem_specs(9),
        out_specs=tuple(vmem_specs(4)),
        scratch_shapes=[lengths_s, pltpu.VMEM((rows, width), BF16), pltpu.VMEM((width, half), F32)]
        + attention_scratch(kv_heads, half, half)
        + [dma],
        compiler_params=params(16),
        name="causal_upper",
    )(
        lengths, own_lower, other_lower, gain, key_held, value_held, query_held,
        branch_upper, normed_upper, pairs_upper,
    )
    causal_out = pl.pallas_call(
        causal_lower_kernel,
        out_shape=jax.ShapeDtypeStruct((rows, q_width), BF16),
        in_specs=hbm_specs(1) + vmem_specs(4),
        out_specs=vmem_specs(1)[0],
        scratch_shapes=[lengths_s] + attention_scratch(kv_heads, 2 * half, half) + [dma],
        compiler_params=params(16),
        name="causal_lower",
    )(lengths, causal_queries, pairs_lower, in_vmem(earlier), causal_upper)
    return (jnp.transpose(branch), causal_out)


def solution(mesh):
    placed = (
        P("ctx", "head"),
        P("ctx", "head"),
        P("ctx", "head"),
        P("head", None),
        P(),
        P(None, "head"),
        P(None, "head"),
        P(None, "head"),
        P(),
    )
    return jax.shard_map(
        local,
        mesh=mesh,
        in_specs=placed,
        out_specs=(P(("ctx", "head"), None), P("ctx", "head")),
        check_vma=False,
    )
```

time: 60.2 us -> 38.2 us (0.63)
  local copies, waits for them, and re-layouts: 9.76 us -> 0.04 us
  Pallas kernels: 37.8 us -> 31.7 us
  waiting for transfers between devices: 3.22 us -> 0.01 us
  starting transfers between devices: 8.31 us -> 5.32 us
    unnamed x20 -> x12, local copies, waits for them, and re-layouts: 8.05 us -> 0.03 us
    ppermute x2, starting transfers between devices: 8.24 us -> 4.72 us  [shifted(): return lax.ppermute(block, axis, [(i, (i + 1) % size) for i in range(size)])]
    ppermute x1 -> x2, waiting for transfers between devices: 3.22 us -> 0.01 us  [swapped(): return lax.ppermute(block, axis, [(i, size - 1 - i) for i in range(size)])]
    pallas_call x1, Pallas kernels: 6.97 us -> 3.81 us  [local(): pl.pallas_call(causal_lower_kernel, out_shape=jax.ShapeDtypeStruct((rows,...]
    pallas_call x4 -> x5, Pallas kernels: 30.8 us -> 27.9 us  [the longest x1 11.7 us: local(): pl.pallas_call(functools.partial(window_upper_kernel, chunk=chunk), out_s...]
    slice x3 -> x0, local copies, waits for them, and re-layouts: 1.7 us -> none  [the longest x1 0.85 us: local(): window_keys[half:]]
  transfers between devices with their start and end apart: 3 -> 4, of which waited for: 1 -> 0; matrix products, arithmetic and copies ran while one was open for 0% -> 0% of each run, Pallas kernels for 32% -> 71%
where the time goes in v2:
time: 38.2 us; the launch traced here: 38 us
  Pallas kernels  31.7 us (83%)
  starting transfers between devices  5.32 us (14%)
  between operations  0.92 us (2%)
    pallas_call x1, Pallas kernels, local(): pl.pallas_call(functools.partial(window_upper_kernel, chunk=chunk), out_s...  11.7 us
    pallas_call x1, Pallas kernels, local(): pl.pallas_call(functools.partial(causal_upper_kernel, chunk=192), out_sha...  7.54 us
    pallas_call x1, Pallas kernels, local(): pl.pallas_call(functools.partial(window_lower_kernel, chunk=chunk), out_s...  6.4 us
    ppermute x2, starting transfers between devices, shifted(): return lax.ppermute(block, axis, [(i, (i + 1) % size) for i in range(size)])  4.72 us
    pallas_call x1, Pallas kernels, local(): pl.pallas_call(causal_lower_kernel, out_shape=jax.ShapeDtypeStruct((rows,...  3.81 us
    pallas_call x1, Pallas kernels, local(): pl.pallas_call(functools.partial(norm_upper_kernel, chunk=192), out_shape...  1.32 us
    pallas_call x1, Pallas kernels, local(): pl.pallas_call(pack_kernel, out_shape=jax.ShapeDtypeStruct((half, 2 * kv_...  0.89 us
  transfers between devices with their start and end apart: 4, of which 0 were waited for; matrix products, arithmetic and copies ran while one was open for 0% of the time, Pallas kernels for 71%

profile of v2, /device:TPU:0, one launch (start us, length us, event | category | flops | bytes accessed | tf_op | source)
XLA Modules:
  0.0 38.0 jit_solution(862551556803016136)
XLA Ops:
  0.6 0.9 %pack.1 = bf16[128,512]{1,0:T(8,128)(2,1)S(1)} custom-call(bf16[256,256]{1,0:T(8,128)(2,1)} %k_ref.5, bf16[256,256]{1,0:T(8,128)(2,1)} %v_ref.5), custom_call_target="tpu_custom_call" | custom-call | tf_op jit(solution)/shard_map/pack/pallas_call | solution.py:329
  1.5 3.0 %collective-permute-start = (bf16[128,512]{1,0:T(8,128)(2,1)S(1)}, bf16[128,512]{1,0:T(8,128)(2,1)S(1)}, u32[]{:S(2)}, u32[]{:S(2)}) collective-permute-start(bf16[128,512]{1,0:T(8,128)(2,1)S(1)} %pack.1), channel_id=1, source_target_pairs={{0,2},{2,4},{4,6},{6,8},{8,10},{10,12},{12,14},{14,16},{16,18},{18... | collective-permute-start | bytes 393224 | tf_op jit(solution)/shard_map/ppermute | solution.py:47
  4.5 0.0 copy-start.2
  4.5 0.0 copy-start
  4.5 0.0 copy-start.1
  4.5 0.0 slice-start
  4.5 0.0 slice-start.1
  4.5 11.7 %window_upper.1 = (bf16[2880,128]{1,0:T(8,128)(2,1)S(1)}, bf16[2880,2048]{1,0:T(8,128)(2,1)S(1)}) custom-call(s32[32]{0:T(128)} %lengths_ref.7, bf16[256,2048]{1,0:T(8,128)(2,1)} %q_ref.3, bf16[256,256]{1,0:T(8,128)(2,1)} %k_ref.5, bf16[256,256]{1,0:T(8,128)(2,1)} %v_ref.5, bf16[2880,2048]{1,0:T(8,128)(2,1)} %bitcast.4), custom_call_target="tpu_custom_call" | custom-call | tf_op jit(solution)/shard_map/window_upper/pallas_call | solution.py:346
  16.3 0.1 collective-permute-start.2
  16.4 0.0 collective-permute-done.halo_ref
  16.4 0.0 slice-start.2
  16.4 6.4 %window_lower.1.own_ref = bf16[2880,128]{1,0:T(8,128)(2,1)S(1)} custom-call(s32[32]{0:T(128)} %lengths_ref.7, bf16[256,2048]{1,0:T(8,128)(2,1)} %q_ref.3, bf16[256,256]{1,0:T(8,128)(2,1)} %k_ref.5, bf16[256,256]{1,0:T(8,128)(2,1)} %v_ref.5, bf16[128,512]{1,0:T(8,128)(2,1)S(1)} %collective-permute-done.halo_ref, bf16[2880,2048]{1,0:T(8,128)(2,1)S(1)} %get-tuple-element.11.held_ref), custom_call_target="tpu_custom_call" | custom-call | tf_op jit(solution)/shard_map/window_lower/pallas_call | solution.py:356
  22.8 0.5 %collective-permute-start.1 = (bf16[2880,128]{1,0:T(8,128)(2,1)S(1)}, bf16[2880,128]{1,0:T(8,128)(2,1)S(1)}, u32[]{:S(2)}, u32[]{:S(2)}) collective-permute-start(bf16[2880,128]{1,0:T(8,128)(2,1)S(1)} %window_lower.1.own_ref), channel_id=1, source_target_pairs={{0,1},{1,0},{2,3},{3,2},{4,5},{5,4},{6,7},{7,6},{8,9},{9,8},{10,11... | collective-permute-start | bytes 2211848 | tf_op jit(solution)/shard_map/ppermute | solution.py:52
  23.3 0.0 copy-done.2
  23.3 0.0 collective-permute-done.2.other_ref
  23.3 0.0 copy-done
  23.4 0.0 copy-done.1
  23.4 1.3 %norm_upper.1 = (bf16[2880,128]{1,0:T(8,128)(2,1)S(1)}, bf16[128,2880]{1,0:T(8,128)(2,1)S(1)}, bf16[128,512]{1,0:T(8,128)(2,1)S(1)}) custom-call(bf16[2880,128]{1,0:T(8,128)(2,1)S(1)} %get-tuple-element.12.own_ref, bf16[2880,128]{1,0:T(8,128)(2,1)S(1)} %collective-permute-done.2.other_ref, f32[1,2880]{1,0:T(1,128)S(1)} %reshape.7.gain_ref, ...), custom_call_target="tpu_custom_call" | custom-call | tf_op jit(solution)/shard_map/norm_upper/pallas_call | solution.py:368
  24.7 1.7 %collective-permute-start.3 = (bf16[128,512]{1,0:T(8,128)(2,1)S(1)}, bf16[128,512]{1,0:T(8,128)(2,1)S(1)}, u32[]{:S(2)}, u32[]{:S(2)}) collective-permute-start(bf16[128,512]{1,0:T(8,128)(2,1)S(1)} %get-tuple-element.15.kv_up_ref), channel_id=1, source_target_pairs={{0,2},{2,4},{4,6},{6,8},{8,10},{10,12},{12,14},{14,16},{16,18},{18... | collective-permute-start | bytes 393224 | tf_op jit(solution)/shard_map/ppermute | solution.py:47
  26.4 0.0 collective-permute-done.1.other_ref
  26.4 0.0 slice-done
  26.4 0.0 slice-done.1
  26.4 0.0 slice-done.2
  26.4 7.5 %causal_upper.1 = (bf16[2880,128]{1,0:T(8,128)(2,1)}, bf16[128,2048]{1,0:T(8,128)(2,1)S(1)}, bf16[128,512]{1,0:T(8,128)(2,1)S(1)}, bf16[128,2048]{1,0:T(8,128)(2,1)S(1)}) custom-call(s32[32]{0:T(128)} %lengths_ref.7, bf16[2880,128]{1,0:T(8,128)(2,1)S(1)} %window_lower.1.own_ref, bf16[2880,128]{1,0:T(8,128)(2,1)S(1)} %collective-permute-done.1.other_ref, ...), custom_call_target="tpu_custom_call" | custom-call | tf_op jit(solution)/shard_map/causal_upper/pallas_call | solution.py:382
  34.0 0.0 collective-permute-done.3.halo_ref
  34.0 3.8 %causal_lower.1 = bf16[256,2048]{1,0:T(8,128)(2,1)} custom-call(s32[32]{0:T(128)} %lengths_ref.7, bf16[128,2048]{1,0:T(8,128)(2,1)S(1)} %get-tuple-element.17.q_ref, bf16[128,512]{1,0:T(8,128)(2,1)S(1)} %get-tuple-element.18.kv_ref, bf16[128,512]{1,0:T(8,128)(2,1)S(1)} %collective-permute-done.3.halo_ref, bf16[128,2048]{1,0:T(8,128)(2,1)S(1)} %get-tuple-element.19.upper_ref), custom_call_target="tpu_custom_call" | custom-call | tf_op jit(solution)/shard_map/causal_lower/pallas_call | solution.py:401
  (2 shorter events, 0.0 us)
Async XLA Ops:
  1.5 14.8 %collective-permute-start = (bf16[128,512]{1,0:T(8,128)(2,1)S(1)}, bf16[128,512]{1,0:T(8,128)(2,1)S(1)}, u32[]{:S(2)}, u32[]{:S(2)}) collective-permute-start(bf16[128,512]{1,0:T(8,128)(2,1)S(1)} %pack.1), channel_id=1, source_target_pairs={{0,2},{2,4},{4,6},{6,8},{8,10},{10,12},{12,14},{14,16},{16,18},{18... | collective-permute-start | bytes 393224 | tf_op jit(solution)/shard_map/ppermute | solution.py:47
  4.5 18.8 %copy-start.2 = (f32[2880]{0:T(1024)S(1)}, f32[2880]{0:T(1024)}, u32[]{:S(2)}) copy-start(f32[2880]{0:T(1024)} %param.13) | copy-start | bytes 34564
  4.5 18.8 %copy-start = (bf16[2880,256]{1,0:T(8,128)(2,1)S(1)}, bf16[2880,256]{1,0:T(8,128)(2,1)}, u32[]{:S(2)}) copy-start(bf16[2880,256]{1,0:T(8,128)(2,1)} %kw_ref.3) | copy-start | bytes 4423684
  4.5 18.8 %copy-start.1 = (bf16[2880,256]{1,0:T(8,128)(2,1)S(1)}, bf16[2880,256]{1,0:T(8,128)(2,1)}, u32[]{:S(2)}) copy-start(bf16[2880,256]{1,0:T(8,128)(2,1)} %vw_ref.3) | copy-start | bytes 4423684
  4.5 21.9 %slice-start = ((s8[11796480]{0:T(1024)(128)(4,1)}), s8[4194304]{0:T(1024)(128)(4,1)S(1)}, s32[]{:S(2)}) async-start(s8[11796480]{0:T(1024)(128)(4,1)} %bitcast.2), calls=%async_computation | async-start | bytes 8388608
  4.5 21.9 %slice-start.1 = ((s8[11796480]{0:T(1024)(128)(4,1)}), s8[4194304]{0:T(1024)(128)(4,1)S(1)}, s32[]{:S(2)}) async-start(s8[11796480]{0:T(1024)(128)(4,1)} %bitcast.2), calls=%async_computation.1 | async-start | bytes 8388608
  16.3 7.1 %collective-permute-start.2 = (bf16[2880,128]{1,0:T(8,128)(2,1)S(1)}, bf16[2880,128]{1,0:T(8,128)(2,1)S(1)}, u32[]{:S(2)}, u32[]{:S(2)}) collective-permute-start(bf16[2880,128]{1,0:T(8,128)(2,1)S(1)} %get-tuple-element.12.own_ref), channel_id=1, source_target_pairs={{0,1},{1,0},{2,3},{3,2},{4,5},{5,4},{6,7},{7,6},{8,9},{9,8},{10,11... | collective-permute-start | bytes 2211848 | tf_op jit(solution)/shard_map/ppermute | solution.py:52
  16.4 10.1 %slice-start.2 = ((s8[11796480]{0:T(1024)(128)(4,1)}), s8[3407872]{0:T(1024)(128)(4,1)S(1)}, s32[]{:S(2)}) async-start(s8[11796480]{0:T(1024)(128)(4,1)} %bitcast.2), calls=%async_computation.2 | async-start | bytes 6815744
  22.8 3.6 %collective-permute-start.1 = (bf16[2880,128]{1,0:T(8,128)(2,1)S(1)}, bf16[2880,128]{1,0:T(8,128)(2,1)S(1)}, u32[]{:S(2)}, u32[]{:S(2)}) collective-permute-start(bf16[2880,128]{1,0:T(8,128)(2,1)S(1)} %window_lower.1.own_ref), channel_id=1, source_target_pairs={{0,1},{1,0},{2,3},{3,2},{4,5},{5,4},{6,7},{7,6},{8,9},{9,8},{10,11... | collective-permute-start | bytes 2211848 | tf_op jit(solution)/shard_map/ppermute | solution.py:52
  24.7 9.3 %collective-permute-start.3 = (bf16[128,512]{1,0:T(8,128)(2,1)S(1)}, bf16[128,512]{1,0:T(8,128)(2,1)S(1)}, u32[]{:S(2)}, u32[]{:S(2)}) collective-permute-start(bf16[128,512]{1,0:T(8,128)(2,1)S(1)} %get-tuple-element.15.kv_up_ref), channel_id=1, source_target_pairs={{0,2},{2,4},{4,6},{6,8},{8,10},{10,12},{12,14},{14,16},{16,18},{18... | collective-permute-start | bytes 393224 | tf_op jit(solution)/shard_map/ppermute | solution.py:47

commit v3 on v2

v3 whole, which is shorter than its diff:
```python
import functools

import jax
import jax.numpy as jnp
from jax import lax
from jax.experimental import pallas as pl
from jax.experimental.pallas import tpu as pltpu
from jax.sharding import PartitionSpec as P

HD = 64
WIN = 128
LANES = 128
NEG = -1e30
TAIL = 16

F32 = jnp.float32
BF16 = jnp.bfloat16
MIB = 1024 * 1024


def params(mib):
    return pltpu.CompilerParams(vmem_limit_bytes=mib * MIB)


def in_vmem(array):
    return pltpu.with_memory_space_constraint(array, pltpu.VMEM)


def in_hbm(array):
    return pltpu.with_memory_space_constraint(array, pltpu.HBM)


def hbm_specs(count):
    return [pl.BlockSpec(memory_space=pltpu.HBM)] * count


def vmem_specs(count):
    return [pl.BlockSpec(memory_space=pltpu.VMEM)] * count


def dot(a, b, dims):
    return lax.dot_general(a, b, (dims, ((), ())), preferred_element_type=F32)


def shifted(block, axis):
    size = lax.axis_size(axis)
    return lax.ppermute(block, axis, [(i, (i + 1) % size) for i in range(size)])


def swapped(block, axis):
    size = lax.axis_size(axis)
    return lax.ppermute(block, axis, [(i, size - 1 - i) for i in range(size)])


def lower_bias(lengths_ref, half, width):
    ctx = lax.axis_index("ctx")
    first = jnp.where(ctx == 0, half, 0)
    split = first + lengths_ref[2 * ctx]
    return bias_of(2 * half, half, half, first, split, width)


def upper_bias(lengths_ref, half, width):
    ctx = lax.axis_index("ctx")
    last = lengths_ref.shape[0] - 1
    split = lengths_ref[jnp.minimum(2 * ctx + 2, last)]
    split = jnp.where(ctx == lax.axis_size("ctx") - 1, 2 * half, split)
    return bias_of(half, half, 0, 0, split, width)


def bias_of(keys, rows, row_offset, first, split, width):
    key = lax.broadcasted_iota(jnp.int32, (keys, rows), 0)
    row = lax.broadcasted_iota(jnp.int32, (keys, rows), 1) + row_offset
    lowest = jnp.where(row >= split, split, first)
    if width is not None:
        lowest = jnp.maximum(lowest, row - (width - 1))
    return jnp.where((key >= lowest) & (key <= row), 0.0, NEG).astype(F32)


def stage_keys(keys, keys_ref):
    scaled = (keys.astype(F32) * HD ** (-0.5)).astype(BF16)
    lane = lax.broadcasted_iota(jnp.int32, (keys.shape[0], LANES), 1)
    zero = jnp.zeros((keys.shape[0], LANES), BF16)
    for pair in range(keys.shape[1] // LANES):
        tile = scaled[:, pair * LANES : (pair + 1) * LANES]
        turned = jnp.concatenate([tile[:, HD:], tile[:, :HD]], axis=1)
        keys_ref[2 * pair, 0] = jnp.where(lane < HD, tile, zero)
        keys_ref[2 * pair, 1] = jnp.where(lane < HD, zero, turned)
        keys_ref[2 * pair + 1, 0] = jnp.where(lane < HD, turned, zero)
        keys_ref[2 * pair + 1, 1] = jnp.where(lane < HD, zero, tile)


def stage_values(values, values_ref):
    count = values.shape[0]
    turned = jnp.transpose(values.astype(F32)).astype(BF16)
    for head in range(values.shape[1] // HD):
        values_ref[head, :HD, :] = turned[head * HD : (head + 1) * HD]
        values_ref[head, HD:, :] = jnp.ones((TAIL, count), BF16)


class Unit:
    def __init__(self, g, lane):
        self.g, self.lane = g, lane


def units_of(kv_heads, q_width):
    step = 2 * LANES
    group = q_width // kv_heads
    return [Unit(lane // group, lane) for lane in range(0, q_width, step)]


def unit_scores(queries, unit, keys_ref):
    stacked = jnp.concatenate([queries[:, :LANES], queries[:, LANES:]], axis=0)
    keys = jnp.concatenate([keys_ref[unit.g, 0], keys_ref[unit.g, 1]], axis=0)
    return dot(keys, stacked, ((1,), (1,)))


def unit_attend(scores, unit, values_ref, bias):
    count = bias.shape[0]
    wide = jnp.concatenate([bias, bias], axis=1)
    patterns = []
    for side in range(2):
        masked = scores[side * count : (side + 1) * count] + wide
        highest = jnp.max(masked, axis=0, keepdims=True)
        patterns.append(jnp.exp(masked - highest).astype(BF16))
    weighted = dot(values_ref[unit.g], jnp.concatenate(patterns, axis=1), ((1,), (0,)))
    return weighted[:HD] * (1.0 / weighted[HD : HD + 1])


def pipelined(units, queries_of, keys_ref, values_ref, bias, write):
    count = len(units)
    queries = queries_of(units[0])
    scores = unit_scores(queries, units[0], keys_ref)
    queries = queries_of(units[1])
    for i, unit in enumerate(units):
        now = scores
        if i + 1 < count:
            scores = unit_scores(queries, units[i + 1], keys_ref)
        if i + 2 < count:
            queries = queries_of(units[i + 2])
        write(unit, unit_attend(now, unit, values_ref, bias))


def window_heads(queries_of, keys_ref, values_ref, bias_ref, out_ref, q_width):
    def write(unit, part):
        rows = part.shape[1] // 4
        rounded = part.astype(BF16)
        for side in range(2):
            for t in range(2):
                at = (side * 2 + t) * rows
                start = unit.lane + t * LANES + side * HD
                out_ref[start : start + HD, :] = rounded[:, at : at + rows]

    pipelined(units_of(keys_ref.shape[0], q_width), queries_of, keys_ref, values_ref, bias_ref[...], write)


def causal_heads(queries_of, keys_ref, values_ref, bias_ref, out_ref, q_width, ready):
    def write(unit, part):
        rows = part.shape[1] // 4
        for t in range(2):
            low = part[:, t * rows : (t + 1) * rows]
            high = part[:, (2 + t) * rows : (3 + t) * rows]
            lane = unit.lane + t * LANES
            out_ref[:, lane : lane + LANES] = jnp.transpose(
                jnp.concatenate([low, high], axis=0)
            ).astype(BF16)
        ready(unit)

    pipelined(units_of(keys_ref.shape[0], q_width), queries_of, keys_ref, values_ref, bias_ref[...], write)


def pack_kernel(k_ref, v_ref, out_ref, sems):
    half = out_ref.shape[0]
    kv_width = k_ref.shape[1]
    copies = [
        pltpu.make_async_copy(k_ref.at[pl.ds(half, half)], out_ref.at[:, pl.ds(0, kv_width)], sems.at[0]),
        pltpu.make_async_copy(
            v_ref.at[pl.ds(half, half)], out_ref.at[:, pl.ds(kv_width, kv_width)], sems.at[1]
        ),
    ]
    for copy in copies:
        copy.start()
    for copy in copies:
        copy.wait()


def window_upper_kernel(
    lengths_ref, q_ref, k_ref, v_ref, weight_ref, gain_ref,
    out_ref, held_ref, q_held, k_held, v_held, window_bias, upper_causal, lower_causal, gain_held,
    lengths_s, attn_s, keys_s, values_s, bias_s, sems, weight_sems, *, chunk
):
    half = out_ref.shape[1]
    upper, lower = pl.ds(half, half), pl.ds(0, half)
    first = [
        pltpu.make_async_copy(lengths_ref, lengths_s, sems.at[0]),
        pltpu.make_async_copy(k_ref.at[upper], k_held.at[upper], sems.at[1]),
        pltpu.make_async_copy(v_ref.at[upper], v_held.at[upper], sems.at[2]),
        pltpu.make_async_copy(q_ref.at[upper], q_held.at[upper], sems.at[3]),
    ]
    count = held_ref.shape[0] // chunk
    weights = [
        pltpu.make_async_copy(
            weight_ref.at[pl.ds(c * chunk, chunk)], held_ref.at[pl.ds(c * chunk, chunk)], weight_sems.at[c]
        )
        for c in range(count)
    ]
    last = [
        pltpu.make_async_copy(k_ref.at[lower], k_held.at[lower], sems.at[4]),
        pltpu.make_async_copy(v_ref.at[lower], v_held.at[lower], sems.at[5]),
        pltpu.make_async_copy(q_ref.at[lower], q_held.at[lower], sems.at[6]),
        pltpu.make_async_copy(gain_ref, gain_held, sems.at[7]),
    ]
    for copy in first + weights + last:
        copy.start()
    first[0].wait()
    bias_s[...] = upper_bias(lengths_s, half, WIN)
    first[1].wait()
    stage_keys(k_held[half:], keys_s)
    first[2].wait()
    stage_values(v_held[half:], values_s)
    first[3].wait()

    def queries_of(unit):
        return q_held[half:, unit.lane : unit.lane + 2 * LANES]

    window_heads(queries_of, keys_s, values_s, bias_s, attn_s, q_held.shape[1])
    window_bias[...] = lower_bias(lengths_s, half, WIN)
    upper_causal[...] = upper_bias(lengths_s, half, None)
    lower_causal[...] = lower_bias(lengths_s, half, None)
    for c in range(count):
        weights[c].wait()
        part = slice(c * chunk, (c + 1) * chunk)
        out_ref[part, :] = dot(held_ref[part, :], attn_s[...], ((1,), (0,))).astype(BF16)
    for copy in last:
        copy.wait()


def window_lower_kernel(
    q_ref, k_ref, v_ref, halo_ref, held_ref, bias_ref, kw_ref, vw_ref, qw_ref,
    out_ref, key_held, value_held, query_held, attn_s, keys_s, values_s, sems, *, chunk
):
    half = halo_ref.shape[0]
    kv_width = k_ref.shape[1]
    copies = [
        pltpu.make_async_copy(kw_ref, key_held, sems.at[0]),
        pltpu.make_async_copy(vw_ref, value_held, sems.at[1]),
        pltpu.make_async_copy(qw_ref.at[:, pl.ds(0, query_held.shape[1])], query_held, sems.at[2]),
    ]
    for copy in copies:
        copy.start()
    stage_keys(jnp.concatenate([halo_ref[:, :kv_width], k_ref[:half]], axis=0), keys_s)
    stage_values(jnp.concatenate([halo_ref[:, kv_width:], v_ref[:half]], axis=0), values_s)

    def queries_of(unit):
        return q_ref[:half, unit.lane : unit.lane + 2 * LANES]

    window_heads(queries_of, keys_s, values_s, bias_ref, attn_s, q_ref.shape[1])
    for first in range(0, out_ref.shape[0], chunk):
        part = slice(first, first + chunk)
        out_ref[part, :] = dot(held_ref[part, :], attn_s[...], ((1,), (0,))).astype(BF16)
    for copy in copies:
        copy.wait()


def add_and_norm(own_ref, other_ref, gain_ref, branch_ref, normed_ref, first_row, sum_s, keep_ref, chunk):
    width, rows = own_ref.shape
    head = lax.axis_index("head")

    def add(c, squares):
        part = pl.ds(pl.multiple_of(c * chunk, 16), chunk)
        total = own_ref[part, :].astype(F32) + other_ref[part, :].astype(F32)
        sum_s[part, :] = total
        rounded = total.astype(BF16)
        if keep_ref is not None:
            rounded = jnp.where(head == 0, rounded, keep_ref[part, :])
        branch_ref[part, :] = rounded
        return squares + jnp.sum(total * total, axis=0, keepdims=True)

    squares = lax.fori_loop(0, width // chunk, add, jnp.zeros((1, rows), F32))
    factor = lax.rsqrt(squares * (1.0 / width) + 1e-05)
    for first in range(0, width, LANES):
        last = min(first + LANES, width)
        piece = jnp.transpose(sum_s[first:last, :] * factor) * gain_ref[first:last][None, :]
        normed_ref[first_row : first_row + rows, first:last] = piece.astype(BF16)


def norm_upper_kernel(
    own_ref, other_ref, gain_ref, kw_ref, vw_ref, branch_ref, normed_ref, kv_ref, sum_s, *, chunk
):
    add_and_norm(own_ref, other_ref, gain_ref, branch_ref, normed_ref, 0, sum_s, None, chunk)
    kv_width = kw_ref.shape[1]
    kv_ref[:, :kv_width] = dot(normed_ref[...], kw_ref[...], ((1,), (0,))).astype(BF16)
    kv_ref[:, kv_width:] = dot(normed_ref[...], vw_ref[...], ((1,), (0,))).astype(BF16)


def causal_upper_kernel(
    own_ref, other_ref, gain_ref, kw_ref, vw_ref, query_held, kept_ref, normed_ref, kv_up_ref, bias_ref,
    qw_ref, branch_ref, q_ref, kv_ref, out_ref,
    rest_s, branch_s, out_s, normed_s, sum_s, keys_s, values_s, sems, *, chunk
):
    half = own_ref.shape[1]
    kv_width = kw_ref.shape[1]
    q_width = qw_ref.shape[1]
    present = query_held.shape[1]
    rest_in = pltpu.make_async_copy(
        qw_ref.at[:, pl.ds(present, q_width - present)], rest_s, sems.at[2]
    )
    rest_in.start()
    normed_s[half:, :] = normed_ref[...]
    add_and_norm(own_ref, other_ref, gain_ref, branch_s, normed_s, 0, sum_s, kept_ref, chunk)
    branch_out = pltpu.make_async_copy(branch_s, branch_ref, sems.at[0])
    branch_out.start()
    stage_keys(kv_up_ref[:, :kv_width], keys_s)
    stage_values(kv_up_ref[:, kv_width:], values_s)

    def queries_of(unit):
        columns = slice(unit.lane, unit.lane + 2 * LANES)
        if unit.lane == present:
            rest_in.wait()
        if unit.lane < present:
            weight = query_held[:, columns]
        else:
            weight = rest_s[:, unit.lane - present : unit.lane - present + 2 * LANES]
        queries = dot(normed_s[...], weight, ((1,), (0,))).astype(BF16)
        q_ref[:, columns] = queries[:half]
        return queries[half:]

    causal_heads(queries_of, keys_s, values_s, bias_ref, out_s, q_width, lambda unit: None)
    upper_out = pltpu.make_async_copy(out_s, out_ref.at[pl.ds(half, half)], sems.at[1])
    upper_out.start()
    kv_ref[:, :kv_width] = dot(normed_s[:half, :], kw_ref[...], ((1,), (0,))).astype(BF16)
    kv_ref[:, kv_width:] = dot(normed_s[:half, :], vw_ref[...], ((1,), (0,))).astype(BF16)
    branch_out.wait()
    upper_out.wait()


def causal_lower_kernel(
    q_ref, kv_ref, halo_ref, bias_ref, given_ref, out_ref, out_s, keys_s, values_s, sems
):
    half, q_width = q_ref.shape
    kv_width = kv_ref.shape[1] // 2
    stage_keys(jnp.concatenate([halo_ref[:, :kv_width], kv_ref[:, :kv_width]], axis=0), keys_s)
    stage_values(jnp.concatenate([halo_ref[:, kv_width:], kv_ref[:, kv_width:]], axis=0), values_s)
    copies = []

    def queries_of(unit):
        return q_ref[:, unit.lane : unit.lane + 2 * LANES]

    def ready(unit):
        columns = pl.ds(unit.lane, 2 * LANES)
        copy = pltpu.make_async_copy(
            out_s.at[:, columns], out_ref.at[pl.ds(0, half), columns], sems.at[len(copies)]
        )
        copy.start()
        copies.append(copy)

    causal_heads(queries_of, keys_s, values_s, bias_ref, out_s, q_width, ready)
    for copy in copies:
        copy.wait()


def attention_scratch(kv_heads, keys):
    return [
        pltpu.VMEM((kv_heads, 2, keys, LANES), BF16),
        pltpu.VMEM((kv_heads, HD + TAIL, keys), BF16),
    ]


def local(
    window_queries,
    window_keys,
    window_values,
    out_weight,
    norm_gain,
    query_weight,
    key_weight,
    value_weight,
    doc_lengths,
):
    rows, q_width = window_queries.shape
    kv_width = window_keys.shape[1]
    kv_heads = kv_width // HD
    width = out_weight.shape[1]
    half = rows // 2
    chunk = 576
    dma = pltpu.SemaphoreType.DMA
    lengths, queries, keys, values = [
        in_hbm(x) for x in (doc_lengths, window_queries, window_keys, window_values)
    ]

    packed = pl.pallas_call(
        pack_kernel,
        out_shape=jax.ShapeDtypeStruct((half, 2 * kv_width), BF16),
        in_specs=hbm_specs(2),
        out_specs=vmem_specs(1)[0],
        scratch_shapes=[dma((2,))],
        compiler_params=params(16),
        name="pack",
    )(keys, values)
    halo = shifted(packed, "ctx")
    attn_s = pltpu.VMEM((q_width, half), BF16)
    (
        own_upper, held, q_held, k_held, v_held, window_bias, upper_causal, lower_causal, gain
    ) = pl.pallas_call(
        functools.partial(window_upper_kernel, chunk=chunk),
        out_shape=(
            pltpu.VMEM((width, half), BF16),
            pltpu.VMEM((width, q_width), BF16),
            pltpu.VMEM((rows, q_width), BF16),
            pltpu.VMEM((rows, kv_width), BF16),
            pltpu.VMEM((rows, kv_width), BF16),
            pltpu.VMEM((rows, half), F32),
            pltpu.VMEM((half, half), F32),
            pltpu.VMEM((rows, half), F32),
            pltpu.VMEM((width,), F32),
        ),
        in_specs=hbm_specs(6),
        out_specs=tuple(vmem_specs(9)),
        scratch_shapes=[pltpu.SMEM(doc_lengths.shape, jnp.int32), attn_s]
        + attention_scratch(kv_heads, half)
        + [pltpu.VMEM((half, half), F32), dma((8,)), dma((width // chunk,))],
        compiler_params=params(16),
        name="window_upper",
    )(lengths, queries, keys, values, in_hbm(jnp.transpose(out_weight)), in_hbm(norm_gain))
    key_weight, value_weight, query_weight = [
        in_hbm(x) for x in (key_weight, value_weight, query_weight)
    ]
    other_upper = swapped(own_upper, "head")
    own_lower, key_held, value_held, query_held = pl.pallas_call(
        functools.partial(window_lower_kernel, chunk=chunk),
        out_shape=(
            pltpu.VMEM((width, half), BF16),
            pltpu.VMEM((width, kv_width), BF16),
            pltpu.VMEM((width, kv_width), BF16),
            pltpu.VMEM((width, q_width // 2), BF16),
        ),
        in_specs=vmem_specs(6) + hbm_specs(3),
        out_specs=tuple(vmem_specs(4)),
        scratch_shapes=[attn_s] + attention_scratch(kv_heads, rows) + [dma((3,))],
        compiler_params=params(16),
        name="window_lower",
    )(
        q_held, k_held, v_held, in_vmem(halo), held, window_bias,
        key_weight, value_weight, query_weight,
    )
    other_lower = swapped(own_lower, "head")
    branch_upper, normed_upper, pairs_upper = pl.pallas_call(
        functools.partial(norm_upper_kernel, chunk=192),
        out_shape=(
            pltpu.VMEM((width, half), BF16),
            pltpu.VMEM((half, width), BF16),
            pltpu.VMEM((half, 2 * kv_width), BF16),
        ),
        in_specs=vmem_specs(5),
        out_specs=tuple(vmem_specs(3)),
        scratch_shapes=[pltpu.VMEM((width, half), F32)],
        compiler_params=params(16),
        name="norm_upper",
    )(own_upper, other_upper, gain, key_held, value_held)
    earlier = shifted(pairs_upper, "ctx")
    branch, causal_queries, pairs_lower, causal_out = pl.pallas_call(
        functools.partial(causal_upper_kernel, chunk=192),
        out_shape=(
            pltpu.HBM((width, half), BF16),
            pltpu.VMEM((half, q_width), BF16),
            pltpu.VMEM((half, 2 * kv_width), BF16),
            pltpu.HBM((rows, q_width), BF16),
        ),
        in_specs=vmem_specs(10) + hbm_specs(1),
        out_specs=(hbm_specs(1)[0], *vmem_specs(2), hbm_specs(1)[0]),
        scratch_shapes=[
            pltpu.VMEM((width, q_width // 2), BF16),
            pltpu.VMEM((width, half), BF16),
            pltpu.VMEM((half, q_width), BF16),
            pltpu.VMEM((rows, width), BF16),
            pltpu.VMEM((width, half), F32),
        ]
        + attention_scratch(kv_heads, half)
        + [dma((3,))],
        compiler_params=params(20),
        name="causal_upper",
    )(
        own_lower, other_lower, gain, key_held, value_held, query_held,
        branch_upper, normed_upper, pairs_upper, upper_causal, query_weight,
    )
    causal_out = pl.pallas_call(
        causal_lower_kernel,
        out_shape=pltpu.HBM((rows, q_width), BF16),
        in_specs=vmem_specs(4) + hbm_specs(1),
        out_specs=hbm_specs(1)[0],
        scratch_shapes=[pltpu.VMEM((half, q_width), BF16)]
        + attention_scratch(kv_heads, rows)
        + [dma((q_width // (2 * LANES),))],
        input_output_aliases={4: 0},
        compiler_params=params(16),
        name="causal_lower",
    )(causal_queries, pairs_lower, in_vmem(earlier), lower_causal, causal_out)
    return (jnp.transpose(branch), causal_out)


def solution(mesh):
    placed = (
        P("ctx", "head"),
        P("ctx", "head"),
        P("ctx", "head"),
        P("head", None),
        P(),
        P(None, "head"),
        P(None, "head"),
        P(None, "head"),
        P(),
    )
    return jax.shard_map(
        local,
        mesh=mesh,
        in_specs=placed,
        out_specs=(P(("ctx", "head"), None), P("ctx", "head")),
        check_vma=False,
    )
```

time: 38.2 us -> 35.4 us (0.927)
  Pallas kernels: 31.7 us -> 29 us
    pallas_call x1, Pallas kernels: 11.7 us -> 8.79 us  [local(): pl.pallas_call(functools.partial(window_upper_kernel, chunk=chunk), out_s...]
    pallas_call x1, Pallas kernels: 7.54 us -> 10.4 us  [local(): pl.pallas_call(functools.partial(causal_upper_kernel, chunk=192), out_sha...]
    pallas_call x1, Pallas kernels: 6.4 us -> 4.95 us  [local(): pl.pallas_call(functools.partial(window_lower_kernel, chunk=chunk), out_s...]
    pallas_call x1, Pallas kernels: 3.81 us -> 2.66 us  [local(): pl.pallas_call(causal_lower_kernel, out_shape=pltpu.HBM((rows, q_width),...]
  transfers between devices with their start and end apart: 4 -> 4, of which waited for: 0 -> 0; matrix products, arithmetic and copies ran while one was open for 0% -> 0% of each run, Pallas kernels for 71% -> 72%
where the time goes in v3:
time: 35.4 us; the launch traced here: 35.2 us
  Pallas kernels  29 us (82%)
  starting transfers between devices  5.35 us (15%)
  between operations  0.86 us (2%)
    pallas_call x1, Pallas kernels, local(): pl.pallas_call(functools.partial(causal_upper_kernel, chunk=192), out_sha...  10.4 us
    pallas_call x1, Pallas kernels, local(): pl.pallas_call(functools.partial(window_upper_kernel, chunk=chunk), out_s...  8.79 us
    pallas_call x1, Pallas kernels, local(): pl.pallas_call(functools.partial(window_lower_kernel, chunk=chunk), out_s...  4.95 us
    ppermute x2, starting transfers between devices, shifted(): return lax.ppermute(block, axis, [(i, (i + 1) % size) for i in range(size)])  4.72 us
    pallas_call x1, Pallas kernels, local(): pl.pallas_call(causal_lower_kernel, out_shape=pltpu.HBM((rows, q_width),...  2.66 us
    pallas_call x1, Pallas kernels, local(): pl.pallas_call(functools.partial(norm_upper_kernel, chunk=192), out_shape...  1.34 us
    pallas_call x1, Pallas kernels, local(): pl.pallas_call(pack_kernel, out_shape=jax.ShapeDtypeStruct((half, 2 * kv_...  0.89 us
  transfers between devices with their start and end apart: 4, of which 0 were waited for; matrix products, arithmetic and copies ran while one was open for 0% of the time, Pallas kernels for 72%

profile of v3, /device:TPU:0, one launch (start us, length us, event | category | flops | bytes accessed | tf_op | source)
XLA Modules:
  0.0 35.2 jit_solution(4977291801887344862)
XLA Ops:
  0.6 0.9 %pack.1 = bf16[128,512]{1,0:T(8,128)(2,1)S(1)} custom-call(bf16[256,256]{1,0:T(8,128)(2,1)} %k_ref.3, bf16[256,256]{1,0:T(8,128)(2,1)} %v_ref.3), custom_call_target="tpu_custom_call" | custom-call | tf_op jit(solution)/shard_map/pack/pallas_call | solution.py:390
  1.5 3.0 %collective-permute-start = (bf16[128,512]{1,0:T(8,128)(2,1)S(1)}, bf16[128,512]{1,0:T(8,128)(2,1)S(1)}, u32[]{:S(2)}, u32[]{:S(2)}) collective-permute-start(bf16[128,512]{1,0:T(8,128)(2,1)S(1)} %pack.1), channel_id=1, source_target_pairs={{0,2},{2,4},{4,6},{6,8},{8,10},{10,12},{12,14},{14,16},{16,18},{18... | collective-permute-start | bytes 393224 | tf_op jit(solution)/shard_map/ppermute | solution.py:47
  4.5 8.8 %window_upper.1 = (bf16[2880,128]{1,0:T(8,128)(2,1)S(1)}, bf16[2880,2048]{1,0:T(8,128)(2,1)S(1)}, bf16[256,2048]{1,0:T(8,128)(2,1)S(1)}, bf16[256,256]{1,0:T(8,1...) custom-call(s32[32]{0:T(128)} %lengths_ref.1, ...), custom_call_target="tpu_custom_call" | custom-call | tf_op jit(solution)/shard_map/window_upper/pallas_call | solution.py:403
  13.3 0.1 collective-permute-start.2
  13.4 0.0 collective-permute-done.halo_ref
  13.4 4.9 %window_lower.1 = (bf16[2880,128]{1,0:T(8,128)(2,1)S(1)}, bf16[2880,256]{1,0:T(8,128)(2,1)S(1)}, bf16[2880,256]{1,0:T(8,128)(2,1)S(1)}, bf16[2880,1024]{1,0:T(8,128)(2,1)S(1)}) custom-call(bf16[256,2048]{1,0:T(8,128)(2,1)S(1)} %get-tuple-element.22.q_ref, bf16[256,256]{1,0:T(8,128)(2,1)S(1)} %get-tuple-element.23.k_ref, ...), custom_call_target="tpu_custom_call" | custom-call | tf_op jit(solution)/shard_map/window_lower/pallas_call | solution.py:428
  18.4 0.6 %collective-permute-start.1 = (bf16[2880,128]{1,0:T(8,128)(2,1)S(1)}, bf16[2880,128]{1,0:T(8,128)(2,1)S(1)}, u32[]{:S(2)}, u32[]{:S(2)}) collective-permute-start(bf16[2880,128]{1,0:T(8,128)(2,1)S(1)} %get-tuple-element.27.own_ref), channel_id=1, source_target_pairs={{0,1},{1,0},{2,3},{3,2},{4,5},{5,4},{6,7},{7,6},{8,9},{9,8},{10,11... | collective-permute-start | bytes 2211848 | tf_op jit(solution)/shard_map/ppermute | solution.py:52
  18.9 0.0 collective-permute-done.2.other_ref
  18.9 1.3 %norm_upper.1 = (bf16[2880,128]{1,0:T(8,128)(2,1)S(1)}, bf16[128,2880]{1,0:T(8,128)(2,1)S(1)}, bf16[128,512]{1,0:T(8,128)(2,1)S(1)}) custom-call(bf16[2880,128]{1,0:T(8,128)(2,1)S(1)} %get-tuple-element.32.own_ref, bf16[2880,128]{1,0:T(8,128)(2,1)S(1)} %collective-permute-done.2.other_ref, f32[2880]{0:T(1024)S(1)} %get-tuple-element.28.gain_ref, ...), custom_call_target="tpu_custom_call" | custom-call | tf_op jit(solution)/shard_map/norm_upper/pallas_call | solution.py:446
  20.3 1.7 %collective-permute-start.3 = (bf16[128,512]{1,0:T(8,128)(2,1)S(1)}, bf16[128,512]{1,0:T(8,128)(2,1)S(1)}, u32[]{:S(2)}, u32[]{:S(2)}) collective-permute-start(bf16[128,512]{1,0:T(8,128)(2,1)S(1)} %get-tuple-element.35.kv_up_ref), channel_id=1, source_target_pairs={{0,2},{2,4},{4,6},{6,8},{8,10},{10,12},{12,14},{14,16},{16,18},{18... | collective-permute-start | bytes 393224 | tf_op jit(solution)/shard_map/ppermute | solution.py:47
  22.0 0.0 collective-permute-done.1.other_ref
  22.0 10.4 %causal_upper.1 = (bf16[2880,128]{1,0:T(8,128)(2,1)}, bf16[128,2048]{1,0:T(8,128)(2,1)S(1)}, bf16[128,512]{1,0:T(8,128)(2,1)S(1)}, bf16[256,2048]{1,0:T(8,128)(2,1)}) custom-call(bf16[2880,128]{1,0:T(8,128)(2,1)S(1)} %get-tuple-element.27.own_ref, bf16[2880,128]{1,0:T(8,128)(2,1)S(1)} %collective-permute-done.1.other_ref, ...), custom_call_target="tpu_custom_call" | custom-call | tf_op jit(solution)/shard_map/causal_upper/pallas_call | solution.py:460
  32.4 0.0 collective-permute-done.3.halo_ref
  32.4 2.7 %causal_lower.1 = bf16[256,2048]{1,0:T(8,128)(2,1)} custom-call(bf16[128,2048]{1,0:T(8,128)(2,1)S(1)} %get-tuple-element.38.q_ref, bf16[128,512]{1,0:T(8,128)(2,1)S(1)} %get-tuple-element.39.kv_ref, bf16[128,512]{1,0:T(8,128)(2,1)S(1)} %collective-permute-done.3.halo_ref, f32[256,128]{1,0:T(8,128)S(1)} %get-tuple-element.40.bias_ref, ...), custom_call_target="tpu_custom_call", output_to_operand_aliasing={{}: (4, {})} | custom-call | tf_op jit(solution)/shard_map/causal_lower/pallas_call | solution.py:485
Async XLA Ops:
  1.5 11.9 %collective-permute-start = (bf16[128,512]{1,0:T(8,128)(2,1)S(1)}, bf16[128,512]{1,0:T(8,128)(2,1)S(1)}, u32[]{:S(2)}, u32[]{:S(2)}) collective-permute-start(bf16[128,512]{1,0:T(8,128)(2,1)S(1)} %pack.1), channel_id=1, source_target_pairs={{0,2},{2,4},{4,6},{6,8},{8,10},{10,12},{12,14},{14,16},{16,18},{18... | collective-permute-start | bytes 393224 | tf_op jit(solution)/shard_map/ppermute | solution.py:47
  13.3 5.6 %collective-permute-start.2 = (bf16[2880,128]{1,0:T(8,128)(2,1)S(1)}, bf16[2880,128]{1,0:T(8,128)(2,1)S(1)}, u32[]{:S(2)}, u32[]{:S(2)}) collective-permute-start(bf16[2880,128]{1,0:T(8,128)(2,1)S(1)} %get-tuple-element.32.own_ref), channel_id=1, source_target_pairs={{0,1},{1,0},{2,3},{3,2},{4,5},{5,4},{6,7},{7,6},{8,9},{9,8},{10,11... | collective-permute-start | bytes 2211848 | tf_op jit(solution)/shard_map/ppermute | solution.py:52
  18.4 3.6 %collective-permute-start.1 = (bf16[2880,128]{1,0:T(8,128)(2,1)S(1)}, bf16[2880,128]{1,0:T(8,128)(2,1)S(1)}, u32[]{:S(2)}, u32[]{:S(2)}) collective-permute-start(bf16[2880,128]{1,0:T(8,128)(2,1)S(1)} %get-tuple-element.27.own_ref), channel_id=1, source_target_pairs={{0,1},{1,0},{2,3},{3,2},{4,5},{5,4},{6,7},{7,6},{8,9},{9,8},{10,11... | collective-permute-start | bytes 2211848 | tf_op jit(solution)/shard_map/ppermute | solution.py:52
  20.3 12.1 %collective-permute-start.3 = (bf16[128,512]{1,0:T(8,128)(2,1)S(1)}, bf16[128,512]{1,0:T(8,128)(2,1)S(1)}, u32[]{:S(2)}, u32[]{:S(2)}) collective-permute-start(bf16[128,512]{1,0:T(8,128)(2,1)S(1)} %get-tuple-element.35.kv_up_ref), channel_id=1, source_target_pairs={{0,2},{2,4},{4,6},{6,8},{8,10},{10,12},{12,14},{14,16},{16,18},{18... | collective-permute-start | bytes 393224 | tf_op jit(solution)/shard_map/ppermute | solution.py:47

commit v4 on v3

--- a/solution.py
+++ b/solution.py
@@ -184,11 +184,11 @@
 
 
 def window_upper_kernel(
-    lengths_ref, q_ref, k_ref, v_ref, weight_ref, gain_ref,
-    out_ref, held_ref, q_held, k_held, v_held, window_bias, upper_causal, lower_causal, gain_held,
-    lengths_s, attn_s, keys_s, values_s, bias_s, sems, weight_sems, *, chunk
-):
-    half = out_ref.shape[1]
+    lengths_ref, q_ref, k_ref, v_ref, gain_ref,
+    attn_ref, q_held, k_held, v_held, window_bias, upper_causal, lower_causal, gain_held,
+    lengths_s, keys_s, values_s, bias_s, sems
+):
+    half = attn_ref.shape[1]
     upper, lower = pl.ds(half, half), pl.ds(0, half)
     first = [
         pltpu.make_async_copy(lengths_ref, lengths_s, sems.at[0]),
@@ -196,23 +196,19 @@
         pltpu.make_async_copy(v_ref.at[upper], v_held.at[upper], sems.at[2]),
         pltpu.make_async_copy(q_ref.at[upper], q_held.at[upper], sems.at[3]),
     ]
-    count = held_ref.shape[0] // chunk
-    weights = [
-        pltpu.make_async_copy(
-            weight_ref.at[pl.ds(c * chunk, chunk)], held_ref.at[pl.ds(c * chunk, chunk)], weight_sems.at[c]
-        )
-        for c in range(count)
-    ]
     last = [
         pltpu.make_async_copy(k_ref.at[lower], k_held.at[lower], sems.at[4]),
         pltpu.make_async_copy(v_ref.at[lower], v_held.at[lower], sems.at[5]),
         pltpu.make_async_copy(q_ref.at[lower], q_held.at[lower], sems.at[6]),
         pltpu.make_async_copy(gain_ref, gain_held, sems.at[7]),
     ]
-    for copy in first + weights + last:
+    for copy in first + last:
         copy.start()
     first[0].wait()
     bias_s[...] = upper_bias(lengths_s, half, WIN)
+    window_bias[...] = lower_bias(lengths_s, half, WIN)
+    upper_causal[...] = upper_bias(lengths_s, half, None)
+    lower_causal[...] = lower_bias(lengths_s, half, None)
     first[1].wait()
     stage_keys(k_held[half:], keys_s)
     first[2].wait()
@@ -222,31 +218,26 @@
     def queries_of(unit):
         return q_held[half:, unit.lane : unit.lane + 2 * LANES]
 
-    window_heads(queries_of, keys_s, values_s, bias_s, attn_s, q_held.shape[1])
-    window_bias[...] = lower_bias(lengths_s, half, WIN)
-    upper_causal[...] = upper_bias(lengths_s, half, None)
-    lower_causal[...] = lower_bias(lengths_s, half, None)
-    for c in range(count):
-        weights[c].wait()
-        part = slice(c * chunk, (c + 1) * chunk)
-        out_ref[part, :] = dot(held_ref[part, :], attn_s[...], ((1,), (0,))).astype(BF16)
+    window_heads(queries_of, keys_s, values_s, bias_s, attn_ref, q_held.shape[1])
     for copy in last:
         copy.wait()
 
 
+def project(weight_ref, attn_ref, out_ref, chunk):
+    for first in range(0, out_ref.shape[0], chunk):
+        part = slice(first, first + chunk)
+        out_ref[part, :] = dot(weight_ref[part, :], attn_ref[...], ((1,), (0,))).astype(BF16)
+
+
+def project_upper_kernel(weight_ref, attn_ref, out_ref, *, chunk):
+    project(weight_ref, attn_ref, out_ref, chunk)
+
+
 def window_lower_kernel(
-    q_ref, k_ref, v_ref, halo_ref, held_ref, bias_ref, kw_ref, vw_ref, qw_ref,
-    out_ref, key_held, value_held, query_held, attn_s, keys_s, values_s, sems, *, chunk
+    q_ref, k_ref, v_ref, halo_ref, weight_ref, bias_ref, out_ref, attn_s, keys_s, values_s, *, chunk
 ):
     half = halo_ref.shape[0]
     kv_width = k_ref.shape[1]
-    copies = [
-        pltpu.make_async_copy(kw_ref, key_held, sems.at[0]),
-        pltpu.make_async_copy(vw_ref, value_held, sems.at[1]),
-        pltpu.make_async_copy(qw_ref.at[:, pl.ds(0, query_held.shape[1])], query_held, sems.at[2]),
-    ]
-    for copy in copies:
-        copy.start()
     stage_keys(jnp.concatenate([halo_ref[:, :kv_width], k_ref[:half]], axis=0), keys_s)
     stage_values(jnp.concatenate([halo_ref[:, kv_width:], v_ref[:half]], axis=0), values_s)
 
@@ -254,11 +245,7 @@
         return q_ref[:half, unit.lane : unit.lane + 2 * LANES]
 
     window_heads(queries_of, keys_s, values_s, bias_ref, attn_s, q_ref.shape[1])
-    for first in range(0, out_ref.shape[0], chunk):
-        part = slice(first, first + chunk)
-        out_ref[part, :] = dot(held_ref[part, :], attn_s[...], ((1,), (0,))).astype(BF16)
-    for copy in copies:
-        copy.wait()
+    project(weight_ref, attn_s, out_ref, chunk)
 
 
 def add_and_norm(own_ref, other_ref, gain_ref, branch_ref, normed_ref, first_row, sum_s, keep_ref, chunk):
@@ -293,18 +280,13 @@
 
 
 def causal_upper_kernel(
-    own_ref, other_ref, gain_ref, kw_ref, vw_ref, query_held, kept_ref, normed_ref, kv_up_ref, bias_ref,
-    qw_ref, branch_ref, q_ref, kv_ref, out_ref,
-    rest_s, branch_s, out_s, normed_s, sum_s, keys_s, values_s, sems, *, chunk
+    own_ref, other_ref, gain_ref, kw_ref, vw_ref, qw_ref, kept_ref, normed_ref, kv_up_ref, bias_ref,
+    branch_ref, q_ref, kv_ref, out_ref,
+    branch_s, out_s, normed_s, sum_s, keys_s, values_s, sems, *, chunk
 ):
     half = own_ref.shape[1]
     kv_width = kw_ref.shape[1]
     q_width = qw_ref.shape[1]
-    present = query_held.shape[1]
-    rest_in = pltpu.make_async_copy(
-        qw_ref.at[:, pl.ds(present, q_width - present)], rest_s, sems.at[2]
-    )
-    rest_in.start()
     normed_s[half:, :] = normed_ref[...]
     add_and_norm(own_ref, other_ref, gain_ref, branch_s, normed_s, 0, sum_s, kept_ref, chunk)
     branch_out = pltpu.make_async_copy(branch_s, branch_ref, sems.at[0])
@@ -314,13 +296,7 @@
 
     def queries_of(unit):
         columns = slice(unit.lane, unit.lane + 2 * LANES)
-        if unit.lane == present:
-            rest_in.wait()
-        if unit.lane < present:
-            weight = query_held[:, columns]
-        else:
-            weight = rest_s[:, unit.lane - present : unit.lane - present + 2 * LANES]
-        queries = dot(normed_s[...], weight, ((1,), (0,))).astype(BF16)
+        queries = dot(normed_s[...], qw_ref[:, columns], ((1,), (0,))).astype(BF16)
         q_ref[:, columns] = queries[:half]
         return queries[half:]
 
@@ -394,17 +370,17 @@
         out_specs=vmem_specs(1)[0],
         scratch_shapes=[dma((2,))],
         compiler_params=params(16),
+        cost_estimate=pl.CostEstimate(flops=10**10, bytes_accessed=10**6, transcendentals=0),
         name="pack",
     )(keys, values)
     halo = shifted(packed, "ctx")
     attn_s = pltpu.VMEM((q_width, half), BF16)
     (
-        own_upper, held, q_held, k_held, v_held, window_bias, upper_causal, lower_causal, gain
+        attn_upper, q_held, k_held, v_held, window_bias, upper_causal, lower_causal, gain
     ) = pl.pallas_call(
-        functools.partial(window_upper_kernel, chunk=chunk),
+        window_upper_kernel,
         out_shape=(
-            pltpu.VMEM((width, half), BF16),
-            pltpu.VMEM((width, q_width), BF16),
+            attn_s,
             pltpu.VMEM((rows, q_width), BF16),
             pltpu.VMEM((rows, kv_width), BF16),
             pltpu.VMEM((rows, kv_width), BF16),
@@ -413,35 +389,34 @@
             pltpu.VMEM((rows, half), F32),
             pltpu.VMEM((width,), F32),
         ),
-        in_specs=hbm_specs(6),
-        out_specs=tuple(vmem_specs(9)),
-        scratch_shapes=[pltpu.SMEM(doc_lengths.shape, jnp.int32), attn_s]
+        in_specs=hbm_specs(5),
+        out_specs=tuple(vmem_specs(8)),
+        scratch_shapes=[pltpu.SMEM(doc_lengths.shape, jnp.int32)]
         + attention_scratch(kv_heads, half)
-        + [pltpu.VMEM((half, half), F32), dma((8,)), dma((width // chunk,))],
-        compiler_params=params(16),
+        + [pltpu.VMEM((half, half), F32), dma((8,))],
+        compiler_params=params(8),
         name="window_upper",
-    )(lengths, queries, keys, values, in_hbm(jnp.transpose(out_weight)), in_hbm(norm_gain))
-    key_weight, value_weight, query_weight = [
-        in_hbm(x) for x in (key_weight, value_weight, query_weight)
-    ]
+    )(lengths, queries, keys, values, in_hbm(norm_gain))
+    held = in_vmem(jnp.transpose(out_weight))
+    own_upper = pl.pallas_call(
+        functools.partial(project_upper_kernel, chunk=chunk),
+        out_shape=pltpu.VMEM((width, half), BF16),
+        in_specs=vmem_specs(2),
+        out_specs=vmem_specs(1)[0],
+        compiler_params=params(8),
+        name="project_upper",
+    )(held, attn_upper)
+    key_held, value_held, query_held = [in_vmem(x) for x in (key_weight, value_weight, query_weight)]
     other_upper = swapped(own_upper, "head")
-    own_lower, key_held, value_held, query_held = pl.pallas_call(
+    own_lower = pl.pallas_call(
         functools.partial(window_lower_kernel, chunk=chunk),
-        out_shape=(
-            pltpu.VMEM((width, half), BF16),
-            pltpu.VMEM((width, kv_width), BF16),
-            pltpu.VMEM((width, kv_width), BF16),
-            pltpu.VMEM((width, q_width // 2), BF16),
-        ),
-        in_specs=vmem_specs(6) + hbm_specs(3),
-        out_specs=tuple(vmem_specs(4)),
-        scratch_shapes=[attn_s] + attention_scratch(kv_heads, rows) + [dma((3,))],
+        out_shape=pltpu.VMEM((width, half), BF16),
+        in_specs=vmem_specs(6),
+        out_specs=vmem_specs(1)[0],
+        scratch_shapes=[attn_s] + attention_scratch(kv_heads, rows),
         compiler_params=params(16),
         name="window_lower",
-    )(
-        q_held, k_held, v_held, in_vmem(halo), held, window_bias,
-        key_weight, value_weight, query_weight,
-    )
+    )(q_held, k_held, v_held, in_vmem(halo), held, window_bias)
     other_lower = swapped(own_lower, "head")
     branch_upper, normed_upper, pairs_upper = pl.pallas_call(
         functools.partial(norm_upper_kernel, chunk=192),
@@ -465,22 +440,21 @@
             pltpu.VMEM((half, 2 * kv_width), BF16),
             pltpu.HBM((rows, q_width), BF16),
         ),
-        in_specs=vmem_specs(10) + hbm_specs(1),
+        in_specs=vmem_specs(10),
         out_specs=(hbm_specs(1)[0], *vmem_specs(2), hbm_specs(1)[0]),
         scratch_shapes=[
-            pltpu.VMEM((width, q_width // 2), BF16),
             pltpu.VMEM((width, half), BF16),
             pltpu.VMEM((half, q_width), BF16),
             pltpu.VMEM((rows, width), BF16),
             pltpu.VMEM((width, half), F32),
         ]
         + attention_scratch(kv_heads, half)
-        + [dma((3,))],
-        compiler_params=params(20),
+        + [dma((2,))],
+        compiler_params=params(16),
         name="causal_upper",
     )(
         own_lower, other_lower, gain, key_held, value_held, query_held,
-        branch_upper, normed_upper, pairs_upper, upper_causal, query_weight,
+        branch_upper, normed_upper, pairs_upper, upper_causal,
     )
     causal_out = pl.pallas_call(
         causal_lower_kernel,

time: 35.4 us -> 33.1 us (0.935)
  Pallas kernels: 29 us -> 25.9 us
  waiting for transfers between devices: 0.01 us -> 1.69 us
  starting transfers between devices: 5.35 us -> 4.38 us
    pallas_call x1 -> x2, Pallas kernels: 8.79 us -> 5.66 us  [the longest x1 3.21 us: local(): pl.pallas_call(functools.partial(project_upper_kernel, chunk=chunk), out_...]
    ppermute x2, waiting for transfers between devices: 0.01 us -> 1.68 us  [shifted(): return lax.ppermute(block, axis, [(i, (i + 1) % size) for i in range(size)])]
    ppermute x2, starting transfers between devices: 0.62 us -> 0.14 us  [swapped(): return lax.ppermute(block, axis, [(i, size - 1 - i) for i in range(size)])]
    ppermute x2, starting transfers between devices: 4.72 us -> 4.24 us  [shifted(): return lax.ppermute(block, axis, [(i, (i + 1) % size) for i in range(size)])]
  transfers between devices with their start and end apart: 4 -> 4, of which waited for: 0 -> 1; matrix products, arithmetic and copies ran while one was open for 0% -> 0% of each run, Pallas kernels for 72% -> 67%
where the time goes in v4:
time: 33.1 us; the launch traced here: 33 us
  Pallas kernels  25.9 us (78%)
  starting transfers between devices  4.38 us (13%)
  waiting for transfers between devices  1.69 us (5%)
  between operations  0.95 us (3%)
    pallas_call x1, Pallas kernels, local(): pl.pallas_call(functools.partial(causal_upper_kernel, chunk=192), out_sha...  10.4 us
    pallas_call x1, Pallas kernels, local(): pl.pallas_call(functools.partial(window_lower_kernel, chunk=chunk), out_s...  4.88 us
    ppermute x2, starting transfers between devices, shifted(): return lax.ppermute(block, axis, [(i, (i + 1) % size) for i in range(size)])  4.24 us
    pallas_call x1, Pallas kernels, local(): pl.pallas_call(functools.partial(project_upper_kernel, chunk=chunk), out_...  3.21 us
    pallas_call x1, Pallas kernels, local(): pl.pallas_call(causal_lower_kernel, out_shape=pltpu.HBM((rows, q_width),...  2.66 us
    pallas_call x1, Pallas kernels, local(): pl.pallas_call(window_upper_kernel, out_shape=(attn_s, pltpu.VMEM((rows,...  2.45 us
    ppermute x2, waiting for transfers between devices, shifted(): return lax.ppermute(block, axis, [(i, (i + 1) % size) for i in range(size)])  1.68 us
    pallas_call x1, Pallas kernels, local(): pl.pallas_call(functools.partial(norm_upper_kernel, chunk=192), out_shape...  1.33 us
  transfers between devices with their start and end apart: 4, of which 1 were waited for; matrix products, arithmetic and copies ran while one was open for 0% of the time, Pallas kernels for 67%

profile of v4, /device:TPU:0, one launch (start us, length us, event | category | flops | bytes accessed | tf_op | source)
XLA Modules:
  0.0 33.0 jit_solution(5892971310524604983)
XLA Ops:
  0.6 0.0 copy-start
  0.6 1.0 %pack.1 = bf16[128,512]{1,0:T(8,128)(2,1)S(1)} custom-call(bf16[256,256]{1,0:T(8,128)(2,1)} %k_ref.3, bf16[256,256]{1,0:T(8,128)(2,1)} %v_ref.3), custom_call_target="tpu_custom_call" | custom-call | flops 10000000000 | bytes 1000000 | tf_op jit(solution)/shard_map/pack/pallas_call | solution.py:366
  1.7 3.0 %collective-permute-start = (bf16[128,512]{1,0:T(8,128)(2,1)S(1)}, bf16[128,512]{1,0:T(8,128)(2,1)S(1)}, u32[]{:S(2)}, u32[]{:S(2)}) collective-permute-start(bf16[128,512]{1,0:T(8,128)(2,1)S(1)} %pack.1), channel_id=1, source_target_pairs={{0,2},{2,4},{4,6},{6,8},{8,10},{10,12},{12,14},{14,16},{16,18},{18... | collective-permute-start | bytes 393224 | tf_op jit(solution)/shard_map/ppermute | solution.py:47
  4.7 2.4 %window_upper.1 = (bf16[2048,128]{1,0:T(8,128)(2,1)S(1)}, bf16[256,2048]{1,0:T(8,128)(2,1)S(1)}, bf16[256,256]{1,0:T(8,128)(2,1)S(1)}, bf16[256,256]{1,0:T(8,128...) custom-call(s32[32]{0:T(128)} %lengths_ref.1, ...), custom_call_target="tpu_custom_call" | custom-call | tf_op jit(solution)/shard_map/window_upper/pallas_call | solution.py:380
  7.1 0.0 copy-done
  7.1 0.0 copy-start.1
  7.2 0.0 copy-start.2
  7.2 0.0 slice-start
  7.2 0.0 slice-start.1
  7.2 3.2 %project_upper.1.own_ref = bf16[2880,128]{1,0:T(8,128)(2,1)S(1)} custom-call(bf16[2880,2048]{1,0:T(8,128)(2,1)S(1)} %bitcast.2, bf16[2048,128]{1,0:T(8,128)(2,1)S(1)} %get-tuple-element.22.attn_ref), custom_call_target="tpu_custom_call" | custom-call | tf_op jit(solution)/shard_map/project_upper/pallas_call | solution.py:401
  10.4 0.1 collective-permute-start.2
  10.5 1.7 %collective-permute-done.halo_ref = bf16[128,512]{1,0:T(8,128)(2,1)S(1)} collective-permute-done((bf16[128,512]{1,0:T(8,128)(2,1)S(1)}, bf16[128,512]{1,0:T(8,128)(2,1)S(1)}, u32[]{:S(2)}, u32[]{:S(2)}) %collective-permute-start) | collective-permute-done | bytes 131104 | tf_op jit(solution)/shard_map/ppermute | solution.py:47
  12.2 0.0 slice-start.2
  12.2 4.9 %window_lower.1.own_ref = bf16[2880,128]{1,0:T(8,128)(2,1)S(1)} custom-call(bf16[256,2048]{1,0:T(8,128)(2,1)S(1)} %get-tuple-element.17.q_ref, bf16[256,256]{1,0:T(8,128)(2,1)S(1)} %get-tuple-element.18.k_ref, bf16[256,256]{1,0:T(8,128)(2,1)S(1)} %get-tuple-element.19.v_ref, bf16[128,512]{1,0:T(8,128)(2,1)S(1)} %collective-permute-done.halo_ref, ...), custom_call_target="tpu_custom_call" | custom-call | tf_op jit(solution)/shard_map/window_lower/pallas_call | solution.py:411
  17.1 0.1 collective-permute-start.1
  17.1 0.0 collective-permute-done.2.other_ref
  17.1 0.0 copy-done.1
  17.2 0.0 copy-done.2
  17.2 1.3 %norm_upper.1 = (bf16[2880,128]{1,0:T(8,128)(2,1)S(1)}, bf16[128,2880]{1,0:T(8,128)(2,1)S(1)}, bf16[128,512]{1,0:T(8,128)(2,1)S(1)}) custom-call(bf16[2880,128]{1,0:T(8,128)(2,1)S(1)} %project_upper.1.own_ref, bf16[2880,128]{1,0:T(8,128)(2,1)S(1)} %collective-permute-done.2.other_ref, f32[2880]{0:T(1024)S(1)} %get-tuple-element.21.gain_ref, ...), custom_call_target="tpu_custom_call" | custom-call | tf_op jit(solution)/shard_map/norm_upper/pallas_call | solution.py:421
  18.5 1.2 %collective-permute-start.3 = (bf16[128,512]{1,0:T(8,128)(2,1)S(1)}, bf16[128,512]{1,0:T(8,128)(2,1)S(1)}, u32[]{:S(2)}, u32[]{:S(2)}) collective-permute-start(bf16[128,512]{1,0:T(8,128)(2,1)S(1)} %get-tuple-element.25.kv_up_ref), channel_id=1, source_target_pairs={{0,2},{2,4},{4,6},{6,8},{8,10},{10,12},{12,14},{14,16},{16,18},{18... | collective-permute-start | bytes 393224 | tf_op jit(solution)/shard_map/ppermute | solution.py:47
  19.8 0.0 collective-permute-done.1.other_ref
  19.8 0.0 slice-done
  19.8 0.0 slice-done.1
  19.8 0.0 slice-done.2
  19.8 10.4 %causal_upper.1 = (bf16[2880,128]{1,0:T(8,128)(2,1)}, bf16[128,2048]{1,0:T(8,128)(2,1)S(1)}, bf16[128,512]{1,0:T(8,128)(2,1)S(1)}, bf16[256,2048]{1,0:T(8,128)(2,1)}) custom-call(bf16[2880,128]{1,0:T(8,128)(2,1)S(1)} %window_lower.1.own_ref, bf16[2880,128]{1,0:T(8,128)(2,1)S(1)} %collective-permute-done.1.other_ref, f32[2880]{0:T(1024)S(1)} %get-tuple-element.21.gain_ref, ...), custom_call_target="tpu_custom_call" | custom-call | tf_op jit(solution)/shard_map/causal_upper/pallas_call | solution.py:435
  30.2 0.0 collective-permute-done.3.halo_ref
  30.2 2.7 %causal_lower.1 = bf16[256,2048]{1,0:T(8,128)(2,1)} custom-call(bf16[128,2048]{1,0:T(8,128)(2,1)S(1)} %get-tuple-element.28.q_ref, bf16[128,512]{1,0:T(8,128)(2,1)S(1)} %get-tuple-element.29.kv_ref, bf16[128,512]{1,0:T(8,128)(2,1)S(1)} %collective-permute-done.3.halo_ref, f32[256,128]{1,0:T(8,128)S(1)} %get-tuple-element.30.bias_ref, ...), custom_call_target="tpu_custom_call", output_to_operand_aliasing={{}: (4, {})} | custom-call | tf_op jit(solution)/shard_map/causal_lower/pallas_call | solution.py:459
  (1 shorter events, 0.0 us)
Async XLA Ops:
  0.6 6.5 %copy-start = (bf16[2048,2880]{0,1:T(8,128)(2,1)S(1)}, bf16[2048,2880]{0,1:T(8,128)(2,1)}, u32[]{:S(2)}) copy-start(bf16[2048,2880]{0,1:T(8,128)(2,1)} %param.12) | copy-start | bytes 35389444
  1.7 10.5 %collective-permute-start = (bf16[128,512]{1,0:T(8,128)(2,1)S(1)}, bf16[128,512]{1,0:T(8,128)(2,1)S(1)}, u32[]{:S(2)}, u32[]{:S(2)}) collective-permute-start(bf16[128,512]{1,0:T(8,128)(2,1)S(1)} %pack.1), channel_id=1, source_target_pairs={{0,2},{2,4},{4,6},{6,8},{8,10},{10,12},{12,14},{14,16},{16,18},{18... | collective-permute-start | bytes 393224 | tf_op jit(solution)/shard_map/ppermute | solution.py:47
  7.1 10.0 %copy-start.1 = (bf16[2880,256]{1,0:T(8,128)(2,1)S(1)}, bf16[2880,256]{1,0:T(8,128)(2,1)}, u32[]{:S(2)}) copy-start(bf16[2880,256]{1,0:T(8,128)(2,1)} %kw_ref.3) | copy-start | bytes 4423684
  7.2 10.0 %copy-start.2 = (bf16[2880,256]{1,0:T(8,128)(2,1)S(1)}, bf16[2880,256]{1,0:T(8,128)(2,1)}, u32[]{:S(2)}) copy-start(bf16[2880,256]{1,0:T(8,128)(2,1)} %vw_ref.3) | copy-start | bytes 4423684
  7.2 12.6 %slice-start = ((s8[11796480]{0:T(1024)(128)(4,1)}), s8[4194304]{0:T(1024)(128)(4,1)S(1)}, s32[]{:S(2)}) async-start(s8[11796480]{0:T(1024)(128)(4,1)} %bitcast.4), calls=%async_computation | async-start | bytes 8388608
  7.2 12.6 %slice-start.1 = ((s8[11796480]{0:T(1024)(128)(4,1)}), s8[4194304]{0:T(1024)(128)(4,1)S(1)}, s32[]{:S(2)}) async-start(s8[11796480]{0:T(1024)(128)(4,1)} %bitcast.4), calls=%async_computation.1 | async-start | bytes 8388608
  10.4 6.7 %collective-permute-start.2 = (bf16[2880,128]{1,0:T(8,128)(2,1)S(1)}, bf16[2880,128]{1,0:T(8,128)(2,1)S(1)}, u32[]{:S(2)}, u32[]{:S(2)}) collective-permute-start(bf16[2880,128]{1,0:T(8,128)(2,1)S(1)} %project_upper.1.own_ref), channel_id=1, source_target_pairs={{0,1},{1,0},{2,3},{3,2},{4,5},{5,4},{6,7},{7,6},{8,9},{9,8},{10,11... | collective-permute-start | bytes 2211848 | tf_op jit(solution)/shard_map/ppermute | solution.py:52
  12.2 7.6 %slice-start.2 = ((s8[11796480]{0:T(1024)(128)(4,1)}), s8[3407872]{0:T(1024)(128)(4,1)S(1)}, s32[]{:S(2)}) async-start(s8[11796480]{0:T(1024)(128)(4,1)} %bitcast.4), calls=%async_computation.2 | async-start | bytes 6815744
  17.1 2.7 %collective-permute-start.1 = (bf16[2880,128]{1,0:T(8,128)(2,1)S(1)}, bf16[2880,128]{1,0:T(8,128)(2,1)S(1)}, u32[]{:S(2)}, u32[]{:S(2)}) collective-permute-start(bf16[2880,128]{1,0:T(8,128)(2,1)S(1)} %window_lower.1.own_ref), channel_id=1, source_target_pairs={{0,1},{1,0},{2,3},{3,2},{4,5},{5,4},{6,7},{7,6},{8,9},{9,8},{10,11... | collective-permute-start | bytes 2211848 | tf_op jit(solution)/shard_map/ppermute | solution.py:52
  18.5 11.7 %collective-permute-start.3 = (bf16[128,512]{1,0:T(8,128)(2,1)S(1)}, bf16[128,512]{1,0:T(8,128)(2,1)S(1)}, u32[]{:S(2)}, u32[]{:S(2)}) collective-permute-start(bf16[128,512]{1,0:T(8,128)(2,1)S(1)} %get-tuple-element.25.kv_up_ref), channel_id=1, source_target_pairs={{0,2},{2,4},{4,6},{6,8},{8,10},{10,12},{12,14},{14,16},{16,18},{18... | collective-permute-start | bytes 393224 | tf_op jit(solution)/shard_map/ppermute | solution.py:47

commit v5 on v4

--- a/solution.py
+++ b/solution.py
@@ -121,7 +121,7 @@
     for side in range(2):
         masked = scores[side * count : (side + 1) * count] + wide
         highest = jnp.max(masked, axis=0, keepdims=True)
-        patterns.append(jnp.exp(masked - highest).astype(BF16))
+        patterns.append(jnp.exp((masked - highest).astype(BF16)))
     weighted = dot(values_ref[unit.g], jnp.concatenate(patterns, axis=1), ((1,), (0,)))
     return weighted[:HD] * (1.0 / weighted[HD : HD + 1])
 
@@ -282,7 +282,7 @@
 def causal_upper_kernel(
     own_ref, other_ref, gain_ref, kw_ref, vw_ref, qw_ref, kept_ref, normed_ref, kv_up_ref, bias_ref,
     branch_ref, q_ref, kv_ref, out_ref,
-    branch_s, out_s, normed_s, sum_s, keys_s, values_s, sems, *, chunk
+    branch_s, out_s, upper_q_s, normed_s, sum_s, keys_s, values_s, sems, *, chunk
 ):
     half = own_ref.shape[1]
     kv_width = kw_ref.shape[1]
@@ -294,11 +294,15 @@
     stage_keys(kv_up_ref[:, :kv_width], keys_s)
     stage_values(kv_up_ref[:, kv_width:], values_s)
 
-    def queries_of(unit):
-        columns = slice(unit.lane, unit.lane + 2 * LANES)
+    piece = q_width // 2
+    for first in range(0, q_width, piece):
+        columns = slice(first, first + piece)
         queries = dot(normed_s[...], qw_ref[:, columns], ((1,), (0,))).astype(BF16)
         q_ref[:, columns] = queries[:half]
-        return queries[half:]
+        upper_q_s[:, columns] = queries[half:]
+
+    def queries_of(unit):
+        return upper_q_s[:, unit.lane : unit.lane + 2 * LANES]
 
     causal_heads(queries_of, keys_s, values_s, bias_ref, out_s, q_width, lambda unit: None)
     upper_out = pltpu.make_async_copy(out_s, out_ref.at[pl.ds(half, half)], sems.at[1])
@@ -445,6 +449,7 @@
         scratch_shapes=[
             pltpu.VMEM((width, half), BF16),
             pltpu.VMEM((half, q_width), BF16),
+            pltpu.VMEM((half, q_width), BF16),
             pltpu.VMEM((rows, width), BF16),
             pltpu.VMEM((width, half), F32),
         ]

time: 33.1 us -> 31.1 us (0.940)
  Pallas kernels: 25.9 us -> 22 us
  waiting for transfers between devices: 1.69 us -> 3.55 us
    pallas_call x1, Pallas kernels: 10.4 us -> 6.56 us  [local(): pl.pallas_call(functools.partial(causal_upper_kernel, chunk=192), out_sha...]
    ppermute x2, waiting for transfers between devices: 1.68 us -> 3.54 us  [shifted(): return lax.ppermute(block, axis, [(i, (i + 1) % size) for i in range(size)])]
  transfers between devices with their start and end apart: 4 -> 4, of which waited for: 1 -> 2; matrix products, arithmetic and copies ran while one was open for 0% -> 0% of each run, Pallas kernels for 67% -> 60%
where the time goes in v5:
time: 31.1 us; the launch traced here: 30.9 us
  Pallas kernels  22 us (71%)
  starting transfers between devices  4.38 us (14%)
  waiting for transfers between devices  3.55 us (11%)
  between operations  0.94 us (3%)
    pallas_call x1, Pallas kernels, local(): pl.pallas_call(functools.partial(causal_upper_kernel, chunk=192), out_sha...  6.56 us
    pallas_call x1, Pallas kernels, local(): pl.pallas_call(functools.partial(window_lower_kernel, chunk=chunk), out_s...  4.84 us
    ppermute x2, starting transfers between devices, shifted(): return lax.ppermute(block, axis, [(i, (i + 1) % size) for i in range(size)])  4.24 us
    ppermute x2, waiting for transfers between devices, shifted(): return lax.ppermute(block, axis, [(i, (i + 1) % size) for i in range(size)])  3.54 us
    pallas_call x1, Pallas kernels, local(): pl.pallas_call(functools.partial(project_upper_kernel, chunk=chunk), out_...  3.21 us
    pallas_call x1, Pallas kernels, local(): pl.pallas_call(causal_lower_kernel, out_shape=pltpu.HBM((rows, q_width),...  2.58 us
    pallas_call x1, Pallas kernels, local(): pl.pallas_call(window_upper_kernel, out_shape=(attn_s, pltpu.VMEM((rows,...  2.45 us
    pallas_call x1, Pallas kernels, local(): pl.pallas_call(functools.partial(norm_upper_kernel, chunk=192), out_shape...  1.34 us
  transfers between devices with their start and end apart: 4, of which 2 were waited for; matrix products, arithmetic and copies ran while one was open for 0% of the time, Pallas kernels for 60%

profile of v5, /device:TPU:0, one launch (start us, length us, event | category | flops | bytes accessed | tf_op | source)
XLA Modules:
  0.0 30.9 jit_solution(14823151454748857618)
XLA Ops:
  0.6 0.0 copy-start
  0.6 1.0 %pack.1 = bf16[128,512]{1,0:T(8,128)(2,1)S(1)} custom-call(bf16[256,256]{1,0:T(8,128)(2,1)} %k_ref.3, bf16[256,256]{1,0:T(8,128)(2,1)} %v_ref.3), custom_call_target="tpu_custom_call" | custom-call | flops 10000000000 | bytes 1000000 | tf_op jit(solution)/shard_map/pack/pallas_call | solution.py:370
  1.7 3.0 %collective-permute-start = (bf16[128,512]{1,0:T(8,128)(2,1)S(1)}, bf16[128,512]{1,0:T(8,128)(2,1)S(1)}, u32[]{:S(2)}, u32[]{:S(2)}) collective-permute-start(bf16[128,512]{1,0:T(8,128)(2,1)S(1)} %pack.1), channel_id=1, source_target_pairs={{0,2},{2,4},{4,6},{6,8},{8,10},{10,12},{12,14},{14,16},{16,18},{18... | collective-permute-start | bytes 393224 | tf_op jit(solution)/shard_map/ppermute | solution.py:47
  4.7 2.5 %window_upper.1 = (bf16[2048,128]{1,0:T(8,128)(2,1)S(1)}, bf16[256,2048]{1,0:T(8,128)(2,1)S(1)}, bf16[256,256]{1,0:T(8,128)(2,1)S(1)}, bf16[256,256]{1,0:T(8,128...) custom-call(s32[32]{0:T(128)} %lengths_ref.1, ...), custom_call_target="tpu_custom_call" | custom-call | tf_op jit(solution)/shard_map/window_upper/pallas_call | solution.py:384
  7.1 0.0 copy-done
  7.1 0.0 copy-start.1
  7.2 0.0 copy-start.2
  7.2 0.0 slice-start
  7.2 0.0 slice-start.1
  7.2 3.2 %project_upper.1.own_ref = bf16[2880,128]{1,0:T(8,128)(2,1)S(1)} custom-call(bf16[2880,2048]{1,0:T(8,128)(2,1)S(1)} %bitcast.2, bf16[2048,128]{1,0:T(8,128)(2,1)S(1)} %get-tuple-element.22.attn_ref), custom_call_target="tpu_custom_call" | custom-call | tf_op jit(solution)/shard_map/project_upper/pallas_call | solution.py:405
  10.4 0.1 collective-permute-start.2
  10.5 1.7 %collective-permute-done.halo_ref = bf16[128,512]{1,0:T(8,128)(2,1)S(1)} collective-permute-done((bf16[128,512]{1,0:T(8,128)(2,1)S(1)}, bf16[128,512]{1,0:T(8,128)(2,1)S(1)}, u32[]{:S(2)}, u32[]{:S(2)}) %collective-permute-start) | collective-permute-done | bytes 131104 | tf_op jit(solution)/shard_map/ppermute | solution.py:47
  12.2 0.0 slice-start.2
  12.2 4.8 %window_lower.1.own_ref = bf16[2880,128]{1,0:T(8,128)(2,1)S(1)} custom-call(bf16[256,2048]{1,0:T(8,128)(2,1)S(1)} %get-tuple-element.17.q_ref, bf16[256,256]{1,0:T(8,128)(2,1)S(1)} %get-tuple-element.18.k_ref, bf16[256,256]{1,0:T(8,128)(2,1)S(1)} %get-tuple-element.19.v_ref, bf16[128,512]{1,0:T(8,128)(2,1)S(1)} %collective-permute-done.halo_ref, ...), custom_call_target="tpu_custom_call" | custom-call | tf_op jit(solution)/shard_map/window_lower/pallas_call | solution.py:415
  17.0 0.1 collective-permute-start.1
  17.1 0.0 collective-permute-done.2.other_ref
  17.1 0.0 copy-done.1
  17.1 0.0 copy-done.2
  17.1 1.3 %norm_upper.1 = (bf16[2880,128]{1,0:T(8,128)(2,1)S(1)}, bf16[128,2880]{1,0:T(8,128)(2,1)S(1)}, bf16[128,512]{1,0:T(8,128)(2,1)S(1)}) custom-call(bf16[2880,128]{1,0:T(8,128)(2,1)S(1)} %project_upper.1.own_ref, bf16[2880,128]{1,0:T(8,128)(2,1)S(1)} %collective-permute-done.2.other_ref, f32[2880]{0:T(1024)S(1)} %get-tuple-element.21.gain_ref, ...), custom_call_target="tpu_custom_call" | custom-call | tf_op jit(solution)/shard_map/norm_upper/pallas_call | solution.py:425
  18.5 1.3 %collective-permute-start.3 = (bf16[128,512]{1,0:T(8,128)(2,1)S(1)}, bf16[128,512]{1,0:T(8,128)(2,1)S(1)}, u32[]{:S(2)}, u32[]{:S(2)}) collective-permute-start(bf16[128,512]{1,0:T(8,128)(2,1)S(1)} %get-tuple-element.25.kv_up_ref), channel_id=1, source_target_pairs={{0,2},{2,4},{4,6},{6,8},{8,10},{10,12},{12,14},{14,16},{16,18},{18... | collective-permute-start | bytes 393224 | tf_op jit(solution)/shard_map/ppermute | solution.py:47
  19.7 0.0 collective-permute-done.1.other_ref
  19.7 0.0 slice-done
  19.7 0.0 slice-done.1
  19.7 0.0 slice-done.2
  19.7 6.6 %causal_upper.1 = (bf16[2880,128]{1,0:T(8,128)(2,1)}, bf16[128,2048]{1,0:T(8,128)(2,1)S(1)}, bf16[128,512]{1,0:T(8,128)(2,1)S(1)}, bf16[256,2048]{1,0:T(8,128)(2,1)}) custom-call(bf16[2880,128]{1,0:T(8,128)(2,1)S(1)} %window_lower.1.own_ref, bf16[2880,128]{1,0:T(8,128)(2,1)S(1)} %collective-permute-done.1.other_ref, f32[2880]{0:T(1024)S(1)} %get-tuple-element.21.gain_ref, ...), custom_call_target="tpu_custom_call" | custom-call | tf_op jit(solution)/shard_map/causal_upper/pallas_call | solution.py:439
  26.3 1.9 %collective-permute-done.3.halo_ref = bf16[128,512]{1,0:T(8,128)(2,1)S(1)} collective-permute-done((bf16[128,512]{1,0:T(8,128)(2,1)S(1)}, bf16[128,512]{1,0:T(8,128)(2,1)S(1)}, u32[]{:S(2)}, u32[]{:S(2)}) %collective-permute-start.3) | collective-permute-done | bytes 131104 | tf_op jit(solution)/shard_map/ppermute | solution.py:47
  28.2 2.6 %causal_lower.1 = bf16[256,2048]{1,0:T(8,128)(2,1)} custom-call(bf16[128,2048]{1,0:T(8,128)(2,1)S(1)} %get-tuple-element.28.q_ref, bf16[128,512]{1,0:T(8,128)(2,1)S(1)} %get-tuple-element.29.kv_ref, bf16[128,512]{1,0:T(8,128)(2,1)S(1)} %collective-permute-done.3.halo_ref, f32[256,128]{1,0:T(8,128)S(1)} %get-tuple-element.30.bias_ref, ...), custom_call_target="tpu_custom_call", output_to_operand_aliasing={{}: (4, {})} | custom-call | tf_op jit(solution)/shard_map/causal_lower/pallas_call | solution.py:464
  (1 shorter events, 0.0 us)
Async XLA Ops:
  0.6 6.5 %copy-start = (bf16[2048,2880]{0,1:T(8,128)(2,1)S(1)}, bf16[2048,2880]{0,1:T(8,128)(2,1)}, u32[]{:S(2)}) copy-start(bf16[2048,2880]{0,1:T(8,128)(2,1)} %param.12) | copy-start | bytes 35389444
  1.7 10.5 %collective-permute-start = (bf16[128,512]{1,0:T(8,128)(2,1)S(1)}, bf16[128,512]{1,0:T(8,128)(2,1)S(1)}, u32[]{:S(2)}, u32[]{:S(2)}) collective-permute-start(bf16[128,512]{1,0:T(8,128)(2,1)S(1)} %pack.1), channel_id=1, source_target_pairs={{0,2},{2,4},{4,6},{6,8},{8,10},{10,12},{12,14},{14,16},{16,18},{18... | collective-permute-start | bytes 393224 | tf_op jit(solution)/shard_map/ppermute | solution.py:47
  7.1 10.0 %copy-start.1 = (bf16[2880,256]{1,0:T(8,128)(2,1)S(1)}, bf16[2880,256]{1,0:T(8,128)(2,1)}, u32[]{:S(2)}) copy-start(bf16[2880,256]{1,0:T(8,128)(2,1)} %kw_ref.3) | copy-start | bytes 4423684
  7.2 10.0 %copy-start.2 = (bf16[2880,256]{1,0:T(8,128)(2,1)S(1)}, bf16[2880,256]{1,0:T(8,128)(2,1)}, u32[]{:S(2)}) copy-start(bf16[2880,256]{1,0:T(8,128)(2,1)} %vw_ref.3) | copy-start | bytes 4423684
  7.2 12.6 %slice-start = ((s8[11796480]{0:T(1024)(128)(4,1)}), s8[4194304]{0:T(1024)(128)(4,1)S(1)}, s32[]{:S(2)}) async-start(s8[11796480]{0:T(1024)(128)(4,1)} %bitcast.4), calls=%async_computation | async-start | bytes 8388608
  7.2 12.5 %slice-start.1 = ((s8[11796480]{0:T(1024)(128)(4,1)}), s8[4194304]{0:T(1024)(128)(4,1)S(1)}, s32[]{:S(2)}) async-start(s8[11796480]{0:T(1024)(128)(4,1)} %bitcast.4), calls=%async_computation.1 | async-start | bytes 8388608
  10.4 6.7 %collective-permute-start.2 = (bf16[2880,128]{1,0:T(8,128)(2,1)S(1)}, bf16[2880,128]{1,0:T(8,128)(2,1)S(1)}, u32[]{:S(2)}, u32[]{:S(2)}) collective-permute-start(bf16[2880,128]{1,0:T(8,128)(2,1)S(1)} %project_upper.1.own_ref), channel_id=1, source_target_pairs={{0,1},{1,0},{2,3},{3,2},{4,5},{5,4},{6,7},{7,6},{8,9},{9,8},{10,11... | collective-permute-start | bytes 2211848 | tf_op jit(solution)/shard_map/ppermute | solution.py:52
  12.2 7.6 %slice-start.2 = ((s8[11796480]{0:T(1024)(128)(4,1)}), s8[3407872]{0:T(1024)(128)(4,1)S(1)}, s32[]{:S(2)}) async-start(s8[11796480]{0:T(1024)(128)(4,1)} %bitcast.4), calls=%async_computation.2 | async-start | bytes 6815744
  17.0 2.7 %collective-permute-start.1 = (bf16[2880,128]{1,0:T(8,128)(2,1)S(1)}, bf16[2880,128]{1,0:T(8,128)(2,1)S(1)}, u32[]{:S(2)}, u32[]{:S(2)}) collective-permute-start(bf16[2880,128]{1,0:T(8,128)(2,1)S(1)} %window_lower.1.own_ref), channel_id=1, source_target_pairs={{0,1},{1,0},{2,3},{3,2},{4,5},{5,4},{6,7},{7,6},{8,9},{9,8},{10,11... | collective-permute-start | bytes 2211848 | tf_op jit(solution)/shard_map/ppermute | solution.py:52
  18.5 9.7 %collective-permute-start.3 = (bf16[128,512]{1,0:T(8,128)(2,1)S(1)}, bf16[128,512]{1,0:T(8,128)(2,1)S(1)}, u32[]{:S(2)}, u32[]{:S(2)}) collective-permute-start(bf16[128,512]{1,0:T(8,128)(2,1)S(1)} %get-tuple-element.25.kv_up_ref), channel_id=1, source_target_pairs={{0,2},{2,4},{4,6},{6,8},{8,10},{10,12},{12,14},{14,16},{16,18},{18... | collective-permute-start | bytes 393224 | tf_op jit(solution)/shard_map/ppermute | solution.py:47

commit v6 on v5

--- a/solution.py
+++ b/solution.py
@@ -42,9 +42,22 @@
     return lax.dot_general(a, b, (dims, ((), ())), preferred_element_type=F32)
 
 
-def shifted(block, axis):
+def neighbours(block, axis):
     size = lax.axis_size(axis)
-    return lax.ppermute(block, axis, [(i, (i + 1) % size) for i in range(size)])
+
+    def swap(first):
+        partner = list(range(size))
+        for i in range(first, size - 1, 2):
+            partner[i], partner[i + 1] = i + 1, i
+        return lax.ppermute(block, axis, list(enumerate(partner)))
+
+    odd, even = swap(1), swap(0)
+    return even, odd
+
+
+def chosen(even_ref, odd_ref):
+    is_odd = lax.rem(lax.axis_index("ctx"), 2) == 1
+    return jnp.where(is_odd, even_ref[...], odd_ref[...])
 
 
 def swapped(block, axis):
@@ -234,12 +247,14 @@
 
 
 def window_lower_kernel(
-    q_ref, k_ref, v_ref, halo_ref, weight_ref, bias_ref, out_ref, attn_s, keys_s, values_s, *, chunk
+    q_ref, k_ref, v_ref, even_ref, odd_ref, weight_ref, bias_ref,
+    out_ref, attn_s, keys_s, values_s, *, chunk
 ):
-    half = halo_ref.shape[0]
+    half = even_ref.shape[0]
     kv_width = k_ref.shape[1]
-    stage_keys(jnp.concatenate([halo_ref[:, :kv_width], k_ref[:half]], axis=0), keys_s)
-    stage_values(jnp.concatenate([halo_ref[:, kv_width:], v_ref[:half]], axis=0), values_s)
+    halo = chosen(even_ref, odd_ref)
+    stage_keys(jnp.concatenate([halo[:, :kv_width], k_ref[:half]], axis=0), keys_s)
+    stage_values(jnp.concatenate([halo[:, kv_width:], v_ref[:half]], axis=0), values_s)
 
     def queries_of(unit):
         return q_ref[:half, unit.lane : unit.lane + 2 * LANES]
@@ -314,12 +329,13 @@
 
 
 def causal_lower_kernel(
-    q_ref, kv_ref, halo_ref, bias_ref, given_ref, out_ref, out_s, keys_s, values_s, sems
+    q_ref, kv_ref, even_ref, odd_ref, bias_ref, given_ref, out_ref, out_s, keys_s, values_s, sems
 ):
     half, q_width = q_ref.shape
     kv_width = kv_ref.shape[1] // 2
-    stage_keys(jnp.concatenate([halo_ref[:, :kv_width], kv_ref[:, :kv_width]], axis=0), keys_s)
-    stage_values(jnp.concatenate([halo_ref[:, kv_width:], kv_ref[:, kv_width:]], axis=0), values_s)
+    halo = chosen(even_ref, odd_ref)
+    stage_keys(jnp.concatenate([halo[:, :kv_width], kv_ref[:, :kv_width]], axis=0), keys_s)
+    stage_values(jnp.concatenate([halo[:, kv_width:], kv_ref[:, kv_width:]], axis=0), values_s)
     copies = []
 
     def queries_of(unit):
@@ -377,7 +393,7 @@
         cost_estimate=pl.CostEstimate(flops=10**10, bytes_accessed=10**6, transcendentals=0),
         name="pack",
     )(keys, values)
-    halo = shifted(packed, "ctx")
+    halos = [in_vmem(x) for x in neighbours(packed, "ctx")]
     attn_s = pltpu.VMEM((q_width, half), BF16)
     (
         attn_upper, q_held, k_held, v_held, window_bias, upper_causal, lower_causal, gain
@@ -415,12 +431,12 @@
     own_lower = pl.pallas_call(
         functools.partial(window_lower_kernel, chunk=chunk),
         out_shape=pltpu.VMEM((width, half), BF16),
-        in_specs=vmem_specs(6),
+        in_specs=vmem_specs(7),
         out_specs=vmem_specs(1)[0],
         scratch_shapes=[attn_s] + attention_scratch(kv_heads, rows),
         compiler_params=params(16),
         name="window_lower",
-    )(q_held, k_held, v_held, in_vmem(halo), held, window_bias)
+    )(q_held, k_held, v_held, *halos, held, window_bias)
     other_lower = swapped(own_lower, "head")
     branch_upper, normed_upper, pairs_upper = pl.pallas_call(
         functools.partial(norm_upper_kernel, chunk=192),
@@ -435,7 +451,7 @@
         compiler_params=params(16),
         name="norm_upper",
     )(own_upper, other_upper, gain, key_held, value_held)
-    earlier = shifted(pairs_upper, "ctx")
+    earlier = [in_vmem(x) for x in neighbours(pairs_upper, "ctx")]
     branch, causal_queries, pairs_lower, causal_out = pl.pallas_call(
         functools.partial(causal_upper_kernel, chunk=192),
         out_shape=(
@@ -464,15 +480,15 @@
     causal_out = pl.pallas_call(
         causal_lower_kernel,
         out_shape=pltpu.HBM((rows, q_width), BF16),
-        in_specs=vmem_specs(4) + hbm_specs(1),
+        in_specs=vmem_specs(5) + hbm_specs(1),
         out_specs=hbm_specs(1)[0],
         scratch_shapes=[pltpu.VMEM((half, q_width), BF16)]
         + attention_scratch(kv_heads, rows)
         + [dma((q_width // (2 * LANES),))],
-        input_output_aliases={4: 0},
+        input_output_aliases={5: 0},
         compiler_params=params(16),
         name="causal_lower",
-    )(causal_queries, pairs_lower, in_vmem(earlier), lower_causal, causal_out)
+    )(causal_queries, pairs_lower, *earlier, lower_causal, causal_out)
     return (jnp.transpose(branch), causal_out)
 
 

time: 31.1 us -> 34.1 us (1.096)
  the two profiles are of different devices: /device:TPU:0 before, /device:TPU:10 now
where the time goes in v6:
time: 34.1 us; the launch traced here: 34 us
  Pallas kernels  22 us (65%)
  starting transfers between devices  11 us (32%)
  between operations  0.99 us (3%)
    ppermute x4, starting transfers between devices, swap(): return lax.ppermute(block, axis, list(enumerate(partner)))  10.3 us
    pallas_call x1, Pallas kernels, local(): pl.pallas_call(functools.partial(causal_upper_kernel, chunk=192), out_sha...  6.56 us
    pallas_call x1, Pallas kernels, local(): pl.pallas_call(functools.partial(window_lower_kernel, chunk=chunk), out_s...  4.81 us
    pallas_call x1, Pallas kernels, local(): pl.pallas_call(functools.partial(project_upper_kernel, chunk=chunk), out_...  3.21 us
    pallas_call x1, Pallas kernels, local(): pl.pallas_call(causal_lower_kernel, out_shape=pltpu.HBM((rows, q_width),...  2.57 us
    pallas_call x1, Pallas kernels, local(): pl.pallas_call(window_upper_kernel, out_shape=(attn_s, pltpu.VMEM((rows,...  2.46 us
    pallas_call x1, Pallas kernels, local(): pl.pallas_call(functools.partial(norm_upper_kernel, chunk=192), out_shape...  1.33 us
    pallas_call x1, Pallas kernels, local(): pl.pallas_call(pack_kernel, out_shape=jax.ShapeDtypeStruct((half, 2 * kv_...  1.04 us
  transfers between devices with their start and end apart: 6, of which 0 were waited for; matrix products, arithmetic and copies ran while one was open for 0% of the time, Pallas kernels for 54%

profile of v6, /device:TPU:10, one launch (start us, length us, event | category | flops | bytes accessed | tf_op | source)
XLA Modules:
  0.0 34.0 jit_solution(12222775486793211179)
XLA Ops:
  0.6 0.0 copy-start
  0.6 1.0 %pack.1 = bf16[128,512]{1,0:T(8,128)(2,1)S(1)} custom-call(bf16[256,256]{1,0:T(8,128)(2,1)} %k_ref.3, bf16[256,256]{1,0:T(8,128)(2,1)} %v_ref.3), custom_call_target="tpu_custom_call" | custom-call | flops 10000000000 | bytes 1000000 | tf_op jit(solution)/shard_map/pack/pallas_call | solution.py:386
  1.7 0.6 %collective-permute-start = (bf16[128,512]{1,0:T(8,128)(2,1)S(1)}, bf16[128,512]{1,0:T(8,128)(2,1)S(1)}, u32[]{:S(2)}, u32[]{:S(2)}) collective-permute-start(bf16[128,512]{1,0:T(8,128)(2,1)S(1)} %pack.1), channel_id=1, source_target_pairs={{0,2},{2,0},{4,6},{6,4},{8,10},{10,8},{12,14},{14,12},{16,18},{18,... | collective-permute-start | bytes 393224 | tf_op jit(solution)/shard_map/ppermute | solution.py:52
  2.3 4.6 %collective-permute-start.1 = (bf16[128,512]{1,0:T(8,128)(2,1)S(1)}, bf16[128,512]{1,0:T(8,128)(2,1)S(1)}, u32[]{:S(2)}, u32[]{:S(2)}) collective-permute-start(bf16[128,512]{1,0:T(8,128)(2,1)S(1)} %pack.1), channel_id=1, source_target_pairs={{0,0},{2,4},{4,2},{6,8},{8,6},{10,12},{12,10},{14,16},{16,14},{18,... | collective-permute-start | bytes 393224 | tf_op jit(solution)/shard_map/ppermute | solution.py:52
  6.9 2.5 %window_upper.1 = (bf16[2048,128]{1,0:T(8,128)(2,1)S(1)}, bf16[256,2048]{1,0:T(8,128)(2,1)S(1)}, bf16[256,256]{1,0:T(8,128)(2,1)S(1)}, bf16[256,256]{1,0:T(8,128...) custom-call(s32[32]{0:T(128)} %lengths_ref.1, ...), custom_call_target="tpu_custom_call" | custom-call | tf_op jit(solution)/shard_map/window_upper/pallas_call | solution.py:400
  9.4 0.0 copy-done
  9.4 0.0 copy-start.1
  9.4 0.0 copy-start.2
  9.4 0.0 slice-start
  9.4 0.0 slice-start.1
  9.4 3.2 %project_upper.1.own_ref = bf16[2880,128]{1,0:T(8,128)(2,1)S(1)} custom-call(bf16[2880,2048]{1,0:T(8,128)(2,1)S(1)} %bitcast.2, bf16[2048,128]{1,0:T(8,128)(2,1)S(1)} %get-tuple-element.22.attn_ref), custom_call_target="tpu_custom_call" | custom-call | tf_op jit(solution)/shard_map/project_upper/pallas_call | solution.py:421
  12.6 0.1 collective-permute-start.3
  12.7 0.0 collective-permute-done.even_ref
  12.7 0.0 collective-permute-done.1.odd_ref
  12.7 0.0 slice-start.2
  12.8 4.8 %window_lower.1.own_ref = bf16[2880,128]{1,0:T(8,128)(2,1)S(1)} custom-call(bf16[256,2048]{1,0:T(8,128)(2,1)S(1)} %get-tuple-element.17.q_ref, bf16[256,256]{1,0:T(8,128)(2,1)S(1)} %get-tuple-element.18.k_ref, bf16[256,256]{1,0:T(8,128)(2,1)S(1)} %get-tuple-element.19.v_ref, bf16[128,512]{1,0:T(8,128)(2,1)S(1)} %collective-permute-done.even_ref, ...), custom_call_target="tpu_custom_call" | custom-call | tf_op jit(solution)/shard_map/window_lower/pallas_call | solution.py:431
  17.6 0.5 %collective-permute-start.2 = (bf16[2880,128]{1,0:T(8,128)(2,1)S(1)}, bf16[2880,128]{1,0:T(8,128)(2,1)S(1)}, u32[]{:S(2)}, u32[]{:S(2)}) collective-permute-start(bf16[2880,128]{1,0:T(8,128)(2,1)S(1)} %window_lower.1.own_ref), channel_id=1, source_target_pairs={{0,1},{1,0},{2,3},{3,2},{4,5},{5,4},{6,7},{7,6},{8,9},{9,8},{10,11... | collective-permute-start | bytes 2211848 | tf_op jit(solution)/shard_map/ppermute | solution.py:65
  18.1 0.0 collective-permute-done.3.other_ref
  18.1 0.0 copy-done.1
  18.1 0.0 copy-done.2
  18.1 1.3 %norm_upper.1 = (bf16[2880,128]{1,0:T(8,128)(2,1)S(1)}, bf16[128,2880]{1,0:T(8,128)(2,1)S(1)}, bf16[128,512]{1,0:T(8,128)(2,1)S(1)}) custom-call(bf16[2880,128]{1,0:T(8,128)(2,1)S(1)} %project_upper.1.own_ref, bf16[2880,128]{1,0:T(8,128)(2,1)S(1)} %collective-permute-done.3.other_ref, f32[2880]{0:T(1024)S(1)} %get-tuple-element.21.gain_ref, ...), custom_call_target="tpu_custom_call" | custom-call | tf_op jit(solution)/shard_map/norm_upper/pallas_call | solution.py:441
  19.5 0.5 %collective-permute-start.4 = (bf16[128,512]{1,0:T(8,128)(2,1)S(1)}, bf16[128,512]{1,0:T(8,128)(2,1)S(1)}, u32[]{:S(2)}, u32[]{:S(2)}) collective-permute-start(bf16[128,512]{1,0:T(8,128)(2,1)S(1)} %get-tuple-element.25.kv_up_ref), channel_id=1, source_target_pairs={{0,2},{2,0},{4,6},{6,4},{8,10},{10,8},{12,14},{14,12},{16,18},{18,... | collective-permute-start | bytes 393224 | tf_op jit(solution)/shard_map/ppermute | solution.py:52
  20.0 4.6 %collective-permute-start.5 = (bf16[128,512]{1,0:T(8,128)(2,1)S(1)}, bf16[128,512]{1,0:T(8,128)(2,1)S(1)}, u32[]{:S(2)}, u32[]{:S(2)}) collective-permute-start(bf16[128,512]{1,0:T(8,128)(2,1)S(1)} %get-tuple-element.25.kv_up_ref), channel_id=1, source_target_pairs={{0,0},{2,4},{4,2},{6,8},{8,6},{10,12},{12,10},{14,16},{16,14},{18,... | collective-permute-start | bytes 393224 | tf_op jit(solution)/shard_map/ppermute | solution.py:52
  24.6 0.0 collective-permute-done.2.other_ref
  24.6 0.0 slice-done
  24.6 0.0 slice-done.1
  24.6 0.0 slice-done.2
  24.7 6.6 %causal_upper.1 = (bf16[2880,128]{1,0:T(8,128)(2,1)}, bf16[128,2048]{1,0:T(8,128)(2,1)S(1)}, bf16[128,512]{1,0:T(8,128)(2,1)S(1)}, bf16[256,2048]{1,0:T(8,128)(2,1)}) custom-call(bf16[2880,128]{1,0:T(8,128)(2,1)S(1)} %window_lower.1.own_ref, bf16[2880,128]{1,0:T(8,128)(2,1)S(1)} %collective-permute-done.2.other_ref, f32[2880]{0:T(1024)S(1)} %get-tuple-element.21.gain_ref, ...), custom_call_target="tpu_custom_call" | custom-call | tf_op jit(solution)/shard_map/causal_upper/pallas_call | solution.py:455
  31.2 0.0 collective-permute-done.4.even_ref
  31.2 0.0 collective-permute-done.5.odd_ref
  31.2 2.6 %causal_lower.1 = bf16[256,2048]{1,0:T(8,128)(2,1)} custom-call(bf16[128,2048]{1,0:T(8,128)(2,1)S(1)} %get-tuple-element.28.q_ref, bf16[128,512]{1,0:T(8,128)(2,1)S(1)} %get-tuple-element.29.kv_ref, bf16[128,512]{1,0:T(8,128)(2,1)S(1)} %collective-permute-done.4.even_ref, ...), custom_call_target="tpu_custom_call", output_to_operand_aliasing={{}: (5, {})} | custom-call | tf_op jit(solution)/shard_map/causal_lower/pallas_call | solution.py:480
  (1 shorter events, 0.0 us)
Async XLA Ops:
  0.6 8.7 %copy-start = (bf16[2048,2880]{0,1:T(8,128)(2,1)S(1)}, bf16[2048,2880]{0,1:T(8,128)(2,1)}, u32[]{:S(2)}) copy-start(bf16[2048,2880]{0,1:T(8,128)(2,1)} %param.12) | copy-start | bytes 35389444
  1.7 11.0 %collective-permute-start = (bf16[128,512]{1,0:T(8,128)(2,1)S(1)}, bf16[128,512]{1,0:T(8,128)(2,1)S(1)}, u32[]{:S(2)}, u32[]{:S(2)}) collective-permute-start(bf16[128,512]{1,0:T(8,128)(2,1)S(1)} %pack.1), channel_id=1, source_target_pairs={{0,2},{2,0},{4,6},{6,4},{8,10},{10,8},{12,14},{14,12},{16,18},{18,... | collective-permute-start | bytes 393224 | tf_op jit(solution)/shard_map/ppermute | solution.py:52
  2.3 10.5 %collective-permute-start.1 = (bf16[128,512]{1,0:T(8,128)(2,1)S(1)}, bf16[128,512]{1,0:T(8,128)(2,1)S(1)}, u32[]{:S(2)}, u32[]{:S(2)}) collective-permute-start(bf16[128,512]{1,0:T(8,128)(2,1)S(1)} %pack.1), channel_id=1, source_target_pairs={{0,0},{2,4},{4,2},{6,8},{8,6},{10,12},{12,10},{14,16},{16,14},{18,... | collective-permute-start | bytes 393224 | tf_op jit(solution)/shard_map/ppermute | solution.py:52
  9.4 8.7 %copy-start.1 = (bf16[2880,256]{1,0:T(8,128)(2,1)S(1)}, bf16[2880,256]{1,0:T(8,128)(2,1)}, u32[]{:S(2)}) copy-start(bf16[2880,256]{1,0:T(8,128)(2,1)} %kw_ref.3) | copy-start | bytes 4423684
  9.4 8.7 %copy-start.2 = (bf16[2880,256]{1,0:T(8,128)(2,1)S(1)}, bf16[2880,256]{1,0:T(8,128)(2,1)}, u32[]{:S(2)}) copy-start(bf16[2880,256]{1,0:T(8,128)(2,1)} %vw_ref.3) | copy-start | bytes 4423684
  9.4 15.2 %slice-start = ((s8[11796480]{0:T(1024)(128)(4,1)}), s8[4194304]{0:T(1024)(128)(4,1)S(1)}, s32[]{:S(2)}) async-start(s8[11796480]{0:T(1024)(128)(4,1)} %bitcast.4), calls=%async_computation | async-start | bytes 8388608
  9.4 15.2 %slice-start.1 = ((s8[11796480]{0:T(1024)(128)(4,1)}), s8[4194304]{0:T(1024)(128)(4,1)S(1)}, s32[]{:S(2)}) async-start(s8[11796480]{0:T(1024)(128)(4,1)} %bitcast.4), calls=%async_computation.1 | async-start | bytes 8388608
  12.6 5.5 %collective-permute-start.3 = (bf16[2880,128]{1,0:T(8,128)(2,1)S(1)}, bf16[2880,128]{1,0:T(8,128)(2,1)S(1)}, u32[]{:S(2)}, u32[]{:S(2)}) collective-permute-start(bf16[2880,128]{1,0:T(8,128)(2,1)S(1)} %project_upper.1.own_ref), channel_id=1, source_target_pairs={{0,1},{1,0},{2,3},{3,2},{4,5},{5,4},{6,7},{7,6},{8,9},{9,8},{10,11... | collective-permute-start | bytes 2211848 | tf_op jit(solution)/shard_map/ppermute | solution.py:65
  12.7 11.9 %slice-start.2 = ((s8[11796480]{0:T(1024)(128)(4,1)}), s8[3407872]{0:T(1024)(128)(4,1)S(1)}, s32[]{:S(2)}) async-start(s8[11796480]{0:T(1024)(128)(4,1)} %bitcast.4), calls=%async_computation.2 | async-start | bytes 6815744
  17.6 7.0 %collective-permute-start.2 = (bf16[2880,128]{1,0:T(8,128)(2,1)S(1)}, bf16[2880,128]{1,0:T(8,128)(2,1)S(1)}, u32[]{:S(2)}, u32[]{:S(2)}) collective-permute-start(bf16[2880,128]{1,0:T(8,128)(2,1)S(1)} %window_lower.1.own_ref), channel_id=1, source_target_pairs={{0,1},{1,0},{2,3},{3,2},{4,5},{5,4},{6,7},{7,6},{8,9},{9,8},{10,11... | collective-permute-start | bytes 2211848 | tf_op jit(solution)/shard_map/ppermute | solution.py:65
  19.5 11.8 %collective-permute-start.4 = (bf16[128,512]{1,0:T(8,128)(2,1)S(1)}, bf16[128,512]{1,0:T(8,128)(2,1)S(1)}, u32[]{:S(2)}, u32[]{:S(2)}) collective-permute-start(bf16[128,512]{1,0:T(8,128)(2,1)S(1)} %get-tuple-element.25.kv_up_ref), channel_id=1, source_target_pairs={{0,2},{2,0},{4,6},{6,4},{8,10},{10,8},{12,14},{14,12},{16,18},{18,... | collective-permute-start | bytes 393224 | tf_op jit(solution)/shard_map/ppermute | solution.py:52
  20.0 11.3 %collective-permute-start.5 = (bf16[128,512]{1,0:T(8,128)(2,1)S(1)}, bf16[128,512]{1,0:T(8,128)(2,1)S(1)}, u32[]{:S(2)}, u32[]{:S(2)}) collective-permute-start(bf16[128,512]{1,0:T(8,128)(2,1)S(1)} %get-tuple-element.25.kv_up_ref), channel_id=1, source_target_pairs={{0,0},{2,4},{4,2},{6,8},{8,6},{10,12},{12,10},{14,16},{16,14},{18,... | collective-permute-start | bytes 393224 | tf_op jit(solution)/shard_map/ppermute | solution.py:52

commit v7 on v5

--- a/solution.py
+++ b/solution.py
@@ -229,22 +229,45 @@
         out_ref[part, :] = dot(weight_ref[part, :], attn_ref[...], ((1,), (0,))).astype(BF16)
 
 
-def project_upper_kernel(weight_ref, attn_ref, out_ref, *, chunk):
+def project_upper_kernel(
+    weight_ref, attn_ref, q_ref, k_ref, v_ref, bias_ref, out_ref, first_ref, keys_s, values_s, *, chunk
+):
+    half = attn_ref.shape[1]
     project(weight_ref, attn_ref, out_ref, chunk)
 
+    @pl.when(lax.axis_index("ctx") == 0)
+    def _():
+        stage_keys(k_ref[:half], keys_s)
+        stage_values(v_ref[:half], values_s)
+
+        def queries_of(unit):
+            return q_ref[:half, unit.lane : unit.lane + 2 * LANES]
+
+        window_heads(queries_of, keys_s, values_s, bias_ref.at[pl.ds(half, half)], first_ref, q_ref.shape[1])
+
 
 def window_lower_kernel(
-    q_ref, k_ref, v_ref, halo_ref, weight_ref, bias_ref, out_ref, attn_s, keys_s, values_s, *, chunk
+    q_ref, k_ref, v_ref, halo_ref, weight_ref, bias_ref, first_ref,
+    out_ref, attn_s, keys_s, values_s, *, chunk
 ):
     half = halo_ref.shape[0]
     kv_width = k_ref.shape[1]
-    stage_keys(jnp.concatenate([halo_ref[:, :kv_width], k_ref[:half]], axis=0), keys_s)
-    stage_values(jnp.concatenate([halo_ref[:, kv_width:], v_ref[:half]], axis=0), values_s)
-
-    def queries_of(unit):
-        return q_ref[:half, unit.lane : unit.lane + 2 * LANES]
-
-    window_heads(queries_of, keys_s, values_s, bias_ref, attn_s, q_ref.shape[1])
+    ctx = lax.axis_index("ctx")
+
+    @pl.when(ctx == 0)
+    def _():
+        attn_s[...] = first_ref[...]
+
+    @pl.when(ctx != 0)
+    def _():
+        stage_keys(jnp.concatenate([halo_ref[:, :kv_width], k_ref[:half]], axis=0), keys_s)
+        stage_values(jnp.concatenate([halo_ref[:, kv_width:], v_ref[:half]], axis=0), values_s)
+
+        def queries_of(unit):
+            return q_ref[:half, unit.lane : unit.lane + 2 * LANES]
+
+        window_heads(queries_of, keys_s, values_s, bias_ref, attn_s, q_ref.shape[1])
+
     project(weight_ref, attn_s, out_ref, chunk)
 
 
@@ -281,7 +304,7 @@
 
 def causal_upper_kernel(
     own_ref, other_ref, gain_ref, kw_ref, vw_ref, qw_ref, kept_ref, normed_ref, kv_up_ref, bias_ref,
-    branch_ref, q_ref, kv_ref, out_ref,
+    lower_bias_ref, branch_ref, q_ref, kv_ref, out_ref,
     branch_s, out_s, upper_q_s, normed_s, sum_s, keys_s, values_s, sems, *, chunk
 ):
     half = own_ref.shape[1]
@@ -312,30 +335,49 @@
     branch_out.wait()
     upper_out.wait()
 
+    @pl.when(lax.axis_index("ctx") == 0)
+    def _():
+        stage_keys(kv_ref[:, :kv_width], keys_s)
+        stage_values(kv_ref[:, kv_width:], values_s)
+
+        def lower_queries_of(unit):
+            return q_ref[:, unit.lane : unit.lane + 2 * LANES]
+
+        causal_heads(
+            lower_queries_of, keys_s, values_s, lower_bias_ref.at[pl.ds(half, half)], out_s, q_width,
+            lambda unit: None,
+        )
+        lower_out = pltpu.make_async_copy(out_s, out_ref.at[pl.ds(0, half)], sems.at[2])
+        lower_out.start()
+        lower_out.wait()
+
 
 def causal_lower_kernel(
     q_ref, kv_ref, halo_ref, bias_ref, given_ref, out_ref, out_s, keys_s, values_s, sems
 ):
     half, q_width = q_ref.shape
     kv_width = kv_ref.shape[1] // 2
-    stage_keys(jnp.concatenate([halo_ref[:, :kv_width], kv_ref[:, :kv_width]], axis=0), keys_s)
-    stage_values(jnp.concatenate([halo_ref[:, kv_width:], kv_ref[:, kv_width:]], axis=0), values_s)
-    copies = []
-
-    def queries_of(unit):
-        return q_ref[:, unit.lane : unit.lane + 2 * LANES]
-
-    def ready(unit):
-        columns = pl.ds(unit.lane, 2 * LANES)
-        copy = pltpu.make_async_copy(
-            out_s.at[:, columns], out_ref.at[pl.ds(0, half), columns], sems.at[len(copies)]
-        )
-        copy.start()
-        copies.append(copy)
-
-    causal_heads(queries_of, keys_s, values_s, bias_ref, out_s, q_width, ready)
-    for copy in copies:
-        copy.wait()
+
+    @pl.when(lax.axis_index("ctx") != 0)
+    def _():
+        stage_keys(jnp.concatenate([halo_ref[:, :kv_width], kv_ref[:, :kv_width]], axis=0), keys_s)
+        stage_values(jnp.concatenate([halo_ref[:, kv_width:], kv_ref[:, kv_width:]], axis=0), values_s)
+        copies = []
+
+        def queries_of(unit):
+            return q_ref[:, unit.lane : unit.lane + 2 * LANES]
+
+        def ready(unit):
+            columns = pl.ds(unit.lane, 2 * LANES)
+            copy = pltpu.make_async_copy(
+                out_s.at[:, columns], out_ref.at[pl.ds(0, half), columns], sems.at[len(copies)]
+            )
+            copy.start()
+            copies.append(copy)
+
+        causal_heads(queries_of, keys_s, values_s, bias_ref, out_s, q_width, ready)
+        for copy in copies:
+            copy.wait()
 
 
 def attention_scratch(kv_heads, keys):
@@ -402,25 +444,26 @@
         name="window_upper",
     )(lengths, queries, keys, values, in_hbm(norm_gain))
     held = in_vmem(jnp.transpose(out_weight))
-    own_upper = pl.pallas_call(
+    own_upper, attn_first = pl.pallas_call(
         functools.partial(project_upper_kernel, chunk=chunk),
-        out_shape=pltpu.VMEM((width, half), BF16),
-        in_specs=vmem_specs(2),
-        out_specs=vmem_specs(1)[0],
+        out_shape=(pltpu.VMEM((width, half), BF16), attn_s),
+        in_specs=vmem_specs(6),
+        out_specs=tuple(vmem_specs(2)),
+        scratch_shapes=attention_scratch(kv_heads, half),
         compiler_params=params(8),
         name="project_upper",
-    )(held, attn_upper)
+    )(held, attn_upper, q_held, k_held, v_held, window_bias)
     key_held, value_held, query_held = [in_vmem(x) for x in (key_weight, value_weight, query_weight)]
     other_upper = swapped(own_upper, "head")
     own_lower = pl.pallas_call(
         functools.partial(window_lower_kernel, chunk=chunk),
         out_shape=pltpu.VMEM((width, half), BF16),
-        in_specs=vmem_specs(6),
+        in_specs=vmem_specs(7),
         out_specs=vmem_specs(1)[0],
         scratch_shapes=[attn_s] + attention_scratch(kv_heads, rows),
         compiler_params=params(16),
         name="window_lower",
-    )(q_held, k_held, v_held, in_vmem(halo), held, window_bias)
+    )(q_held, k_held, v_held, in_vmem(halo), held, window_bias, attn_first)
     other_lower = swapped(own_lower, "head")
     branch_upper, normed_upper, pairs_upper = pl.pallas_call(
         functools.partial(norm_upper_kernel, chunk=192),
@@ -444,7 +487,7 @@
             pltpu.VMEM((half, 2 * kv_width), BF16),
             pltpu.HBM((rows, q_width), BF16),
         ),
-        in_specs=vmem_specs(10),
+        in_specs=vmem_specs(11),
         out_specs=(hbm_specs(1)[0], *vmem_specs(2), hbm_specs(1)[0]),
         scratch_shapes=[
             pltpu.VMEM((width, half), BF16),
@@ -454,12 +497,12 @@
             pltpu.VMEM((width, half), F32),
         ]
         + attention_scratch(kv_heads, half)
-        + [dma((2,))],
+        + [dma((3,))],
         compiler_params=params(16),
         name="causal_upper",
     )(
         own_lower, other_lower, gain, key_held, value_held, query_held,
-        branch_upper, normed_upper, pairs_upper, upper_causal,
+        branch_upper, normed_upper, pairs_upper, upper_causal, lower_causal,
     )
     causal_out = pl.pallas_call(
         causal_lower_kernel,

time: 31.1 us -> 29 us (0.932)
  waiting for transfers between devices: 3.55 us -> 0.39 us
  starting transfers between devices: 4.38 us -> 6.17 us
  Pallas kernels: 22 us -> 21.4 us
    ppermute x2, waiting for transfers between devices: 3.54 us -> 0.39 us  [shifted(): return lax.ppermute(block, axis, [(i, (i + 1) % size) for i in range(size)])]
    pallas_call x1, Pallas kernels: 2.58 us -> 0.09 us  [local(): pl.pallas_call(causal_lower_kernel, out_shape=pltpu.HBM((rows, q_width),...]
    pallas_call x1, Pallas kernels: 6.56 us -> 8.71 us  [local(): pl.pallas_call(functools.partial(causal_upper_kernel, chunk=192), out_sha...]
    ppermute x2, starting transfers between devices: 4.24 us -> 5.92 us  [shifted(): return lax.ppermute(block, axis, [(i, (i + 1) % size) for i in range(size)])]
    pallas_call x1, Pallas kernels: 4.84 us -> 3.24 us  [local(): pl.pallas_call(functools.partial(window_lower_kernel, chunk=chunk), out_s...]
    pallas_call x1, Pallas kernels: 3.21 us -> 4.5 us  [local(): pl.pallas_call(functools.partial(project_upper_kernel, chunk=chunk), out_...]
  transfers between devices with their start and end apart: 4 -> 4, of which waited for: 2 -> 1; matrix products, arithmetic and copies ran while one was open for 0% -> 0% of each run, Pallas kernels for 60% -> 70%
where the time goes in v7:
time: 29 us; the launch traced here: 28.9 us
  Pallas kernels  21.4 us (74%)
  starting transfers between devices  6.17 us (21%)
  between operations  0.92 us (3%)
  waiting for transfers between devices  0.39 us (1%)
    pallas_call x1, Pallas kernels, local(): pl.pallas_call(functools.partial(causal_upper_kernel, chunk=192), out_sha...  8.71 us
    ppermute x2, starting transfers between devices, shifted(): return lax.ppermute(block, axis, [(i, (i + 1) % size) for i in range(size)])  5.92 us
    pallas_call x1, Pallas kernels, local(): pl.pallas_call(functools.partial(project_upper_kernel, chunk=chunk), out_...  4.5 us
    pallas_call x1, Pallas kernels, local(): pl.pallas_call(functools.partial(window_lower_kernel, chunk=chunk), out_s...  3.24 us
    pallas_call x1, Pallas kernels, local(): pl.pallas_call(window_upper_kernel, out_shape=(attn_s, pltpu.VMEM((rows,...  2.45 us
    pallas_call x1, Pallas kernels, local(): pl.pallas_call(functools.partial(norm_upper_kernel, chunk=192), out_shape...  1.32 us
    pallas_call x1, Pallas kernels, local(): pl.pallas_call(pack_kernel, out_shape=jax.ShapeDtypeStruct((half, 2 * kv_...  1.04 us
  transfers between devices with their start and end apart: 4, of which 1 were waited for; matrix products, arithmetic and copies ran while one was open for 0% of the time, Pallas kernels for 70%

profile of v7, /device:TPU:0, one launch (start us, length us, event | category | flops | bytes accessed | tf_op | source)
XLA Modules:
  0.0 28.9 jit_solution(14478433559275927072)
XLA Ops:
  0.6 0.0 copy-start
  0.6 1.0 %pack.1 = bf16[128,512]{1,0:T(8,128)(2,1)S(1)} custom-call(bf16[256,256]{1,0:T(8,128)(2,1)} %k_ref.3, bf16[256,256]{1,0:T(8,128)(2,1)} %v_ref.3), custom_call_target="tpu_custom_call" | custom-call | flops 10000000000 | bytes 1000000 | tf_op jit(solution)/shard_map/pack/pallas_call | solution.py:412
  1.7 3.0 %collective-permute-start = (bf16[128,512]{1,0:T(8,128)(2,1)S(1)}, bf16[128,512]{1,0:T(8,128)(2,1)S(1)}, u32[]{:S(2)}, u32[]{:S(2)}) collective-permute-start(bf16[128,512]{1,0:T(8,128)(2,1)S(1)} %pack.1), channel_id=1, source_target_pairs={{0,2},{2,4},{4,6},{6,8},{8,10},{10,12},{12,14},{14,16},{16,18},{18... | collective-permute-start | bytes 393224 | tf_op jit(solution)/shard_map/ppermute | solution.py:47
  4.7 2.5 %window_upper.1 = (bf16[2048,128]{1,0:T(8,128)(2,1)S(1)}, bf16[256,2048]{1,0:T(8,128)(2,1)S(1)}, bf16[256,256]{1,0:T(8,128)(2,1)S(1)}, bf16[256,256]{1,0:T(8,128...) custom-call(s32[32]{0:T(128)} %lengths_ref.1, ...), custom_call_target="tpu_custom_call" | custom-call | tf_op jit(solution)/shard_map/window_upper/pallas_call | solution.py:426
  7.1 0.0 copy-done
  7.1 0.0 copy-start.1
  7.2 0.0 copy-start.2
  7.2 0.0 slice-start
  7.2 0.0 slice-start.1
  7.2 4.5 %project_upper.1 = (bf16[2880,128]{1,0:T(8,128)(2,1)S(1)}, bf16[2048,128]{1,0:T(8,128)(2,1)S(1)}) custom-call(bf16[2880,2048]{1,0:T(8,128)(2,1)S(1)} %bitcast.2, bf16[2048,128]{1,0:T(8,128)(2,1)S(1)} %get-tuple-element.23.attn_ref, bf16[256,2048]{1,0:T(8,128)(2,1)S(1)} %get-tuple-element.19.q_ref, bf16[256,256]{1,0:T(8,128)(2,1)S(1)} %get-tuple-element.20.k_ref, ...), custom_call_target="tpu_custom_call" | custom-call | tf_op jit(solution)/shard_map/project_upper/pallas_call | solution.py:447
  11.7 0.1 collective-permute-start.2
  11.8 0.4 %collective-permute-done.halo_ref = bf16[128,512]{1,0:T(8,128)(2,1)S(1)} collective-permute-done((bf16[128,512]{1,0:T(8,128)(2,1)S(1)}, bf16[128,512]{1,0:T(8,128)(2,1)S(1)}, u32[]{:S(2)}, u32[]{:S(2)}) %collective-permute-start) | collective-permute-done | bytes 131104 | tf_op jit(solution)/shard_map/ppermute | solution.py:47
  12.2 0.0 slice-start.2
  12.2 3.2 %window_lower.1.own_ref = bf16[2880,128]{1,0:T(8,128)(2,1)S(1)} custom-call(bf16[256,2048]{1,0:T(8,128)(2,1)S(1)} %get-tuple-element.19.q_ref, bf16[256,256]{1,0:T(8,128)(2,1)S(1)} %get-tuple-element.20.k_ref, bf16[256,256]{1,0:T(8,128)(2,1)S(1)} %get-tuple-element.21.v_ref, bf16[128,512]{1,0:T(8,128)(2,1)S(1)} %collective-permute-done.halo_ref, ...), custom_call_target="tpu_custom_call" | custom-call | tf_op jit(solution)/shard_map/window_lower/pallas_call | solution.py:458
  15.4 0.2 collective-permute-start.1
  15.6 0.0 collective-permute-done.2.other_ref
  15.6 0.0 copy-done.1
  15.6 0.0 copy-done.2
  15.6 1.3 %norm_upper.1 = (bf16[2880,128]{1,0:T(8,128)(2,1)S(1)}, bf16[128,2880]{1,0:T(8,128)(2,1)S(1)}, bf16[128,512]{1,0:T(8,128)(2,1)S(1)}) custom-call(bf16[2880,128]{1,0:T(8,128)(2,1)S(1)} %get-tuple-element.26.own_ref, bf16[2880,128]{1,0:T(8,128)(2,1)S(1)} %collective-permute-done.2.other_ref, f32[2880]{0:T(1024)S(1)} %get-tuple-element.25.gain_ref, ...), custom_call_target="tpu_custom_call" | custom-call | tf_op jit(solution)/shard_map/norm_upper/pallas_call | solution.py:468
  16.9 2.9 %collective-permute-start.3 = (bf16[128,512]{1,0:T(8,128)(2,1)S(1)}, bf16[128,512]{1,0:T(8,128)(2,1)S(1)}, u32[]{:S(2)}, u32[]{:S(2)}) collective-permute-start(bf16[128,512]{1,0:T(8,128)(2,1)S(1)} %get-tuple-element.29.kv_up_ref), channel_id=1, source_target_pairs={{0,2},{2,4},{4,6},{6,8},{8,10},{10,12},{12,14},{14,16},{16,18},{18... | collective-permute-start | bytes 393224 | tf_op jit(solution)/shard_map/ppermute | solution.py:47
  19.9 0.0 collective-permute-done.1.other_ref
  19.9 0.0 slice-done
  19.9 0.0 slice-done.1
  19.9 0.0 slice-done.2
  19.9 8.7 %causal_upper.1 = (bf16[2880,128]{1,0:T(8,128)(2,1)}, bf16[128,2048]{1,0:T(8,128)(2,1)S(1)}, bf16[128,512]{1,0:T(8,128)(2,1)S(1)}, bf16[256,2048]{1,0:T(8,128)(2,1)}) custom-call(bf16[2880,128]{1,0:T(8,128)(2,1)S(1)} %window_lower.1.own_ref, bf16[2880,128]{1,0:T(8,128)(2,1)S(1)} %collective-permute-done.1.other_ref, f32[2880]{0:T(1024)S(1)} %get-tuple-element.25.gain_ref, ...), custom_call_target="tpu_custom_call" | custom-call | tf_op jit(solution)/shard_map/causal_upper/pallas_call | solution.py:482
  28.6 0.0 collective-permute-done.3.halo_ref
  28.6 0.1 causal_lower.1
  (1 shorter events, 0.0 us)
Async XLA Ops:
  0.6 6.5 %copy-start = (bf16[2048,2880]{0,1:T(8,128)(2,1)S(1)}, bf16[2048,2880]{0,1:T(8,128)(2,1)}, u32[]{:S(2)}) copy-start(bf16[2048,2880]{0,1:T(8,128)(2,1)} %param.12) | copy-start | bytes 35389444
  1.7 10.5 %collective-permute-start = (bf16[128,512]{1,0:T(8,128)(2,1)S(1)}, bf16[128,512]{1,0:T(8,128)(2,1)S(1)}, u32[]{:S(2)}, u32[]{:S(2)}) collective-permute-start(bf16[128,512]{1,0:T(8,128)(2,1)S(1)} %pack.1), channel_id=1, source_target_pairs={{0,2},{2,4},{4,6},{6,8},{8,10},{10,12},{12,14},{14,16},{16,18},{18... | collective-permute-start | bytes 393224 | tf_op jit(solution)/shard_map/ppermute | solution.py:47
  7.1 8.5 %copy-start.1 = (bf16[2880,256]{1,0:T(8,128)(2,1)S(1)}, bf16[2880,256]{1,0:T(8,128)(2,1)}, u32[]{:S(2)}) copy-start(bf16[2880,256]{1,0:T(8,128)(2,1)} %kw_ref.3) | copy-start | bytes 4423684
  7.2 8.4 %copy-start.2 = (bf16[2880,256]{1,0:T(8,128)(2,1)S(1)}, bf16[2880,256]{1,0:T(8,128)(2,1)}, u32[]{:S(2)}) copy-start(bf16[2880,256]{1,0:T(8,128)(2,1)} %vw_ref.3) | copy-start | bytes 4423684
  7.2 12.7 %slice-start = ((s8[11796480]{0:T(1024)(128)(4,1)}), s8[4194304]{0:T(1024)(128)(4,1)S(1)}, s32[]{:S(2)}) async-start(s8[11796480]{0:T(1024)(128)(4,1)} %bitcast.4), calls=%async_computation | async-start | bytes 8388608
  7.2 12.7 %slice-start.1 = ((s8[11796480]{0:T(1024)(128)(4,1)}), s8[4194304]{0:T(1024)(128)(4,1)S(1)}, s32[]{:S(2)}) async-start(s8[11796480]{0:T(1024)(128)(4,1)} %bitcast.4), calls=%async_computation.1 | async-start | bytes 8388608
  11.7 3.9 %collective-permute-start.2 = (bf16[2880,128]{1,0:T(8,128)(2,1)S(1)}, bf16[2880,128]{1,0:T(8,128)(2,1)S(1)}, u32[]{:S(2)}, u32[]{:S(2)}) collective-permute-start(bf16[2880,128]{1,0:T(8,128)(2,1)S(1)} %get-tuple-element.26.own_ref), channel_id=1, source_target_pairs={{0,1},{1,0},{2,3},{3,2},{4,5},{5,4},{6,7},{7,6},{8,9},{9,8},{10,11... | collective-permute-start | bytes 2211848 | tf_op jit(solution)/shard_map/ppermute | solution.py:52
  12.2 7.7 %slice-start.2 = ((s8[11796480]{0:T(1024)(128)(4,1)}), s8[3407872]{0:T(1024)(128)(4,1)S(1)}, s32[]{:S(2)}) async-start(s8[11796480]{0:T(1024)(128)(4,1)} %bitcast.4), calls=%async_computation.2 | async-start | bytes 6815744
  15.4 4.4 %collective-permute-start.1 = (bf16[2880,128]{1,0:T(8,128)(2,1)S(1)}, bf16[2880,128]{1,0:T(8,128)(2,1)S(1)}, u32[]{:S(2)}, u32[]{:S(2)}) collective-permute-start(bf16[2880,128]{1,0:T(8,128)(2,1)S(1)} %window_lower.1.own_ref), channel_id=1, source_target_pairs={{0,1},{1,0},{2,3},{3,2},{4,5},{5,4},{6,7},{7,6},{8,9},{9,8},{10,11... | collective-permute-start | bytes 2211848 | tf_op jit(solution)/shard_map/ppermute | solution.py:52
  16.9 11.7 %collective-permute-start.3 = (bf16[128,512]{1,0:T(8,128)(2,1)S(1)}, bf16[128,512]{1,0:T(8,128)(2,1)S(1)}, u32[]{:S(2)}, u32[]{:S(2)}) collective-permute-start(bf16[128,512]{1,0:T(8,128)(2,1)S(1)} %get-tuple-element.29.kv_up_ref), channel_id=1, source_target_pairs={{0,2},{2,4},{4,6},{6,8},{8,10},{10,12},{12,14},{14,16},{16,18},{18... | collective-permute-start | bytes 393224 | tf_op jit(solution)/shard_map/ppermute | solution.py:47

commit v8 on v7

--- a/solution.py
+++ b/solution.py
@@ -114,7 +114,7 @@
     return dot(keys, stacked, ((1,), (1,)))
 
 
-def unit_attend(scores, unit, values_ref, bias):
+def unit_weighted(scores, unit, values_ref, bias):
     count = bias.shape[0]
     wide = jnp.concatenate([bias, bias], axis=1)
     patterns = []
@@ -122,22 +122,26 @@
         masked = scores[side * count : (side + 1) * count] + wide
         highest = jnp.max(masked, axis=0, keepdims=True)
         patterns.append(jnp.exp((masked - highest).astype(BF16)))
-    weighted = dot(values_ref[unit.g], jnp.concatenate(patterns, axis=1), ((1,), (0,)))
-    return weighted[:HD] * (1.0 / weighted[HD : HD + 1])
+    return dot(values_ref[unit.g], jnp.concatenate(patterns, axis=1), ((1,), (0,)))
 
 
 def pipelined(units, queries_of, keys_ref, values_ref, bias, write):
     count = len(units)
-    queries = queries_of(units[0])
-    scores = unit_scores(queries, units[0], keys_ref)
-    queries = queries_of(units[1])
+    scores = [unit_scores(queries_of(unit), unit, keys_ref) for unit in units[:2]]
+
+    def finish(unit, weighted):
+        write(unit, weighted[:HD] * (1.0 / weighted[HD : HD + 1]))
+
+    before = None
     for i, unit in enumerate(units):
-        now = scores
-        if i + 1 < count:
-            scores = unit_scores(queries, units[i + 1], keys_ref)
+        now = scores.pop(0)
         if i + 2 < count:
-            queries = queries_of(units[i + 2])
-        write(unit, unit_attend(now, unit, values_ref, bias))
+            scores.append(unit_scores(queries_of(units[i + 2]), units[i + 2], keys_ref))
+        weighted = unit_weighted(now, unit, values_ref, bias)
+        if before is not None:
+            finish(*before)
+        before = (unit, weighted)
+    finish(*before)
 
 
 def window_heads(queries_of, keys_ref, values_ref, bias_ref, out_ref, q_width):
@@ -305,7 +309,7 @@
 def causal_upper_kernel(
     own_ref, other_ref, gain_ref, kw_ref, vw_ref, qw_ref, kept_ref, normed_ref, kv_up_ref, bias_ref,
     lower_bias_ref, branch_ref, q_ref, kv_ref, out_ref,
-    branch_s, out_s, upper_q_s, normed_s, sum_s, keys_s, values_s, sems, *, chunk
+    branch_s, out_s, upper_q_s, normed_s, sum_s, keys_s, values_s, sems, unit_sems, *, chunk
 ):
     half = own_ref.shape[1]
     kv_width = kw_ref.shape[1]
@@ -339,17 +343,27 @@
     def _():
         stage_keys(kv_ref[:, :kv_width], keys_s)
         stage_values(kv_ref[:, kv_width:], values_s)
-
-        def lower_queries_of(unit):
-            return q_ref[:, unit.lane : unit.lane + 2 * LANES]
-
-        causal_heads(
-            lower_queries_of, keys_s, values_s, lower_bias_ref.at[pl.ds(half, half)], out_s, q_width,
-            lambda unit: None,
+        attend_lower(q_ref, keys_s, values_s, lower_bias_ref.at[pl.ds(half, half)], out_s, out_ref, unit_sems)
+
+
+def attend_lower(q_ref, keys_s, values_s, bias_ref, out_s, out_ref, sems):
+    half, q_width = q_ref.shape
+    copies = []
+
+    def queries_of(unit):
+        return q_ref[:, unit.lane : unit.lane + 2 * LANES]
+
+    def ready(unit):
+        columns = pl.ds(unit.lane, 2 * LANES)
+        copy = pltpu.make_async_copy(
+            out_s.at[:, columns], out_ref.at[pl.ds(0, half), columns], sems.at[len(copies)]
         )
-        lower_out = pltpu.make_async_copy(out_s, out_ref.at[pl.ds(0, half)], sems.at[2])
-        lower_out.start()
-        lower_out.wait()
+        copy.start()
+        copies.append(copy)
+
+    causal_heads(queries_of, keys_s, values_s, bias_ref, out_s, q_width, ready)
+    for copy in copies:
+        copy.wait()
 
 
 def causal_lower_kernel(
@@ -362,22 +376,7 @@
     def _():
         stage_keys(jnp.concatenate([halo_ref[:, :kv_width], kv_ref[:, :kv_width]], axis=0), keys_s)
         stage_values(jnp.concatenate([halo_ref[:, kv_width:], kv_ref[:, kv_width:]], axis=0), values_s)
-        copies = []
-
-        def queries_of(unit):
-            return q_ref[:, unit.lane : unit.lane + 2 * LANES]
-
-        def ready(unit):
-            columns = pl.ds(unit.lane, 2 * LANES)
-            copy = pltpu.make_async_copy(
-                out_s.at[:, columns], out_ref.at[pl.ds(0, half), columns], sems.at[len(copies)]
-            )
-            copy.start()
-            copies.append(copy)
-
-        causal_heads(queries_of, keys_s, values_s, bias_ref, out_s, q_width, ready)
-        for copy in copies:
-            copy.wait()
+        attend_lower(q_ref, keys_s, values_s, bias_ref, out_s, out_ref, sems)
 
 
 def attention_scratch(kv_heads, keys):
@@ -403,7 +402,7 @@
     kv_heads = kv_width // HD
     width = out_weight.shape[1]
     half = rows // 2
-    chunk = 576
+    chunk = width // 2
     dma = pltpu.SemaphoreType.DMA
     lengths, queries, keys, values = [
         in_hbm(x) for x in (doc_lengths, window_queries, window_keys, window_values)
@@ -497,7 +496,7 @@
             pltpu.VMEM((width, half), F32),
         ]
         + attention_scratch(kv_heads, half)
-        + [dma((3,))],
+        + [dma((2,)), dma((q_width // (2 * LANES),))],
         compiler_params=params(16),
         name="causal_upper",
     )(

time: 29 us -> 28.1 us (0.969)
  Pallas kernels: 21.4 us -> 20.5 us
  starting transfers between devices: 6.17 us -> 5.72 us
  waiting for transfers between devices: 0.39 us -> 0.79 us
    pallas_call x1, Pallas kernels: 8.71 us -> 8.23 us  [local(): pl.pallas_call(functools.partial(causal_upper_kernel, chunk=192), out_sha...]
    ppermute x2, waiting for transfers between devices: 0.39 us -> 0.78 us  [shifted(): return lax.ppermute(block, axis, [(i, (i + 1) % size) for i in range(size)])]
    ppermute x2, starting transfers between devices: 5.92 us -> 5.58 us  [shifted(): return lax.ppermute(block, axis, [(i, (i + 1) % size) for i in range(size)])]
  transfers between devices with their start and end apart: 4 -> 4, of which waited for: 1 -> 1; matrix products, arithmetic and copies ran while one was open for 0% -> 0% of each run, Pallas kernels for 70% -> 69%
where the time goes in v8:
time: 28.1 us; the launch traced here: 28 us
  Pallas kernels  20.5 us (73%)
  starting transfers between devices  5.72 us (20%)
  between operations  0.95 us (3%)
  waiting for transfers between devices  0.79 us (3%)
    pallas_call x1, Pallas kernels, local(): pl.pallas_call(functools.partial(causal_upper_kernel, chunk=192), out_sha...  8.23 us
    ppermute x2, starting transfers between devices, shifted(): return lax.ppermute(block, axis, [(i, (i + 1) % size) for i in range(size)])  5.58 us
    pallas_call x1, Pallas kernels, local(): pl.pallas_call(functools.partial(project_upper_kernel, chunk=chunk), out_...  4.31 us
    pallas_call x1, Pallas kernels, local(): pl.pallas_call(functools.partial(window_lower_kernel, chunk=chunk), out_s...  3.25 us
    pallas_call x1, Pallas kernels, local(): pl.pallas_call(window_upper_kernel, out_shape=(attn_s, pltpu.VMEM((rows,...  2.25 us
    pallas_call x1, Pallas kernels, local(): pl.pallas_call(functools.partial(norm_upper_kernel, chunk=192), out_shape...  1.32 us
    pallas_call x1, Pallas kernels, local(): pl.pallas_call(pack_kernel, out_shape=jax.ShapeDtypeStruct((half, 2 * kv_...  1.04 us
    ppermute x2, waiting for transfers between devices, shifted(): return lax.ppermute(block, axis, [(i, (i + 1) % size) for i in range(size)])  0.78 us
  transfers between devices with their start and end apart: 4, of which 1 were waited for; matrix products, arithmetic and copies ran while one was open for 0% of the time, Pallas kernels for 69%

profile of v8, /device:TPU:0, one launch (start us, length us, event | category | flops | bytes accessed | tf_op | source)
XLA Modules:
  0.0 28.0 jit_solution(13866344707453351338)
XLA Ops:
  0.6 0.0 copy-start
  0.6 1.0 %pack.1 = bf16[128,512]{1,0:T(8,128)(2,1)S(1)} custom-call(bf16[256,256]{1,0:T(8,128)(2,1)} %k_ref.3, bf16[256,256]{1,0:T(8,128)(2,1)} %v_ref.3), custom_call_target="tpu_custom_call" | custom-call | flops 10000000000 | bytes 1000000 | tf_op jit(solution)/shard_map/pack/pallas_call | solution.py:411
  1.7 3.0 %collective-permute-start = (bf16[128,512]{1,0:T(8,128)(2,1)S(1)}, bf16[128,512]{1,0:T(8,128)(2,1)S(1)}, u32[]{:S(2)}, u32[]{:S(2)}) collective-permute-start(bf16[128,512]{1,0:T(8,128)(2,1)S(1)} %pack.1), channel_id=1, source_target_pairs={{0,2},{2,4},{4,6},{6,8},{8,10},{10,12},{12,14},{14,16},{16,18},{18... | collective-permute-start | bytes 393224 | tf_op jit(solution)/shard_map/ppermute | solution.py:47
  4.7 2.2 %window_upper.1 = (bf16[2048,128]{1,0:T(8,128)(2,1)S(1)}, bf16[256,2048]{1,0:T(8,128)(2,1)S(1)}, bf16[256,256]{1,0:T(8,128)(2,1)S(1)}, bf16[256,256]{1,0:T(8,128...) custom-call(s32[32]{0:T(128)} %lengths_ref.1, ...), custom_call_target="tpu_custom_call" | custom-call | tf_op jit(solution)/shard_map/window_upper/pallas_call | solution.py:425
  6.9 0.0 copy-done
  6.9 0.0 copy-start.1
  7.0 0.0 copy-start.2
  7.0 0.0 slice-start
  7.0 0.0 slice-start.1
  7.0 4.3 %project_upper.1 = (bf16[2880,128]{1,0:T(8,128)(2,1)S(1)}, bf16[2048,128]{1,0:T(8,128)(2,1)S(1)}) custom-call(bf16[2880,2048]{1,0:T(8,128)(2,1)S(1)} %bitcast.2, bf16[2048,128]{1,0:T(8,128)(2,1)S(1)} %get-tuple-element.23.attn_ref, bf16[256,2048]{1,0:T(8,128)(2,1)S(1)} %get-tuple-element.19.q_ref, bf16[256,256]{1,0:T(8,128)(2,1)S(1)} %get-tuple-element.20.k_ref, ...), custom_call_target="tpu_custom_call" | custom-call | tf_op jit(solution)/shard_map/project_upper/pallas_call | solution.py:446
  11.3 0.1 collective-permute-start.2
  11.4 0.8 %collective-permute-done.halo_ref = bf16[128,512]{1,0:T(8,128)(2,1)S(1)} collective-permute-done((bf16[128,512]{1,0:T(8,128)(2,1)S(1)}, bf16[128,512]{1,0:T(8,128)(2,1)S(1)}, u32[]{:S(2)}, u32[]{:S(2)}) %collective-permute-start) | collective-permute-done | bytes 131104 | tf_op jit(solution)/shard_map/ppermute | solution.py:47
  12.2 0.0 slice-start.2
  12.2 3.3 %window_lower.1.own_ref = bf16[2880,128]{1,0:T(8,128)(2,1)S(1)} custom-call(bf16[256,2048]{1,0:T(8,128)(2,1)S(1)} %get-tuple-element.19.q_ref, bf16[256,256]{1,0:T(8,128)(2,1)S(1)} %get-tuple-element.20.k_ref, bf16[256,256]{1,0:T(8,128)(2,1)S(1)} %get-tuple-element.21.v_ref, bf16[128,512]{1,0:T(8,128)(2,1)S(1)} %collective-permute-done.halo_ref, ...), custom_call_target="tpu_custom_call" | custom-call | tf_op jit(solution)/shard_map/window_lower/pallas_call | solution.py:457
  15.4 0.1 collective-permute-start.1
  15.5 0.0 collective-permute-done.2.other_ref
  15.5 0.0 copy-done.1
  15.5 0.0 copy-done.2
  15.5 1.3 %norm_upper.1 = (bf16[2880,128]{1,0:T(8,128)(2,1)S(1)}, bf16[128,2880]{1,0:T(8,128)(2,1)S(1)}, bf16[128,512]{1,0:T(8,128)(2,1)S(1)}) custom-call(bf16[2880,128]{1,0:T(8,128)(2,1)S(1)} %get-tuple-element.26.own_ref, bf16[2880,128]{1,0:T(8,128)(2,1)S(1)} %collective-permute-done.2.other_ref, f32[2880]{0:T(1024)S(1)} %get-tuple-element.25.gain_ref, ...), custom_call_target="tpu_custom_call" | custom-call | tf_op jit(solution)/shard_map/norm_upper/pallas_call | solution.py:467
  16.9 2.6 %collective-permute-start.3 = (bf16[128,512]{1,0:T(8,128)(2,1)S(1)}, bf16[128,512]{1,0:T(8,128)(2,1)S(1)}, u32[]{:S(2)}, u32[]{:S(2)}) collective-permute-start(bf16[128,512]{1,0:T(8,128)(2,1)S(1)} %get-tuple-element.29.kv_up_ref), channel_id=1, source_target_pairs={{0,2},{2,4},{4,6},{6,8},{8,10},{10,12},{12,14},{14,16},{16,18},{18... | collective-permute-start | bytes 393224 | tf_op jit(solution)/shard_map/ppermute | solution.py:47
  19.5 0.0 collective-permute-done.1.other_ref
  19.5 0.0 slice-done
  19.5 0.0 slice-done.1
  19.5 0.0 slice-done.2
  19.5 8.2 %causal_upper.1 = (bf16[2880,128]{1,0:T(8,128)(2,1)}, bf16[128,2048]{1,0:T(8,128)(2,1)S(1)}, bf16[128,512]{1,0:T(8,128)(2,1)S(1)}, bf16[256,2048]{1,0:T(8,128)(2,1)}) custom-call(bf16[2880,128]{1,0:T(8,128)(2,1)S(1)} %window_lower.1.own_ref, bf16[2880,128]{1,0:T(8,128)(2,1)S(1)} %collective-permute-done.1.other_ref, f32[2880]{0:T(1024)S(1)} %get-tuple-element.25.gain_ref, ...), custom_call_target="tpu_custom_call" | custom-call | tf_op jit(solution)/shard_map/causal_upper/pallas_call | solution.py:481
  27.7 0.0 collective-permute-done.3.halo_ref
  27.7 0.1 causal_lower.1
  (1 shorter events, 0.0 us)
Async XLA Ops:
  0.6 6.3 %copy-start = (bf16[2048,2880]{0,1:T(8,128)(2,1)S(1)}, bf16[2048,2880]{0,1:T(8,128)(2,1)}, u32[]{:S(2)}) copy-start(bf16[2048,2880]{0,1:T(8,128)(2,1)} %param.12) | copy-start | bytes 35389444
  1.7 10.5 %collective-permute-start = (bf16[128,512]{1,0:T(8,128)(2,1)S(1)}, bf16[128,512]{1,0:T(8,128)(2,1)S(1)}, u32[]{:S(2)}, u32[]{:S(2)}) collective-permute-start(bf16[128,512]{1,0:T(8,128)(2,1)S(1)} %pack.1), channel_id=1, source_target_pairs={{0,2},{2,4},{4,6},{6,8},{8,10},{10,12},{12,14},{14,16},{16,18},{18... | collective-permute-start | bytes 393224 | tf_op jit(solution)/shard_map/ppermute | solution.py:47
  6.9 8.6 %copy-start.1 = (bf16[2880,256]{1,0:T(8,128)(2,1)S(1)}, bf16[2880,256]{1,0:T(8,128)(2,1)}, u32[]{:S(2)}) copy-start(bf16[2880,256]{1,0:T(8,128)(2,1)} %kw_ref.3) | copy-start | bytes 4423684
  7.0 8.6 %copy-start.2 = (bf16[2880,256]{1,0:T(8,128)(2,1)S(1)}, bf16[2880,256]{1,0:T(8,128)(2,1)}, u32[]{:S(2)}) copy-start(bf16[2880,256]{1,0:T(8,128)(2,1)} %vw_ref.3) | copy-start | bytes 4423684
  7.0 12.5 %slice-start = ((s8[11796480]{0:T(1024)(128)(4,1)}), s8[4194304]{0:T(1024)(128)(4,1)S(1)}, s32[]{:S(2)}) async-start(s8[11796480]{0:T(1024)(128)(4,1)} %bitcast.4), calls=%async_computation | async-start | bytes 8388608
  7.0 12.5 %slice-start.1 = ((s8[11796480]{0:T(1024)(128)(4,1)}), s8[4194304]{0:T(1024)(128)(4,1)S(1)}, s32[]{:S(2)}) async-start(s8[11796480]{0:T(1024)(128)(4,1)} %bitcast.4), calls=%async_computation.1 | async-start | bytes 8388608
  11.3 4.2 %collective-permute-start.2 = (bf16[2880,128]{1,0:T(8,128)(2,1)S(1)}, bf16[2880,128]{1,0:T(8,128)(2,1)S(1)}, u32[]{:S(2)}, u32[]{:S(2)}) collective-permute-start(bf16[2880,128]{1,0:T(8,128)(2,1)S(1)} %get-tuple-element.26.own_ref), channel_id=1, source_target_pairs={{0,1},{1,0},{2,3},{3,2},{4,5},{5,4},{6,7},{7,6},{8,9},{9,8},{10,11... | collective-permute-start | bytes 2211848 | tf_op jit(solution)/shard_map/ppermute | solution.py:52
  12.2 7.3 %slice-start.2 = ((s8[11796480]{0:T(1024)(128)(4,1)}), s8[3407872]{0:T(1024)(128)(4,1)S(1)}, s32[]{:S(2)}) async-start(s8[11796480]{0:T(1024)(128)(4,1)} %bitcast.4), calls=%async_computation.2 | async-start | bytes 6815744
  15.4 4.0 %collective-permute-start.1 = (bf16[2880,128]{1,0:T(8,128)(2,1)S(1)}, bf16[2880,128]{1,0:T(8,128)(2,1)S(1)}, u32[]{:S(2)}, u32[]{:S(2)}) collective-permute-start(bf16[2880,128]{1,0:T(8,128)(2,1)S(1)} %window_lower.1.own_ref), channel_id=1, source_target_pairs={{0,1},{1,0},{2,3},{3,2},{4,5},{5,4},{6,7},{7,6},{8,9},{9,8},{10,11... | collective-permute-start | bytes 2211848 | tf_op jit(solution)/shard_map/ppermute | solution.py:52
  16.9 10.9 %collective-permute-start.3 = (bf16[128,512]{1,0:T(8,128)(2,1)S(1)}, bf16[128,512]{1,0:T(8,128)(2,1)S(1)}, u32[]{:S(2)}, u32[]{:S(2)}) collective-permute-start(bf16[128,512]{1,0:T(8,128)(2,1)S(1)} %get-tuple-element.29.kv_up_ref), channel_id=1, source_target_pairs={{0,2},{2,4},{4,6},{6,8},{8,10},{10,12},{12,14},{14,16},{16,18},{18... | collective-permute-start | bytes 393224 | tf_op jit(solution)/shard_map/ppermute | solution.py:47

commit v9 on v8

--- a/solution.py
+++ b/solution.py
@@ -189,24 +189,19 @@
 
 def window_upper_kernel(
     lengths_ref, q_ref, k_ref, v_ref, gain_ref,
-    attn_ref, q_held, k_held, v_held, window_bias, upper_causal, lower_causal, gain_held,
-    lengths_s, keys_s, values_s, bias_s, sems
+    attn_ref, window_bias, upper_causal, lower_causal, gain_held,
+    lengths_s, q_s, k_s, v_s, keys_s, values_s, bias_s, sems
 ):
     half = attn_ref.shape[1]
-    upper, lower = pl.ds(half, half), pl.ds(0, half)
+    upper = pl.ds(half, half)
     first = [
         pltpu.make_async_copy(lengths_ref, lengths_s, sems.at[0]),
-        pltpu.make_async_copy(k_ref.at[upper], k_held.at[upper], sems.at[1]),
-        pltpu.make_async_copy(v_ref.at[upper], v_held.at[upper], sems.at[2]),
-        pltpu.make_async_copy(q_ref.at[upper], q_held.at[upper], sems.at[3]),
+        pltpu.make_async_copy(k_ref.at[upper], k_s, sems.at[1]),
+        pltpu.make_async_copy(v_ref.at[upper], v_s, sems.at[2]),
+        pltpu.make_async_copy(q_ref.at[upper], q_s, sems.at[3]),
     ]
-    last = [
-        pltpu.make_async_copy(k_ref.at[lower], k_held.at[lower], sems.at[4]),
-        pltpu.make_async_copy(v_ref.at[lower], v_held.at[lower], sems.at[5]),
-        pltpu.make_async_copy(q_ref.at[lower], q_held.at[lower], sems.at[6]),
-        pltpu.make_async_copy(gain_ref, gain_held, sems.at[7]),
-    ]
-    for copy in first + last:
+    gain_in = pltpu.make_async_copy(gain_ref, gain_held, sems.at[4])
+    for copy in first + [gain_in]:
         copy.start()
     first[0].wait()
     bias_s[...] = upper_bias(lengths_s, half, WIN)
@@ -214,17 +209,16 @@
     upper_causal[...] = upper_bias(lengths_s, half, None)
     lower_causal[...] = lower_bias(lengths_s, half, None)
     first[1].wait()
-    stage_keys(k_held[half:], keys_s)
+    stage_keys(k_s[...], keys_s)
     first[2].wait()
-    stage_values(v_held[half:], values_s)
+    stage_values(v_s[...], values_s)
     first[3].wait()
 
     def queries_of(unit):
-        return q_held[half:, unit.lane : unit.lane + 2 * LANES]
-
-    window_heads(queries_of, keys_s, values_s, bias_s, attn_ref, q_held.shape[1])
-    for copy in last:
-        copy.wait()
+        return q_s[:, unit.lane : unit.lane + 2 * LANES]
+
+    window_heads(queries_of, keys_s, values_s, bias_s, attn_ref, q_s.shape[1])
+    gain_in.wait()
 
 
 def project(weight_ref, attn_ref, out_ref, chunk):
@@ -234,27 +228,37 @@
 
 
 def project_upper_kernel(
-    weight_ref, attn_ref, q_ref, k_ref, v_ref, bias_ref, out_ref, first_ref, keys_s, values_s, *, chunk
+    weight_ref, attn_ref, bias_ref, q_ref, k_ref, v_ref,
+    out_ref, first_ref, q_held, k_held, v_held, keys_s, values_s, sems, *, chunk
 ):
     half = attn_ref.shape[1]
+    lower = pl.ds(0, half)
+    copies = [
+        pltpu.make_async_copy(k_ref.at[lower], k_held, sems.at[0]),
+        pltpu.make_async_copy(v_ref.at[lower], v_held, sems.at[1]),
+        pltpu.make_async_copy(q_ref.at[lower], q_held, sems.at[2]),
+    ]
+    for copy in copies:
+        copy.start()
     project(weight_ref, attn_ref, out_ref, chunk)
+    for copy in copies:
+        copy.wait()
 
     @pl.when(lax.axis_index("ctx") == 0)
     def _():
-        stage_keys(k_ref[:half], keys_s)
-        stage_values(v_ref[:half], values_s)
+        stage_keys(k_held[...], keys_s)
+        stage_values(v_held[...], values_s)
 
         def queries_of(unit):
-            return q_ref[:half, unit.lane : unit.lane + 2 * LANES]
-
-        window_heads(queries_of, keys_s, values_s, bias_ref.at[pl.ds(half, half)], first_ref, q_ref.shape[1])
+            return q_held[:, unit.lane : unit.lane + 2 * LANES]
+
+        window_heads(queries_of, keys_s, values_s, bias_ref.at[pl.ds(half, half)], first_ref, q_held.shape[1])
 
 
 def window_lower_kernel(
     q_ref, k_ref, v_ref, halo_ref, weight_ref, bias_ref, first_ref,
     out_ref, attn_s, keys_s, values_s, *, chunk
 ):
-    half = halo_ref.shape[0]
     kv_width = k_ref.shape[1]
     ctx = lax.axis_index("ctx")
 
@@ -264,11 +268,11 @@
 
     @pl.when(ctx != 0)
     def _():
-        stage_keys(jnp.concatenate([halo_ref[:, :kv_width], k_ref[:half]], axis=0), keys_s)
-        stage_values(jnp.concatenate([halo_ref[:, kv_width:], v_ref[:half]], axis=0), values_s)
+        stage_keys(jnp.concatenate([halo_ref[:, :kv_width], k_ref[...]], axis=0), keys_s)
+        stage_values(jnp.concatenate([halo_ref[:, kv_width:], v_ref[...]], axis=0), values_s)
 
         def queries_of(unit):
-            return q_ref[:half, unit.lane : unit.lane + 2 * LANES]
+            return q_ref[:, unit.lane : unit.lane + 2 * LANES]
 
         window_heads(queries_of, keys_s, values_s, bias_ref, attn_s, q_ref.shape[1])
 
@@ -309,7 +313,7 @@
 def causal_upper_kernel(
     own_ref, other_ref, gain_ref, kw_ref, vw_ref, qw_ref, kept_ref, normed_ref, kv_up_ref, bias_ref,
     lower_bias_ref, branch_ref, q_ref, kv_ref, out_ref,
-    branch_s, out_s, upper_q_s, normed_s, sum_s, keys_s, values_s, sems, unit_sems, *, chunk
+    branch_s, out_s, normed_s, sum_s, keys_s, values_s, sems, unit_sems, *, chunk
 ):
     half = own_ref.shape[1]
     kv_width = kw_ref.shape[1]
@@ -321,15 +325,17 @@
     stage_keys(kv_up_ref[:, :kv_width], keys_s)
     stage_values(kv_up_ref[:, kv_width:], values_s)
 
-    piece = q_width // 2
-    for first in range(0, q_width, piece):
-        columns = slice(first, first + piece)
-        queries = dot(normed_s[...], qw_ref[:, columns], ((1,), (0,))).astype(BF16)
-        q_ref[:, columns] = queries[:half]
-        upper_q_s[:, columns] = queries[half:]
+    piece = 4 * LANES
+    pieces = {}
 
     def queries_of(unit):
-        return upper_q_s[:, unit.lane : unit.lane + 2 * LANES]
+        first = unit.lane // piece * piece
+        if first not in pieces:
+            columns = slice(first, first + piece)
+            queries = dot(normed_s[...], qw_ref[:, columns], ((1,), (0,))).astype(BF16)
+            q_ref[:, columns] = queries[:half]
+            pieces[first] = queries[half:]
+        return pieces[first][:, unit.lane - first : unit.lane - first + 2 * LANES]
 
     causal_heads(queries_of, keys_s, values_s, bias_ref, out_s, q_width, lambda unit: None)
     upper_out = pltpu.make_async_copy(out_s, out_ref.at[pl.ds(half, half)], sems.at[1])
@@ -420,38 +426,39 @@
     )(keys, values)
     halo = shifted(packed, "ctx")
     attn_s = pltpu.VMEM((q_width, half), BF16)
-    (
-        attn_upper, q_held, k_held, v_held, window_bias, upper_causal, lower_causal, gain
-    ) = pl.pallas_call(
+    inputs_s = [
+        pltpu.VMEM((half, q_width), BF16),
+        pltpu.VMEM((half, kv_width), BF16),
+        pltpu.VMEM((half, kv_width), BF16),
+    ]
+    attn_upper, window_bias, upper_causal, lower_causal, gain = pl.pallas_call(
         window_upper_kernel,
         out_shape=(
             attn_s,
-            pltpu.VMEM((rows, q_width), BF16),
-            pltpu.VMEM((rows, kv_width), BF16),
-            pltpu.VMEM((rows, kv_width), BF16),
             pltpu.VMEM((rows, half), F32),
             pltpu.VMEM((half, half), F32),
             pltpu.VMEM((rows, half), F32),
             pltpu.VMEM((width,), F32),
         ),
         in_specs=hbm_specs(5),
-        out_specs=tuple(vmem_specs(8)),
+        out_specs=tuple(vmem_specs(5)),
         scratch_shapes=[pltpu.SMEM(doc_lengths.shape, jnp.int32)]
+        + inputs_s
         + attention_scratch(kv_heads, half)
-        + [pltpu.VMEM((half, half), F32), dma((8,))],
+        + [pltpu.VMEM((half, half), F32), dma((5,))],
         compiler_params=params(8),
         name="window_upper",
     )(lengths, queries, keys, values, in_hbm(norm_gain))
     held = in_vmem(jnp.transpose(out_weight))
-    own_upper, attn_first = pl.pallas_call(
+    own_upper, attn_first, q_held, k_held, v_held = pl.pallas_call(
         functools.partial(project_upper_kernel, chunk=chunk),
-        out_shape=(pltpu.VMEM((width, half), BF16), attn_s),
-        in_specs=vmem_specs(6),
-        out_specs=tuple(vmem_specs(2)),
-        scratch_shapes=attention_scratch(kv_heads, half),
+        out_shape=(pltpu.VMEM((width, half), BF16), attn_s, *inputs_s),
+        in_specs=vmem_specs(3) + hbm_specs(3),
+        out_specs=tuple(vmem_specs(5)),
+        scratch_shapes=attention_scratch(kv_heads, half) + [dma((3,))],
         compiler_params=params(8),
         name="project_upper",
-    )(held, attn_upper, q_held, k_held, v_held, window_bias)
+    )(held, attn_upper, window_bias, queries, keys, values)
     key_held, value_held, query_held = [in_vmem(x) for x in (key_weight, value_weight, query_weight)]
     other_upper = swapped(own_upper, "head")
     own_lower = pl.pallas_call(
@@ -491,7 +498,6 @@
         scratch_shapes=[
             pltpu.VMEM((width, half), BF16),
             pltpu.VMEM((half, q_width), BF16),
-            pltpu.VMEM((half, q_width), BF16),
             pltpu.VMEM((rows, width), BF16),
             pltpu.VMEM((width, half), F32),
         ]

time: 28.1 us -> 28.4 us (1.011)
  Pallas kernels: 20.5 us -> 20.8 us
  transfers between devices with their start and end apart: 4 -> 4, of which waited for: 1 -> 1; matrix products, arithmetic and copies ran while one was open for 0% -> 0% of each run, Pallas kernels for 69% -> 70%
where the time goes in v9:
time: 28.4 us; the launch traced here: 28.2 us
  Pallas kernels  20.8 us (73%)
  starting transfers between devices  5.72 us (20%)
  between operations  0.95 us (3%)
  waiting for transfers between devices  0.78 us (3%)
    pallas_call x1, Pallas kernels, local(): pl.pallas_call(functools.partial(causal_upper_kernel, chunk=192), out_sha...  8.47 us
    ppermute x2, starting transfers between devices, shifted(): return lax.ppermute(block, axis, [(i, (i + 1) % size) for i in range(size)])  5.58 us
    pallas_call x1, Pallas kernels, local(): pl.pallas_call(functools.partial(project_upper_kernel, chunk=chunk), out_...  4.36 us
    pallas_call x1, Pallas kernels, local(): pl.pallas_call(functools.partial(window_lower_kernel, chunk=chunk), out_s...  3.25 us
    pallas_call x1, Pallas kernels, local(): pl.pallas_call(window_upper_kernel, out_shape=(attn_s, pltpu.VMEM((rows,...  2.21 us
    pallas_call x1, Pallas kernels, local(): pl.pallas_call(functools.partial(norm_upper_kernel, chunk=192), out_shape...  1.34 us
    pallas_call x1, Pallas kernels, local(): pl.pallas_call(pack_kernel, out_shape=jax.ShapeDtypeStruct((half, 2 * kv_...  1.04 us
    ppermute x2, waiting for transfers between devices, shifted(): return lax.ppermute(block, axis, [(i, (i + 1) % size) for i in range(size)])  0.77 us
  transfers between devices with their start and end apart: 4, of which 1 were waited for; matrix products, arithmetic and copies ran while one was open for 0% of the time, Pallas kernels for 70%

profile of v9, /device:TPU:0, one launch (start us, length us, event | category | flops | bytes accessed | tf_op | source)
XLA Modules:
  0.0 28.2 jit_solution(7721986131014146550)
XLA Ops:
  0.6 0.0 copy-start
  0.6 1.0 %pack.1 = bf16[128,512]{1,0:T(8,128)(2,1)S(1)} custom-call(bf16[256,256]{1,0:T(8,128)(2,1)} %k_ref.5, bf16[256,256]{1,0:T(8,128)(2,1)} %v_ref.5), custom_call_target="tpu_custom_call" | custom-call | flops 10000000000 | bytes 1000000 | tf_op jit(solution)/shard_map/pack/pallas_call | solution.py:417
  1.7 3.0 %collective-permute-start = (bf16[128,512]{1,0:T(8,128)(2,1)S(1)}, bf16[128,512]{1,0:T(8,128)(2,1)S(1)}, u32[]{:S(2)}, u32[]{:S(2)}) collective-permute-start(bf16[128,512]{1,0:T(8,128)(2,1)S(1)} %pack.1), channel_id=1, source_target_pairs={{0,2},{2,4},{4,6},{6,8},{8,10},{10,12},{12,14},{14,16},{16,18},{18... | collective-permute-start | bytes 393224 | tf_op jit(solution)/shard_map/ppermute | solution.py:47
  4.7 2.2 %window_upper.1 = (bf16[2048,128]{1,0:T(8,128)(2,1)S(1)}, f32[256,128]{1,0:T(8,128)S(1)}, f32[128,128]{1,0:T(8,128)S(1)}, f32[256,128]{1,0:T(8,128)S(1)}, f32[2880]{0:T(1024)S(1)}) custom-call(s32[32]{0:T(128)} %lengths_ref.1, bf16[256,2048]{1,0:T(8,128)(2,1)} %q_ref.3, bf16[256,256]{1,0:T(8,128)(2,1)} %k_ref.5, bf16[256,256]{1,0:T(8,128)(2,1)} %v_ref.5, ...), custom_call_target="tpu_custom_call" | custom-call | tf_op jit(solution)/shard_map/window_upper/pallas_call | solution.py:434
  6.9 0.0 copy-done
  6.9 0.0 copy-start.1
  6.9 0.0 copy-start.2
  6.9 0.0 slice-start
  6.9 0.0 slice-start.1
  7.0 4.4 %project_upper.1 = (bf16[2880,128]{1,0:T(8,128)(2,1)S(1)}, bf16[2048,128]{1,0:T(8,128)(2,1)S(1)}, bf16[128,2048]{1,0:T(8,128)(2,1)S(1)}, bf16[128,256]{1,0:T(8,128)(2,1)S(1)}, bf16[128,256]{1,0:T(8,128)(2,1)S(1)}) custom-call(bf16[2880,2048]{1,0:T(8,128)(2,1)S(1)} %bitcast.2, bf16[2048,128]{1,0:T(8,128)(2,1)S(1)} %get-tuple-element.19.attn_ref, ...), custom_call_target="tpu_custom_call" | custom-call | tf_op jit(solution)/shard_map/project_upper/pallas_call | solution.py:453
  11.3 0.1 collective-permute-start.2
  11.4 0.8 %collective-permute-done.halo_ref = bf16[128,512]{1,0:T(8,128)(2,1)S(1)} collective-permute-done((bf16[128,512]{1,0:T(8,128)(2,1)S(1)}, bf16[128,512]{1,0:T(8,128)(2,1)S(1)}, u32[]{:S(2)}, u32[]{:S(2)}) %collective-permute-start) | collective-permute-done | bytes 131104 | tf_op jit(solution)/shard_map/ppermute | solution.py:47
  12.2 0.0 slice-start.2
  12.2 3.3 %window_lower.1.own_ref = bf16[2880,128]{1,0:T(8,128)(2,1)S(1)} custom-call(bf16[128,2048]{1,0:T(8,128)(2,1)S(1)} %get-tuple-element.21.q_ref, bf16[128,256]{1,0:T(8,128)(2,1)S(1)} %get-tuple-element.22.k_ref, bf16[128,256]{1,0:T(8,128)(2,1)S(1)} %get-tuple-element.23.v_ref, bf16[128,512]{1,0:T(8,128)(2,1)S(1)} %collective-permute-done.halo_ref, ...), custom_call_target="tpu_custom_call" | custom-call | tf_op jit(solution)/shard_map/window_lower/pallas_call | solution.py:464
  15.4 0.1 collective-permute-start.1
  15.5 0.0 collective-permute-done.2.other_ref
  15.5 0.0 copy-done.1
  15.5 0.0 copy-done.2
  15.5 1.3 %norm_upper.1 = (bf16[2880,128]{1,0:T(8,128)(2,1)S(1)}, bf16[128,2880]{1,0:T(8,128)(2,1)S(1)}, bf16[128,512]{1,0:T(8,128)(2,1)S(1)}) custom-call(bf16[2880,128]{1,0:T(8,128)(2,1)S(1)} %get-tuple-element.26.own_ref, bf16[2880,128]{1,0:T(8,128)(2,1)S(1)} %collective-permute-done.2.other_ref, f32[2880]{0:T(1024)S(1)} %get-tuple-element.25.gain_ref, ...), custom_call_target="tpu_custom_call" | custom-call | tf_op jit(solution)/shard_map/norm_upper/pallas_call | solution.py:474
  16.9 2.6 %collective-permute-start.3 = (bf16[128,512]{1,0:T(8,128)(2,1)S(1)}, bf16[128,512]{1,0:T(8,128)(2,1)S(1)}, u32[]{:S(2)}, u32[]{:S(2)}) collective-permute-start(bf16[128,512]{1,0:T(8,128)(2,1)S(1)} %get-tuple-element.29.kv_up_ref), channel_id=1, source_target_pairs={{0,2},{2,4},{4,6},{6,8},{8,10},{10,12},{12,14},{14,16},{16,18},{18... | collective-permute-start | bytes 393224 | tf_op jit(solution)/shard_map/ppermute | solution.py:47
  19.5 0.0 collective-permute-done.1.other_ref
  19.5 0.0 slice-done
  19.5 0.0 slice-done.1
  19.5 0.0 slice-done.2
  19.5 8.5 %causal_upper.1 = (bf16[2880,128]{1,0:T(8,128)(2,1)}, bf16[128,2048]{1,0:T(8,128)(2,1)S(1)}, bf16[128,512]{1,0:T(8,128)(2,1)S(1)}, bf16[256,2048]{1,0:T(8,128)(2,1)}) custom-call(bf16[2880,128]{1,0:T(8,128)(2,1)S(1)} %window_lower.1.own_ref, bf16[2880,128]{1,0:T(8,128)(2,1)S(1)} %collective-permute-done.1.other_ref, f32[2880]{0:T(1024)S(1)} %get-tuple-element.25.gain_ref, ...), custom_call_target="tpu_custom_call" | custom-call | tf_op jit(solution)/shard_map/causal_upper/pallas_call | solution.py:488
  28.0 0.0 collective-permute-done.3.halo_ref
  28.0 0.1 causal_lower.1
  (1 shorter events, 0.0 us)
Async XLA Ops:
  0.6 6.3 %copy-start = (bf16[2048,2880]{0,1:T(8,128)(2,1)S(1)}, bf16[2048,2880]{0,1:T(8,128)(2,1)}, u32[]{:S(2)}) copy-start(bf16[2048,2880]{0,1:T(8,128)(2,1)} %param.12) | copy-start | bytes 35389444
  1.7 10.5 %collective-permute-start = (bf16[128,512]{1,0:T(8,128)(2,1)S(1)}, bf16[128,512]{1,0:T(8,128)(2,1)S(1)}, u32[]{:S(2)}, u32[]{:S(2)}) collective-permute-start(bf16[128,512]{1,0:T(8,128)(2,1)S(1)} %pack.1), channel_id=1, source_target_pairs={{0,2},{2,4},{4,6},{6,8},{8,10},{10,12},{12,14},{14,16},{16,18},{18... | collective-permute-start | bytes 393224 | tf_op jit(solution)/shard_map/ppermute | solution.py:47
  6.9 8.6 %copy-start.1 = (bf16[2880,256]{1,0:T(8,128)(2,1)S(1)}, bf16[2880,256]{1,0:T(8,128)(2,1)}, u32[]{:S(2)}) copy-start(bf16[2880,256]{1,0:T(8,128)(2,1)} %kw_ref.3) | copy-start | bytes 4423684
  6.9 8.6 %copy-start.2 = (bf16[2880,256]{1,0:T(8,128)(2,1)S(1)}, bf16[2880,256]{1,0:T(8,128)(2,1)}, u32[]{:S(2)}) copy-start(bf16[2880,256]{1,0:T(8,128)(2,1)} %vw_ref.3) | copy-start | bytes 4423684
  6.9 12.5 %slice-start = ((s8[11796480]{0:T(1024)(128)(4,1)}), s8[4194304]{0:T(1024)(128)(4,1)S(1)}, s32[]{:S(2)}) async-start(s8[11796480]{0:T(1024)(128)(4,1)} %bitcast.4), calls=%async_computation | async-start | bytes 8388608
  6.9 12.5 %slice-start.1 = ((s8[11796480]{0:T(1024)(128)(4,1)}), s8[4194304]{0:T(1024)(128)(4,1)S(1)}, s32[]{:S(2)}) async-start(s8[11796480]{0:T(1024)(128)(4,1)} %bitcast.4), calls=%async_computation.1 | async-start | bytes 8388608
  11.3 4.2 %collective-permute-start.2 = (bf16[2880,128]{1,0:T(8,128)(2,1)S(1)}, bf16[2880,128]{1,0:T(8,128)(2,1)S(1)}, u32[]{:S(2)}, u32[]{:S(2)}) collective-permute-start(bf16[2880,128]{1,0:T(8,128)(2,1)S(1)} %get-tuple-element.26.own_ref), channel_id=1, source_target_pairs={{0,1},{1,0},{2,3},{3,2},{4,5},{5,4},{6,7},{7,6},{8,9},{9,8},{10,11... | collective-permute-start | bytes 2211848 | tf_op jit(solution)/shard_map/ppermute | solution.py:52
  12.2 7.3 %slice-start.2 = ((s8[11796480]{0:T(1024)(128)(4,1)}), s8[3407872]{0:T(1024)(128)(4,1)S(1)}, s32[]{:S(2)}) async-start(s8[11796480]{0:T(1024)(128)(4,1)} %bitcast.4), calls=%async_computation.2 | async-start | bytes 6815744
  15.4 4.0 %collective-permute-start.1 = (bf16[2880,128]{1,0:T(8,128)(2,1)S(1)}, bf16[2880,128]{1,0:T(8,128)(2,1)S(1)}, u32[]{:S(2)}, u32[]{:S(2)}) collective-permute-start(bf16[2880,128]{1,0:T(8,128)(2,1)S(1)} %window_lower.1.own_ref), channel_id=1, source_target_pairs={{0,1},{1,0},{2,3},{3,2},{4,5},{5,4},{6,7},{7,6},{8,9},{9,8},{10,11... | collective-permute-start | bytes 2211848 | tf_op jit(solution)/shard_map/ppermute | solution.py:52
  16.9 11.1 %collective-permute-start.3 = (bf16[128,512]{1,0:T(8,128)(2,1)S(1)}, bf16[128,512]{1,0:T(8,128)(2,1)S(1)}, u32[]{:S(2)}, u32[]{:S(2)}) collective-permute-start(bf16[128,512]{1,0:T(8,128)(2,1)S(1)} %get-tuple-element.29.kv_up_ref), channel_id=1, source_target_pairs={{0,2},{2,4},{4,6},{6,8},{8,10},{10,12},{12,14},{14,16},{16,18},{18... | collective-permute-start | bytes 393224 | tf_op jit(solution)/shard_map/ppermute | solution.py:47

commit v10 on v8

--- a/solution.py
+++ b/solution.py
@@ -188,11 +188,13 @@
 
 
 def window_upper_kernel(
-    lengths_ref, q_ref, k_ref, v_ref, gain_ref,
-    attn_ref, q_held, k_held, v_held, window_bias, upper_causal, lower_causal, gain_held,
-    lengths_s, keys_s, values_s, bias_s, sems
+    lengths_ref, q_ref, k_ref, v_ref, weight_ref, gain_ref,
+    out_ref, held_ref, first_ref, q_held, k_held, v_held, window_bias, upper_causal, lower_causal, gain_held,
+    lengths_s, attn_s, keys_s, values_s, bias_s, sems, weight_sems
 ):
-    half = attn_ref.shape[1]
+    half = out_ref.shape[1]
+    count = weight_sems.shape[0]
+    chunk = held_ref.shape[0] // count
     upper, lower = pl.ds(half, half), pl.ds(0, half)
     first = [
         pltpu.make_async_copy(lengths_ref, lengths_s, sems.at[0]),
@@ -206,7 +208,14 @@
         pltpu.make_async_copy(q_ref.at[lower], q_held.at[lower], sems.at[6]),
         pltpu.make_async_copy(gain_ref, gain_held, sems.at[7]),
     ]
-    for copy in first + last:
+    weights = [
+        pltpu.make_async_copy(
+            weight_ref.at[pl.ds(c * chunk, chunk)], held_ref.at[pl.ds(c * chunk, chunk)], weight_sems.at[c]
+        )
+        for c in range(count)
+    ]
+    early = count // 2
+    for copy in first + weights[:2]:
         copy.start()
     first[0].wait()
     bias_s[...] = upper_bias(lengths_s, half, WIN)
@@ -218,13 +227,36 @@
     first[2].wait()
     stage_values(v_held[half:], values_s)
     first[3].wait()
+    for copy in weights[2:early] + last:
+        copy.start()
 
     def queries_of(unit):
         return q_held[half:, unit.lane : unit.lane + 2 * LANES]
 
-    window_heads(queries_of, keys_s, values_s, bias_s, attn_ref, q_held.shape[1])
-    for copy in last:
+    window_heads(queries_of, keys_s, values_s, bias_s, attn_s, q_held.shape[1])
+    for copy in weights[early : early + 3]:
+        copy.start()
+    for copy in weights[:early] + last:
         copy.wait()
+    for c in range(count):
+        if early <= c + 2 < count:
+            weights[c + 2].wait()
+            if c + 5 < count:
+                weights[c + 5].start()
+        part = slice(c * chunk, (c + 1) * chunk)
+        out_ref[part, :] = dot(held_ref[part, :], attn_s[...], ((1,), (0,))).astype(BF16)
+
+    @pl.when(lax.axis_index("ctx") == 0)
+    def _():
+        stage_keys(k_held[:half], keys_s)
+        stage_values(v_held[:half], values_s)
+
+        def lower_queries_of(unit):
+            return q_held[:half, unit.lane : unit.lane + 2 * LANES]
+
+        window_heads(
+            lower_queries_of, keys_s, values_s, window_bias.at[pl.ds(half, half)], first_ref, q_held.shape[1]
+        )
 
 
 def project(weight_ref, attn_ref, out_ref, chunk):
@@ -233,27 +265,17 @@
         out_ref[part, :] = dot(weight_ref[part, :], attn_ref[...], ((1,), (0,))).astype(BF16)
 
 
-def project_upper_kernel(
-    weight_ref, attn_ref, q_ref, k_ref, v_ref, bias_ref, out_ref, first_ref, keys_s, values_s, *, chunk
+def window_lower_kernel(
+    q_ref, k_ref, v_ref, halo_ref, weight_ref, bias_ref, first_ref, kw_ref, vw_ref, qw_ref,
+    out_ref, key_held, value_held, query_held, attn_s, keys_s, values_s, sems, *, chunk
 ):
-    half = attn_ref.shape[1]
-    project(weight_ref, attn_ref, out_ref, chunk)
-
-    @pl.when(lax.axis_index("ctx") == 0)
-    def _():
-        stage_keys(k_ref[:half], keys_s)
-        stage_values(v_ref[:half], values_s)
-
-        def queries_of(unit):
-            return q_ref[:half, unit.lane : unit.lane + 2 * LANES]
-
-        window_heads(queries_of, keys_s, values_s, bias_ref.at[pl.ds(half, half)], first_ref, q_ref.shape[1])
-
-
-def window_lower_kernel(
-    q_ref, k_ref, v_ref, halo_ref, weight_ref, bias_ref, first_ref,
-    out_ref, attn_s, keys_s, values_s, *, chunk
-):
+    copies = [
+        pltpu.make_async_copy(kw_ref, key_held, sems.at[0]),
+        pltpu.make_async_copy(vw_ref, value_held, sems.at[1]),
+        pltpu.make_async_copy(qw_ref.at[:, pl.ds(0, query_held.shape[1])], query_held, sems.at[2]),
+    ]
+    for copy in copies:
+        copy.start()
     half = halo_ref.shape[0]
     kv_width = k_ref.shape[1]
     ctx = lax.axis_index("ctx")
@@ -273,6 +295,8 @@
         window_heads(queries_of, keys_s, values_s, bias_ref, attn_s, q_ref.shape[1])
 
     project(weight_ref, attn_s, out_ref, chunk)
+    for copy in copies:
+        copy.wait()
 
 
 def add_and_norm(own_ref, other_ref, gain_ref, branch_ref, normed_ref, first_row, sum_s, keep_ref, chunk):
@@ -307,13 +331,16 @@
 
 
 def causal_upper_kernel(
-    own_ref, other_ref, gain_ref, kw_ref, vw_ref, qw_ref, kept_ref, normed_ref, kv_up_ref, bias_ref,
-    lower_bias_ref, branch_ref, q_ref, kv_ref, out_ref,
-    branch_s, out_s, upper_q_s, normed_s, sum_s, keys_s, values_s, sems, unit_sems, *, chunk
+    own_ref, other_ref, gain_ref, kw_ref, vw_ref, query_held, kept_ref, normed_ref, kv_up_ref, bias_ref,
+    lower_bias_ref, qw_ref, branch_ref, q_ref, kv_ref, out_ref,
+    rest_s, branch_s, out_s, upper_q_s, normed_s, sum_s, keys_s, values_s, sems, unit_sems, *, chunk
 ):
     half = own_ref.shape[1]
     kv_width = kw_ref.shape[1]
     q_width = qw_ref.shape[1]
+    piece = query_held.shape[1]
+    rest_in = pltpu.make_async_copy(qw_ref.at[:, pl.ds(piece, q_width - piece)], rest_s, sems.at[2])
+    rest_in.start()
     normed_s[half:, :] = normed_ref[...]
     add_and_norm(own_ref, other_ref, gain_ref, branch_s, normed_s, 0, sum_s, kept_ref, chunk)
     branch_out = pltpu.make_async_copy(branch_s, branch_ref, sems.at[0])
@@ -321,10 +348,11 @@
     stage_keys(kv_up_ref[:, :kv_width], keys_s)
     stage_values(kv_up_ref[:, kv_width:], values_s)
 
-    piece = q_width // 2
-    for first in range(0, q_width, piece):
+    for first, weight_ref in ((0, query_held), (piece, rest_s)):
+        if first > 0:
+            rest_in.wait()
         columns = slice(first, first + piece)
-        queries = dot(normed_s[...], qw_ref[:, columns], ((1,), (0,))).astype(BF16)
+        queries = dot(normed_s[...], weight_ref[...], ((1,), (0,))).astype(BF16)
         q_ref[:, columns] = queries[:half]
         upper_q_s[:, columns] = queries[half:]
 
@@ -415,16 +443,17 @@
         out_specs=vmem_specs(1)[0],
         scratch_shapes=[dma((2,))],
         compiler_params=params(16),
-        cost_estimate=pl.CostEstimate(flops=10**10, bytes_accessed=10**6, transcendentals=0),
         name="pack",
     )(keys, values)
     halo = shifted(packed, "ctx")
     attn_s = pltpu.VMEM((q_width, half), BF16)
     (
-        attn_upper, q_held, k_held, v_held, window_bias, upper_causal, lower_causal, gain
+        own_upper, held, attn_first, q_held, k_held, v_held, window_bias, upper_causal, lower_causal, gain
     ) = pl.pallas_call(
         window_upper_kernel,
         out_shape=(
+            pltpu.VMEM((width, half), BF16),
+            pltpu.VMEM((width, q_width), BF16),
             attn_s,
             pltpu.VMEM((rows, q_width), BF16),
             pltpu.VMEM((rows, kv_width), BF16),
@@ -434,35 +463,35 @@
             pltpu.VMEM((rows, half), F32),
             pltpu.VMEM((width,), F32),
         ),
-        in_specs=hbm_specs(5),
-        out_specs=tuple(vmem_specs(8)),
-        scratch_shapes=[pltpu.SMEM(doc_lengths.shape, jnp.int32)]
+        in_specs=hbm_specs(6),
+        out_specs=tuple(vmem_specs(10)),
+        scratch_shapes=[pltpu.SMEM(doc_lengths.shape, jnp.int32), attn_s]
         + attention_scratch(kv_heads, half)
-        + [pltpu.VMEM((half, half), F32), dma((8,))],
-        compiler_params=params(8),
+        + [pltpu.VMEM((half, half), F32), dma((8,)), dma((10,))],
+        compiler_params=params(12),
         name="window_upper",
-    )(lengths, queries, keys, values, in_hbm(norm_gain))
-    held = in_vmem(jnp.transpose(out_weight))
-    own_upper, attn_first = pl.pallas_call(
-        functools.partial(project_upper_kernel, chunk=chunk),
-        out_shape=(pltpu.VMEM((width, half), BF16), attn_s),
-        in_specs=vmem_specs(6),
-        out_specs=tuple(vmem_specs(2)),
-        scratch_shapes=attention_scratch(kv_heads, half),
-        compiler_params=params(8),
-        name="project_upper",
-    )(held, attn_upper, q_held, k_held, v_held, window_bias)
-    key_held, value_held, query_held = [in_vmem(x) for x in (key_weight, value_weight, query_weight)]
+    )(lengths, queries, keys, values, in_hbm(jnp.transpose(out_weight)), in_hbm(norm_gain))
+    key_weight, value_weight, query_weight = [
+        in_hbm(x) for x in (key_weight, value_weight, query_weight)
+    ]
     other_upper = swapped(own_upper, "head")
-    own_lower = pl.pallas_call(
+    own_lower, key_held, value_held, query_held = pl.pallas_call(
         functools.partial(window_lower_kernel, chunk=chunk),
-        out_shape=pltpu.VMEM((width, half), BF16),
-        in_specs=vmem_specs(7),
-        out_specs=vmem_specs(1)[0],
-        scratch_shapes=[attn_s] + attention_scratch(kv_heads, rows),
+        out_shape=(
+            pltpu.VMEM((width, half), BF16),
+            pltpu.VMEM((width, kv_width), BF16),
+            pltpu.VMEM((width, kv_width), BF16),
+            pltpu.VMEM((width, q_width // 2), BF16),
+        ),
+        in_specs=vmem_specs(7) + hbm_specs(3),
+        out_specs=tuple(vmem_specs(4)),
+        scratch_shapes=[attn_s] + attention_scratch(kv_heads, rows) + [dma((3,))],
         compiler_params=params(16),
         name="window_lower",
-    )(q_held, k_held, v_held, in_vmem(halo), held, window_bias, attn_first)
+    )(
+        q_held, k_held, v_held, in_vmem(halo), held, window_bias, attn_first,
+        key_weight, value_weight, query_weight,
+    )
     other_lower = swapped(own_lower, "head")
     branch_upper, normed_upper, pairs_upper = pl.pallas_call(
         functools.partial(norm_upper_kernel, chunk=192),
@@ -486,9 +515,10 @@
             pltpu.VMEM((half, 2 * kv_width), BF16),
             pltpu.HBM((rows, q_width), BF16),
         ),
-        in_specs=vmem_specs(11),
+        in_specs=vmem_specs(11) + hbm_specs(1),
         out_specs=(hbm_specs(1)[0], *vmem_specs(2), hbm_specs(1)[0]),
         scratch_shapes=[
+            pltpu.VMEM((width, q_width // 2), BF16),
             pltpu.VMEM((width, half), BF16),
             pltpu.VMEM((half, q_width), BF16),
             pltpu.VMEM((half, q_width), BF16),
@@ -496,12 +526,13 @@
             pltpu.VMEM((width, half), F32),
         ]
         + attention_scratch(kv_heads, half)
-        + [dma((2,)), dma((q_width // (2 * LANES),))],
-        compiler_params=params(16),
+        + [dma((3,)), dma((q_width // (2 * LANES),))],
+        compiler_params=params(22),
         name="causal_upper",
     )(
         own_lower, other_lower, gain, key_held, value_held, query_held,
         branch_upper, normed_upper, pairs_upper, upper_causal, lower_causal,
+        query_weight,
     )
     causal_out = pl.pallas_call(
         causal_lower_kernel,

time: 28.1 us -> 32.2 us (1.15)
  Pallas kernels: 20.5 us -> 25.7 us
  waiting for transfers between devices: 0.79 us -> 0.01 us
    pallas_call x2 -> x1, Pallas kernels: 6.56 us -> 11.2 us  [local(): pl.pallas_call(window_upper_kernel, out_shape=(pltpu.VMEM((width, half),...]
    ppermute x2, waiting for transfers between devices: 0.78 us -> 0.01 us  [shifted(): return lax.ppermute(block, axis, [(i, (i + 1) % size) for i in range(size)])]
    ppermute x2, starting transfers between devices: 5.58 us -> 4.85 us  [shifted(): return lax.ppermute(block, axis, [(i, (i + 1) % size) for i in range(size)])]
    ppermute x2, starting transfers between devices: 0.14 us -> 0.62 us  [swapped(): return lax.ppermute(block, axis, [(i, size - 1 - i) for i in range(size)])]
    pallas_call x1, Pallas kernels: 3.25 us -> 3.61 us  [local(): pl.pallas_call(functools.partial(window_lower_kernel, chunk=chunk), out_s...]
  transfers between devices with their start and end apart: 4 -> 4, of which waited for: 1 -> 0; matrix products, arithmetic and copies ran while one was open for 0% -> 0% of each run, Pallas kernels for 69% -> 77%
where the time goes in v10:
time: 32.2 us; the launch traced here: 32 us
  Pallas kernels  25.7 us (80%)
  starting transfers between devices  5.47 us (17%)
  between operations  0.86 us (3%)
    pallas_call x1, Pallas kernels, local(): pl.pallas_call(window_upper_kernel, out_shape=(pltpu.VMEM((width, half),...  11.2 us
    pallas_call x1, Pallas kernels, local(): pl.pallas_call(functools.partial(causal_upper_kernel, chunk=192), out_sha...  8.51 us
    ppermute x2, starting transfers between devices, shifted(): return lax.ppermute(block, axis, [(i, (i + 1) % size) for i in range(size)])  4.85 us
    pallas_call x1, Pallas kernels, local(): pl.pallas_call(functools.partial(window_lower_kernel, chunk=chunk), out_s...  3.61 us
    pallas_call x1, Pallas kernels, local(): pl.pallas_call(functools.partial(norm_upper_kernel, chunk=192), out_shape...  1.33 us
    pallas_call x1, Pallas kernels, local(): pl.pallas_call(pack_kernel, out_shape=jax.ShapeDtypeStruct((half, 2 * kv_...  0.89 us
  transfers between devices with their start and end apart: 4, of which 0 were waited for; matrix products, arithmetic and copies ran while one was open for 0% of the time, Pallas kernels for 77%

profile of v10, /device:TPU:0, one launch (start us, length us, event | category | flops | bytes accessed | tf_op | source)
XLA Modules:
  0.0 32.0 jit_solution(6353536976980416107)
XLA Ops:
  0.6 0.9 %pack.1 = bf16[128,512]{1,0:T(8,128)(2,1)S(1)} custom-call(bf16[256,256]{1,0:T(8,128)(2,1)} %k_ref.3, bf16[256,256]{1,0:T(8,128)(2,1)} %v_ref.3), custom_call_target="tpu_custom_call" | custom-call | tf_op jit(solution)/shard_map/pack/pallas_call | solution.py:439
  1.5 3.0 %collective-permute-start = (bf16[128,512]{1,0:T(8,128)(2,1)S(1)}, bf16[128,512]{1,0:T(8,128)(2,1)S(1)}, u32[]{:S(2)}, u32[]{:S(2)}) collective-permute-start(bf16[128,512]{1,0:T(8,128)(2,1)S(1)} %pack.1), channel_id=1, source_target_pairs={{0,2},{2,4},{4,6},{6,8},{8,10},{10,12},{12,14},{14,16},{16,18},{18... | collective-permute-start | bytes 393224 | tf_op jit(solution)/shard_map/ppermute | solution.py:47
  4.5 11.2 %window_upper.1 = (bf16[2880,128]{1,0:T(8,128)(2,1)S(1)}, bf16[2880,2048]{1,0:T(8,128)(2,1)S(1)}, bf16[2048,128]{1,0:T(8,128)(2,1)S(1)}, bf16[256,2048]{1,0:T(8,...) custom-call(s32[32]{0:T(128)} %lengths_ref.1, ...), custom_call_target="tpu_custom_call" | custom-call | tf_op jit(solution)/shard_map/window_upper/pallas_call | solution.py:452
  15.8 0.1 collective-permute-start.2
  15.8 0.0 collective-permute-done.halo_ref
  15.8 3.6 %window_lower.1 = (bf16[2880,128]{1,0:T(8,128)(2,1)S(1)}, bf16[2880,256]{1,0:T(8,128)(2,1)S(1)}, bf16[2880,256]{1,0:T(8,128)(2,1)S(1)}, bf16[2880,1024]{1,0:T(8,128)(2,1)S(1)}) custom-call(bf16[256,2048]{1,0:T(8,128)(2,1)S(1)} %get-tuple-element.23.q_ref, bf16[256,256]{1,0:T(8,128)(2,1)S(1)} %get-tuple-element.24.k_ref, ...), custom_call_target="tpu_custom_call" | custom-call | tf_op jit(solution)/shard_map/window_lower/pallas_call | solution.py:478
  19.5 0.5 %collective-permute-start.1 = (bf16[2880,128]{1,0:T(8,128)(2,1)S(1)}, bf16[2880,128]{1,0:T(8,128)(2,1)S(1)}, u32[]{:S(2)}, u32[]{:S(2)}) collective-permute-start(bf16[2880,128]{1,0:T(8,128)(2,1)S(1)} %get-tuple-element.29.own_ref), channel_id=1, source_target_pairs={{0,1},{1,0},{2,3},{3,2},{4,5},{5,4},{6,7},{7,6},{8,9},{9,8},{10,11... | collective-permute-start | bytes 2211848 | tf_op jit(solution)/shard_map/ppermute | solution.py:52
  20.0 0.0 collective-permute-done.2.other_ref
  20.0 1.3 %norm_upper.1 = (bf16[2880,128]{1,0:T(8,128)(2,1)S(1)}, bf16[128,2880]{1,0:T(8,128)(2,1)S(1)}, bf16[128,512]{1,0:T(8,128)(2,1)S(1)}) custom-call(bf16[2880,128]{1,0:T(8,128)(2,1)S(1)} %get-tuple-element.34.own_ref, bf16[2880,128]{1,0:T(8,128)(2,1)S(1)} %collective-permute-done.2.other_ref, f32[2880]{0:T(1024)S(1)} %get-tuple-element.30.gain_ref, ...), custom_call_target="tpu_custom_call" | custom-call | tf_op jit(solution)/shard_map/norm_upper/pallas_call | solution.py:496
  21.4 1.9 %collective-permute-start.3 = (bf16[128,512]{1,0:T(8,128)(2,1)S(1)}, bf16[128,512]{1,0:T(8,128)(2,1)S(1)}, u32[]{:S(2)}, u32[]{:S(2)}) collective-permute-start(bf16[128,512]{1,0:T(8,128)(2,1)S(1)} %get-tuple-element.37.kv_up_ref), channel_id=1, source_target_pairs={{0,2},{2,4},{4,6},{6,8},{8,10},{10,12},{12,14},{14,16},{16,18},{18... | collective-permute-start | bytes 393224 | tf_op jit(solution)/shard_map/ppermute | solution.py:47
  23.2 0.0 collective-permute-done.1.other_ref
  23.2 8.5 %causal_upper.1 = (bf16[2880,128]{1,0:T(8,128)(2,1)}, bf16[128,2048]{1,0:T(8,128)(2,1)S(1)}, bf16[128,512]{1,0:T(8,128)(2,1)S(1)}, bf16[256,2048]{1,0:T(8,128)(2,1)}) custom-call(bf16[2880,128]{1,0:T(8,128)(2,1)S(1)} %get-tuple-element.29.own_ref, bf16[2880,128]{1,0:T(8,128)(2,1)S(1)} %collective-permute-done.1.other_ref, ...), custom_call_target="tpu_custom_call" | custom-call | tf_op jit(solution)/shard_map/causal_upper/pallas_call | solution.py:510
  31.7 0.0 collective-permute-done.3.halo_ref
  31.7 0.1 causal_lower.1
Async XLA Ops:
  1.5 14.3 %collective-permute-start = (bf16[128,512]{1,0:T(8,128)(2,1)S(1)}, bf16[128,512]{1,0:T(8,128)(2,1)S(1)}, u32[]{:S(2)}, u32[]{:S(2)}) collective-permute-start(bf16[128,512]{1,0:T(8,128)(2,1)S(1)} %pack.1), channel_id=1, source_target_pairs={{0,2},{2,4},{4,6},{6,8},{8,10},{10,12},{12,14},{14,16},{16,18},{18... | collective-permute-start | bytes 393224 | tf_op jit(solution)/shard_map/ppermute | solution.py:47
  15.8 4.3 %collective-permute-start.2 = (bf16[2880,128]{1,0:T(8,128)(2,1)S(1)}, bf16[2880,128]{1,0:T(8,128)(2,1)S(1)}, u32[]{:S(2)}, u32[]{:S(2)}) collective-permute-start(bf16[2880,128]{1,0:T(8,128)(2,1)S(1)} %get-tuple-element.34.own_ref), channel_id=1, source_target_pairs={{0,1},{1,0},{2,3},{3,2},{4,5},{5,4},{6,7},{7,6},{8,9},{9,8},{10,11... | collective-permute-start | bytes 2211848 | tf_op jit(solution)/shard_map/ppermute | solution.py:52
  19.5 3.8 %collective-permute-start.1 = (bf16[2880,128]{1,0:T(8,128)(2,1)S(1)}, bf16[2880,128]{1,0:T(8,128)(2,1)S(1)}, u32[]{:S(2)}, u32[]{:S(2)}) collective-permute-start(bf16[2880,128]{1,0:T(8,128)(2,1)S(1)} %get-tuple-element.29.own_ref), channel_id=1, source_target_pairs={{0,1},{1,0},{2,3},{3,2},{4,5},{5,4},{6,7},{7,6},{8,9},{9,8},{10,11... | collective-permute-start | bytes 2211848 | tf_op jit(solution)/shard_map/ppermute | solution.py:52
  21.4 10.4 %collective-permute-start.3 = (bf16[128,512]{1,0:T(8,128)(2,1)S(1)}, bf16[128,512]{1,0:T(8,128)(2,1)S(1)}, u32[]{:S(2)}, u32[]{:S(2)}) collective-permute-start(bf16[128,512]{1,0:T(8,128)(2,1)S(1)} %get-tuple-element.37.kv_up_ref), channel_id=1, source_target_pairs={{0,2},{2,4},{4,6},{6,8},{8,10},{10,12},{12,14},{14,16},{16,18},{18... | collective-permute-start | bytes 393224 | tf_op jit(solution)/shard_map/ppermute | solution.py:47

commit v11 on v8

--- a/solution.py
+++ b/solution.py
@@ -251,9 +251,16 @@
 
 
 def window_lower_kernel(
-    q_ref, k_ref, v_ref, halo_ref, weight_ref, bias_ref, first_ref,
-    out_ref, attn_s, keys_s, values_s, *, chunk
-):
+    q_ref, k_ref, v_ref, halo_ref, weight_ref, bias_ref, first_ref, kw_ref, vw_ref,
+    out_ref, pair_held, attn_s, keys_s, values_s, sems, *, chunk
+):
+    width = kw_ref.shape[1]
+    copies = [
+        pltpu.make_async_copy(kw_ref, pair_held.at[:, pl.ds(0, width)], sems.at[0]),
+        pltpu.make_async_copy(vw_ref, pair_held.at[:, pl.ds(width, width)], sems.at[1]),
+    ]
+    for copy in copies:
+        copy.start()
     half = halo_ref.shape[0]
     kv_width = k_ref.shape[1]
     ctx = lax.axis_index("ctx")
@@ -273,6 +280,8 @@
         window_heads(queries_of, keys_s, values_s, bias_ref, attn_s, q_ref.shape[1])
 
     project(weight_ref, attn_s, out_ref, chunk)
+    for copy in copies:
+        copy.wait()
 
 
 def add_and_norm(own_ref, other_ref, gain_ref, branch_ref, normed_ref, first_row, sum_s, keep_ref, chunk):
@@ -298,21 +307,19 @@
 
 
 def norm_upper_kernel(
-    own_ref, other_ref, gain_ref, kw_ref, vw_ref, branch_ref, normed_ref, kv_ref, sum_s, *, chunk
+    own_ref, other_ref, gain_ref, pair_ref, branch_ref, normed_ref, kv_ref, sum_s, *, chunk
 ):
     add_and_norm(own_ref, other_ref, gain_ref, branch_ref, normed_ref, 0, sum_s, None, chunk)
-    kv_width = kw_ref.shape[1]
-    kv_ref[:, :kv_width] = dot(normed_ref[...], kw_ref[...], ((1,), (0,))).astype(BF16)
-    kv_ref[:, kv_width:] = dot(normed_ref[...], vw_ref[...], ((1,), (0,))).astype(BF16)
+    kv_ref[...] = dot(normed_ref[...], pair_ref[...], ((1,), (0,))).astype(BF16)
 
 
 def causal_upper_kernel(
-    own_ref, other_ref, gain_ref, kw_ref, vw_ref, qw_ref, kept_ref, normed_ref, kv_up_ref, bias_ref,
+    own_ref, other_ref, gain_ref, pair_ref, qw_ref, kept_ref, normed_ref, kv_up_ref, bias_ref,
     lower_bias_ref, branch_ref, q_ref, kv_ref, out_ref,
     branch_s, out_s, upper_q_s, normed_s, sum_s, keys_s, values_s, sems, unit_sems, *, chunk
 ):
     half = own_ref.shape[1]
-    kv_width = kw_ref.shape[1]
+    kv_width = kv_ref.shape[1] // 2
     q_width = qw_ref.shape[1]
     normed_s[half:, :] = normed_ref[...]
     add_and_norm(own_ref, other_ref, gain_ref, branch_s, normed_s, 0, sum_s, kept_ref, chunk)
@@ -321,12 +328,9 @@
     stage_keys(kv_up_ref[:, :kv_width], keys_s)
     stage_values(kv_up_ref[:, kv_width:], values_s)
 
-    piece = q_width // 2
-    for first in range(0, q_width, piece):
-        columns = slice(first, first + piece)
-        queries = dot(normed_s[...], qw_ref[:, columns], ((1,), (0,))).astype(BF16)
-        q_ref[:, columns] = queries[:half]
-        upper_q_s[:, columns] = queries[half:]
+    queries = dot(normed_s[...], qw_ref[...], ((1,), (0,))).astype(BF16)
+    q_ref[...] = queries[:half]
+    upper_q_s[...] = queries[half:]
 
     def queries_of(unit):
         return upper_q_s[:, unit.lane : unit.lane + 2 * LANES]
@@ -334,8 +338,7 @@
     causal_heads(queries_of, keys_s, values_s, bias_ref, out_s, q_width, lambda unit: None)
     upper_out = pltpu.make_async_copy(out_s, out_ref.at[pl.ds(half, half)], sems.at[1])
     upper_out.start()
-    kv_ref[:, :kv_width] = dot(normed_s[:half, :], kw_ref[...], ((1,), (0,))).astype(BF16)
-    kv_ref[:, kv_width:] = dot(normed_s[:half, :], vw_ref[...], ((1,), (0,))).astype(BF16)
+    kv_ref[...] = dot(normed_s[:half, :], pair_ref[...], ((1,), (0,))).astype(BF16)
     branch_out.wait()
     upper_out.wait()
 
@@ -452,17 +455,17 @@
         compiler_params=params(8),
         name="project_upper",
     )(held, attn_upper, q_held, k_held, v_held, window_bias)
-    key_held, value_held, query_held = [in_vmem(x) for x in (key_weight, value_weight, query_weight)]
+    query_held = in_vmem(query_weight)
     other_upper = swapped(own_upper, "head")
-    own_lower = pl.pallas_call(
+    own_lower, pair_held = pl.pallas_call(
         functools.partial(window_lower_kernel, chunk=chunk),
-        out_shape=pltpu.VMEM((width, half), BF16),
-        in_specs=vmem_specs(7),
-        out_specs=vmem_specs(1)[0],
-        scratch_shapes=[attn_s] + attention_scratch(kv_heads, rows),
+        out_shape=(pltpu.VMEM((width, half), BF16), pltpu.VMEM((width, 2 * kv_width), BF16)),
+        in_specs=vmem_specs(7) + hbm_specs(2),
+        out_specs=tuple(vmem_specs(2)),
+        scratch_shapes=[attn_s] + attention_scratch(kv_heads, rows) + [dma((2,))],
         compiler_params=params(16),
         name="window_lower",
-    )(q_held, k_held, v_held, in_vmem(halo), held, window_bias, attn_first)
+    )(q_held, k_held, v_held, in_vmem(halo), held, window_bias, attn_first, in_hbm(key_weight), in_hbm(value_weight))
     other_lower = swapped(own_lower, "head")
     branch_upper, normed_upper, pairs_upper = pl.pallas_call(
         functools.partial(norm_upper_kernel, chunk=192),
@@ -471,12 +474,12 @@
             pltpu.VMEM((half, width), BF16),
             pltpu.VMEM((half, 2 * kv_width), BF16),
         ),
-        in_specs=vmem_specs(5),
+        in_specs=vmem_specs(4),
         out_specs=tuple(vmem_specs(3)),
         scratch_shapes=[pltpu.VMEM((width, half), F32)],
         compiler_params=params(16),
         name="norm_upper",
-    )(own_upper, other_upper, gain, key_held, value_held)
+    )(own_upper, other_upper, gain, pair_held)
     earlier = shifted(pairs_upper, "ctx")
     branch, causal_queries, pairs_lower, causal_out = pl.pallas_call(
         functools.partial(causal_upper_kernel, chunk=192),
@@ -486,7 +489,7 @@
             pltpu.VMEM((half, 2 * kv_width), BF16),
             pltpu.HBM((rows, q_width), BF16),
         ),
-        in_specs=vmem_specs(11),
+        in_specs=vmem_specs(10),
         out_specs=(hbm_specs(1)[0], *vmem_specs(2), hbm_specs(1)[0]),
         scratch_shapes=[
             pltpu.VMEM((width, half), BF16),
@@ -500,7 +503,7 @@
         compiler_params=params(16),
         name="causal_upper",
     )(
-        own_lower, other_lower, gain, key_held, value_held, query_held,
+        own_lower, other_lower, gain, pair_held, query_held,
         branch_upper, normed_upper, pairs_upper, upper_causal, lower_causal,
     )
     causal_out = pl.pallas_call(

time: 28.1 us -> 28.1 us (level)
  no operation moved by 1% of the time
where the time goes in v11:
time: 28.1 us; the launch traced here: 27.9 us
  Pallas kernels  20.5 us (73%)
  starting transfers between devices  5.69 us (20%)
  between operations  0.91 us (3%)
  waiting for transfers between devices  0.84 us (3%)
    pallas_call x1, Pallas kernels, local(): pl.pallas_call(functools.partial(causal_upper_kernel, chunk=192), out_sha...  8.2 us
    ppermute x2, starting transfers between devices, shifted(): return lax.ppermute(block, axis, [(i, (i + 1) % size) for i in range(size)])  5.55 us
    pallas_call x1, Pallas kernels, local(): pl.pallas_call(functools.partial(project_upper_kernel, chunk=chunk), out_...  4.31 us
    pallas_call x1, Pallas kernels, local(): pl.pallas_call(functools.partial(window_lower_kernel, chunk=chunk), out_s...  3.28 us
    pallas_call x1, Pallas kernels, local(): pl.pallas_call(window_upper_kernel, out_shape=(attn_s, pltpu.VMEM((rows,...  2.25 us
    pallas_call x1, Pallas kernels, local(): pl.pallas_call(functools.partial(norm_upper_kernel, chunk=192), out_shape...  1.32 us
    pallas_call x1, Pallas kernels, local(): pl.pallas_call(pack_kernel, out_shape=jax.ShapeDtypeStruct((half, 2 * kv_...  1.04 us
    ppermute x2, waiting for transfers between devices, shifted(): return lax.ppermute(block, axis, [(i, (i + 1) % size) for i in range(size)])  0.83 us
  transfers between devices with their start and end apart: 4, of which 1 were waited for; matrix products, arithmetic and copies ran while one was open for 0% of the time, Pallas kernels for 69%

profile of v11, /device:TPU:0, one launch (start us, length us, event | category | flops | bytes accessed | tf_op | source)
XLA Modules:
  0.0 27.9 jit_solution(8246788542144974284)
XLA Ops:
  0.6 0.0 copy-start
  0.6 1.0 %pack.1 = bf16[128,512]{1,0:T(8,128)(2,1)S(1)} custom-call(bf16[256,256]{1,0:T(8,128)(2,1)} %k_ref.3, bf16[256,256]{1,0:T(8,128)(2,1)} %v_ref.3), custom_call_target="tpu_custom_call" | custom-call | flops 10000000000 | bytes 1000000 | tf_op jit(solution)/shard_map/pack/pallas_call | solution.py:414
  1.7 3.0 %collective-permute-start = (bf16[128,512]{1,0:T(8,128)(2,1)S(1)}, bf16[128,512]{1,0:T(8,128)(2,1)S(1)}, u32[]{:S(2)}, u32[]{:S(2)}) collective-permute-start(bf16[128,512]{1,0:T(8,128)(2,1)S(1)} %pack.1), channel_id=1, source_target_pairs={{0,2},{2,4},{4,6},{6,8},{8,10},{10,12},{12,14},{14,16},{16,18},{18... | collective-permute-start | bytes 393224 | tf_op jit(solution)/shard_map/ppermute | solution.py:47
  4.7 2.2 %window_upper.1 = (bf16[2048,128]{1,0:T(8,128)(2,1)S(1)}, bf16[256,2048]{1,0:T(8,128)(2,1)S(1)}, bf16[256,256]{1,0:T(8,128)(2,1)S(1)}, bf16[256,256]{1,0:T(8,128...) custom-call(s32[32]{0:T(128)} %lengths_ref.1, ...), custom_call_target="tpu_custom_call" | custom-call | tf_op jit(solution)/shard_map/window_upper/pallas_call | solution.py:428
  6.9 0.0 copy-done
  6.9 4.3 %project_upper.1 = (bf16[2880,128]{1,0:T(8,128)(2,1)S(1)}, bf16[2048,128]{1,0:T(8,128)(2,1)S(1)}) custom-call(bf16[2880,2048]{1,0:T(8,128)(2,1)S(1)} %bitcast.2, bf16[2048,128]{1,0:T(8,128)(2,1)S(1)} %get-tuple-element.25.attn_ref, bf16[256,2048]{1,0:T(8,128)(2,1)S(1)} %get-tuple-element.21.q_ref, bf16[256,256]{1,0:T(8,128)(2,1)S(1)} %get-tuple-element.22.k_ref, ...), custom_call_target="tpu_custom_call" | custom-call | tf_op jit(solution)/shard_map/project_upper/pallas_call | solution.py:449
  11.3 0.1 collective-permute-start.2
  11.3 0.8 %collective-permute-done.halo_ref = bf16[128,512]{1,0:T(8,128)(2,1)S(1)} collective-permute-done((bf16[128,512]{1,0:T(8,128)(2,1)S(1)}, bf16[128,512]{1,0:T(8,128)(2,1)S(1)}, u32[]{:S(2)}, u32[]{:S(2)}) %collective-permute-start) | collective-permute-done | bytes 131104 | tf_op jit(solution)/shard_map/ppermute | solution.py:47
  12.2 0.0 slice-start
  12.2 0.0 slice-start.1
  12.2 0.0 slice-start.2
  12.2 3.3 %window_lower.1 = (bf16[2880,128]{1,0:T(8,128)(2,1)S(1)}, bf16[2880,512]{1,0:T(8,128)(2,1)S(1)}) custom-call(bf16[256,2048]{1,0:T(8,128)(2,1)S(1)} %get-tuple-element.21.q_ref, bf16[256,256]{1,0:T(8,128)(2,1)S(1)} %get-tuple-element.22.k_ref, bf16[256,256]{1,0:T(8,128)(2,1)S(1)} %get-tuple-element.23.v_ref, ...), custom_call_target="tpu_custom_call" | custom-call | tf_op jit(solution)/shard_map/window_lower/pallas_call | solution.py:460
  15.5 0.1 collective-permute-start.1
  15.5 0.0 collective-permute-done.2.other_ref
  15.6 1.3 %norm_upper.1 = (bf16[2880,128]{1,0:T(8,128)(2,1)S(1)}, bf16[128,2880]{1,0:T(8,128)(2,1)S(1)}, bf16[128,512]{1,0:T(8,128)(2,1)S(1)}) custom-call(bf16[2880,128]{1,0:T(8,128)(2,1)S(1)} %get-tuple-element.30.own_ref, bf16[2880,128]{1,0:T(8,128)(2,1)S(1)} %collective-permute-done.2.other_ref, f32[2880]{0:T(1024)S(1)} %get-tuple-element.28.gain_ref, ...), custom_call_target="tpu_custom_call" | custom-call | tf_op jit(solution)/shard_map/norm_upper/pallas_call | solution.py:470
  16.9 2.6 %collective-permute-start.3 = (bf16[128,512]{1,0:T(8,128)(2,1)S(1)}, bf16[128,512]{1,0:T(8,128)(2,1)S(1)}, u32[]{:S(2)}, u32[]{:S(2)}) collective-permute-start(bf16[128,512]{1,0:T(8,128)(2,1)S(1)} %get-tuple-element.33.kv_up_ref), channel_id=1, source_target_pairs={{0,2},{2,4},{4,6},{6,8},{8,10},{10,12},{12,14},{14,16},{16,18},{18... | collective-permute-start | bytes 393224 | tf_op jit(solution)/shard_map/ppermute | solution.py:47
  19.4 0.0 collective-permute-done.1.other_ref
  19.4 0.0 slice-done
  19.4 0.0 slice-done.1
  19.4 0.0 slice-done.2
  19.5 8.2 %causal_upper.1 = (bf16[2880,128]{1,0:T(8,128)(2,1)}, bf16[128,2048]{1,0:T(8,128)(2,1)S(1)}, bf16[128,512]{1,0:T(8,128)(2,1)S(1)}, bf16[256,2048]{1,0:T(8,128)(2,1)}) custom-call(bf16[2880,128]{1,0:T(8,128)(2,1)S(1)} %get-tuple-element.27.own_ref, bf16[2880,128]{1,0:T(8,128)(2,1)S(1)} %collective-permute-done.1.other_ref, ...), custom_call_target="tpu_custom_call" | custom-call | tf_op jit(solution)/shard_map/causal_upper/pallas_call | solution.py:484
  27.7 0.0 collective-permute-done.3.halo_ref
  27.7 0.1 causal_lower.1
  (1 shorter events, 0.0 us)
Async XLA Ops:
  0.6 6.3 %copy-start = (bf16[2048,2880]{0,1:T(8,128)(2,1)S(1)}, bf16[2048,2880]{0,1:T(8,128)(2,1)}, u32[]{:S(2)}) copy-start(bf16[2048,2880]{0,1:T(8,128)(2,1)} %param.12) | copy-start | bytes 35389444
  1.7 10.5 %collective-permute-start = (bf16[128,512]{1,0:T(8,128)(2,1)S(1)}, bf16[128,512]{1,0:T(8,128)(2,1)S(1)}, u32[]{:S(2)}, u32[]{:S(2)}) collective-permute-start(bf16[128,512]{1,0:T(8,128)(2,1)S(1)} %pack.1), channel_id=1, source_target_pairs={{0,2},{2,4},{4,6},{6,8},{8,10},{10,12},{12,14},{14,16},{16,18},{18... | collective-permute-start | bytes 393224 | tf_op jit(solution)/shard_map/ppermute | solution.py:47
  11.3 4.3 %collective-permute-start.2 = (bf16[2880,128]{1,0:T(8,128)(2,1)S(1)}, bf16[2880,128]{1,0:T(8,128)(2,1)S(1)}, u32[]{:S(2)}, u32[]{:S(2)}) collective-permute-start(bf16[2880,128]{1,0:T(8,128)(2,1)S(1)} %get-tuple-element.30.own_ref), channel_id=1, source_target_pairs={{0,1},{1,0},{2,3},{3,2},{4,5},{5,4},{6,7},{7,6},{8,9},{9,8},{10,11... | collective-permute-start | bytes 2211848 | tf_op jit(solution)/shard_map/ppermute | solution.py:52
  12.2 7.3 %slice-start = ((s8[11796480]{0:T(1024)(128)(4,1)}), s8[4194304]{0:T(1024)(128)(4,1)S(1)}, s32[]{:S(2)}) async-start(s8[11796480]{0:T(1024)(128)(4,1)} %bitcast.4), calls=%async_computation | async-start | bytes 8388608
  12.2 7.3 %slice-start.1 = ((s8[11796480]{0:T(1024)(128)(4,1)}), s8[4194304]{0:T(1024)(128)(4,1)S(1)}, s32[]{:S(2)}) async-start(s8[11796480]{0:T(1024)(128)(4,1)} %bitcast.4), calls=%async_computation.1 | async-start | bytes 8388608
  12.2 7.3 %slice-start.2 = ((s8[11796480]{0:T(1024)(128)(4,1)}), s8[3407872]{0:T(1024)(128)(4,1)S(1)}, s32[]{:S(2)}) async-start(s8[11796480]{0:T(1024)(128)(4,1)} %bitcast.4), calls=%async_computation.2 | async-start | bytes 6815744
  15.5 4.0 %collective-permute-start.1 = (bf16[2880,128]{1,0:T(8,128)(2,1)S(1)}, bf16[2880,128]{1,0:T(8,128)(2,1)S(1)}, u32[]{:S(2)}, u32[]{:S(2)}) collective-permute-start(bf16[2880,128]{1,0:T(8,128)(2,1)S(1)} %get-tuple-element.27.own_ref), channel_id=1, source_target_pairs={{0,1},{1,0},{2,3},{3,2},{4,5},{5,4},{6,7},{7,6},{8,9},{9,8},{10,11... | collective-permute-start | bytes 2211848 | tf_op jit(solution)/shard_map/ppermute | solution.py:52
  16.9 10.8 %collective-permute-start.3 = (bf16[128,512]{1,0:T(8,128)(2,1)S(1)}, bf16[128,512]{1,0:T(8,128)(2,1)S(1)}, u32[]{:S(2)}, u32[]{:S(2)}) collective-permute-start(bf16[128,512]{1,0:T(8,128)(2,1)S(1)} %get-tuple-element.33.kv_up_ref), channel_id=1, source_target_pairs={{0,2},{2,4},{4,6},{6,8},{8,10},{10,12},{12,14},{14,16},{16,18},{18... | collective-permute-start | bytes 393224 | tf_op jit(solution)/shard_map/ppermute | solution.py:47

commit v12 on v11

--- a/solution.py
+++ b/solution.py
@@ -91,7 +91,7 @@
 
 def stage_values(values, values_ref):
     count = values.shape[0]
-    turned = jnp.transpose(values.astype(F32)).astype(BF16)
+    turned = jnp.transpose(values)
     for head in range(values.shape[1] // HD):
         values_ref[head, :HD, :] = turned[head * HD : (head + 1) * HD]
         values_ref[head, HD:, :] = jnp.ones((TAIL, count), BF16)
@@ -165,8 +165,8 @@
             high = part[:, (2 + t) * rows : (3 + t) * rows]
             lane = unit.lane + t * LANES
             out_ref[:, lane : lane + LANES] = jnp.transpose(
-                jnp.concatenate([low, high], axis=0)
-            ).astype(BF16)
+                jnp.concatenate([low, high], axis=0).astype(BF16)
+            )
         ready(unit)
 
     pipelined(units_of(keys_ref.shape[0], q_width), queries_of, keys_ref, values_ref, bias_ref[...], write)

time: 28.1 us -> 28.1 us (level)
  no operation moved by 1% of the time
where the time goes in v12:
time: 28.1 us; the launch traced here: 27.9 us
  Pallas kernels  20.5 us (73%)
  starting transfers between devices  5.66 us (20%)
  between operations  0.91 us (3%)
  waiting for transfers between devices  0.84 us (3%)
    pallas_call x1, Pallas kernels, local(): pl.pallas_call(functools.partial(causal_upper_kernel, chunk=192), out_sha...  8.19 us
    ppermute x2, starting transfers between devices, shifted(): return lax.ppermute(block, axis, [(i, (i + 1) % size) for i in range(size)])  5.52 us
    pallas_call x1, Pallas kernels, local(): pl.pallas_call(functools.partial(project_upper_kernel, chunk=chunk), out_...  4.3 us
    pallas_call x1, Pallas kernels, local(): pl.pallas_call(functools.partial(window_lower_kernel, chunk=chunk), out_s...  3.28 us
    pallas_call x1, Pallas kernels, local(): pl.pallas_call(window_upper_kernel, out_shape=(attn_s, pltpu.VMEM((rows,...  2.25 us
    pallas_call x1, Pallas kernels, local(): pl.pallas_call(functools.partial(norm_upper_kernel, chunk=192), out_shape...  1.32 us
    pallas_call x1, Pallas kernels, local(): pl.pallas_call(pack_kernel, out_shape=jax.ShapeDtypeStruct((half, 2 * kv_...  1.04 us
    ppermute x2, waiting for transfers between devices, shifted(): return lax.ppermute(block, axis, [(i, (i + 1) % size) for i in range(size)])  0.84 us
  transfers between devices with their start and end apart: 4, of which 1 were waited for; matrix products, arithmetic and copies ran while one was open for 0% of the time, Pallas kernels for 69%

profile of v12, /device:TPU:0, one launch (start us, length us, event | category | flops | bytes accessed | tf_op | source)
XLA Modules:
  0.0 27.9 jit_solution(15520595162938784917)
XLA Ops:
  0.6 0.0 copy-start
  0.6 1.0 %pack.1 = bf16[128,512]{1,0:T(8,128)(2,1)S(1)} custom-call(bf16[256,256]{1,0:T(8,128)(2,1)} %k_ref.3, bf16[256,256]{1,0:T(8,128)(2,1)} %v_ref.3), custom_call_target="tpu_custom_call" | custom-call | flops 10000000000 | bytes 1000000 | tf_op jit(solution)/shard_map/pack/pallas_call | solution.py:414
  1.7 3.0 %collective-permute-start = (bf16[128,512]{1,0:T(8,128)(2,1)S(1)}, bf16[128,512]{1,0:T(8,128)(2,1)S(1)}, u32[]{:S(2)}, u32[]{:S(2)}) collective-permute-start(bf16[128,512]{1,0:T(8,128)(2,1)S(1)} %pack.1), channel_id=1, source_target_pairs={{0,2},{2,4},{4,6},{6,8},{8,10},{10,12},{12,14},{14,16},{16,18},{18... | collective-permute-start | bytes 393224 | tf_op jit(solution)/shard_map/ppermute | solution.py:47
  4.7 2.2 %window_upper.1 = (bf16[2048,128]{1,0:T(8,128)(2,1)S(1)}, bf16[256,2048]{1,0:T(8,128)(2,1)S(1)}, bf16[256,256]{1,0:T(8,128)(2,1)S(1)}, bf16[256,256]{1,0:T(8,128...) custom-call(s32[32]{0:T(128)} %lengths_ref.1, ...), custom_call_target="tpu_custom_call" | custom-call | tf_op jit(solution)/shard_map/window_upper/pallas_call | solution.py:428
  6.9 0.0 copy-done
  6.9 4.3 %project_upper.1 = (bf16[2880,128]{1,0:T(8,128)(2,1)S(1)}, bf16[2048,128]{1,0:T(8,128)(2,1)S(1)}) custom-call(bf16[2880,2048]{1,0:T(8,128)(2,1)S(1)} %bitcast.2, bf16[2048,128]{1,0:T(8,128)(2,1)S(1)} %get-tuple-element.25.attn_ref, bf16[256,2048]{1,0:T(8,128)(2,1)S(1)} %get-tuple-element.21.q_ref, bf16[256,256]{1,0:T(8,128)(2,1)S(1)} %get-tuple-element.22.k_ref, ...), custom_call_target="tpu_custom_call" | custom-call | tf_op jit(solution)/shard_map/project_upper/pallas_call | solution.py:449
  11.3 0.1 collective-permute-start.2
  11.3 0.8 %collective-permute-done.halo_ref = bf16[128,512]{1,0:T(8,128)(2,1)S(1)} collective-permute-done((bf16[128,512]{1,0:T(8,128)(2,1)S(1)}, bf16[128,512]{1,0:T(8,128)(2,1)S(1)}, u32[]{:S(2)}, u32[]{:S(2)}) %collective-permute-start) | collective-permute-done | bytes 131104 | tf_op jit(solution)/shard_map/ppermute | solution.py:47
  12.2 0.0 slice-start
  12.2 0.0 slice-start.1
  12.2 0.0 slice-start.2
  12.2 3.3 %window_lower.1 = (bf16[2880,128]{1,0:T(8,128)(2,1)S(1)}, bf16[2880,512]{1,0:T(8,128)(2,1)S(1)}) custom-call(bf16[256,2048]{1,0:T(8,128)(2,1)S(1)} %get-tuple-element.21.q_ref, bf16[256,256]{1,0:T(8,128)(2,1)S(1)} %get-tuple-element.22.k_ref, bf16[256,256]{1,0:T(8,128)(2,1)S(1)} %get-tuple-element.23.v_ref, ...), custom_call_target="tpu_custom_call" | custom-call | tf_op jit(solution)/shard_map/window_lower/pallas_call | solution.py:460
  15.5 0.1 collective-permute-start.1
  15.5 0.0 collective-permute-done.2.other_ref
  15.6 1.3 %norm_upper.1 = (bf16[2880,128]{1,0:T(8,128)(2,1)S(1)}, bf16[128,2880]{1,0:T(8,128)(2,1)S(1)}, bf16[128,512]{1,0:T(8,128)(2,1)S(1)}) custom-call(bf16[2880,128]{1,0:T(8,128)(2,1)S(1)} %get-tuple-element.30.own_ref, bf16[2880,128]{1,0:T(8,128)(2,1)S(1)} %collective-permute-done.2.other_ref, f32[2880]{0:T(1024)S(1)} %get-tuple-element.28.gain_ref, ...), custom_call_target="tpu_custom_call" | custom-call | tf_op jit(solution)/shard_map/norm_upper/pallas_call | solution.py:470
  16.9 2.5 %collective-permute-start.3 = (bf16[128,512]{1,0:T(8,128)(2,1)S(1)}, bf16[128,512]{1,0:T(8,128)(2,1)S(1)}, u32[]{:S(2)}, u32[]{:S(2)}) collective-permute-start(bf16[128,512]{1,0:T(8,128)(2,1)S(1)} %get-tuple-element.33.kv_up_ref), channel_id=1, source_target_pairs={{0,2},{2,4},{4,6},{6,8},{8,10},{10,12},{12,14},{14,16},{16,18},{18... | collective-permute-start | bytes 393224 | tf_op jit(solution)/shard_map/ppermute | solution.py:47
  19.4 0.0 collective-permute-done.1.other_ref
  19.4 0.0 slice-done
  19.4 0.0 slice-done.1
  19.4 0.0 slice-done.2
  19.4 8.2 %causal_upper.1 = (bf16[2880,128]{1,0:T(8,128)(2,1)}, bf16[128,2048]{1,0:T(8,128)(2,1)S(1)}, bf16[128,512]{1,0:T(8,128)(2,1)S(1)}, bf16[256,2048]{1,0:T(8,128)(2,1)}) custom-call(bf16[2880,128]{1,0:T(8,128)(2,1)S(1)} %get-tuple-element.27.own_ref, bf16[2880,128]{1,0:T(8,128)(2,1)S(1)} %collective-permute-done.1.other_ref, ...), custom_call_target="tpu_custom_call" | custom-call | tf_op jit(solution)/shard_map/causal_upper/pallas_call | solution.py:484
  27.6 0.0 collective-permute-done.3.halo_ref
  27.6 0.1 causal_lower.1
  (1 shorter events, 0.0 us)
Async XLA Ops:
  0.6 6.3 %copy-start = (bf16[2048,2880]{0,1:T(8,128)(2,1)S(1)}, bf16[2048,2880]{0,1:T(8,128)(2,1)}, u32[]{:S(2)}) copy-start(bf16[2048,2880]{0,1:T(8,128)(2,1)} %param.12) | copy-start | bytes 35389444
  1.7 10.5 %collective-permute-start = (bf16[128,512]{1,0:T(8,128)(2,1)S(1)}, bf16[128,512]{1,0:T(8,128)(2,1)S(1)}, u32[]{:S(2)}, u32[]{:S(2)}) collective-permute-start(bf16[128,512]{1,0:T(8,128)(2,1)S(1)} %pack.1), channel_id=1, source_target_pairs={{0,2},{2,4},{4,6},{6,8},{8,10},{10,12},{12,14},{14,16},{16,18},{18... | collective-permute-start | bytes 393224 | tf_op jit(solution)/shard_map/ppermute | solution.py:47
  11.3 4.3 %collective-permute-start.2 = (bf16[2880,128]{1,0:T(8,128)(2,1)S(1)}, bf16[2880,128]{1,0:T(8,128)(2,1)S(1)}, u32[]{:S(2)}, u32[]{:S(2)}) collective-permute-start(bf16[2880,128]{1,0:T(8,128)(2,1)S(1)} %get-tuple-element.30.own_ref), channel_id=1, source_target_pairs={{0,1},{1,0},{2,3},{3,2},{4,5},{5,4},{6,7},{7,6},{8,9},{9,8},{10,11... | collective-permute-start | bytes 2211848 | tf_op jit(solution)/shard_map/ppermute | solution.py:52
  12.2 7.2 %slice-start = ((s8[11796480]{0:T(1024)(128)(4,1)}), s8[4194304]{0:T(1024)(128)(4,1)S(1)}, s32[]{:S(2)}) async-start(s8[11796480]{0:T(1024)(128)(4,1)} %bitcast.4), calls=%async_computation | async-start | bytes 8388608
  12.2 7.2 %slice-start.1 = ((s8[11796480]{0:T(1024)(128)(4,1)}), s8[4194304]{0:T(1024)(128)(4,1)S(1)}, s32[]{:S(2)}) async-start(s8[11796480]{0:T(1024)(128)(4,1)} %bitcast.4), calls=%async_computation.1 | async-start | bytes 8388608
  12.2 7.2 %slice-start.2 = ((s8[11796480]{0:T(1024)(128)(4,1)}), s8[3407872]{0:T(1024)(128)(4,1)S(1)}, s32[]{:S(2)}) async-start(s8[11796480]{0:T(1024)(128)(4,1)} %bitcast.4), calls=%async_computation.2 | async-start | bytes 6815744
  15.5 4.0 %collective-permute-start.1 = (bf16[2880,128]{1,0:T(8,128)(2,1)S(1)}, bf16[2880,128]{1,0:T(8,128)(2,1)S(1)}, u32[]{:S(2)}, u32[]{:S(2)}) collective-permute-start(bf16[2880,128]{1,0:T(8,128)(2,1)S(1)} %get-tuple-element.27.own_ref), channel_id=1, source_target_pairs={{0,1},{1,0},{2,3},{3,2},{4,5},{5,4},{6,7},{7,6},{8,9},{9,8},{10,11... | collective-permute-start | bytes 2211848 | tf_op jit(solution)/shard_map/ppermute | solution.py:52
  16.9 10.8 %collective-permute-start.3 = (bf16[128,512]{1,0:T(8,128)(2,1)S(1)}, bf16[128,512]{1,0:T(8,128)(2,1)S(1)}, u32[]{:S(2)}, u32[]{:S(2)}) collective-permute-start(bf16[128,512]{1,0:T(8,128)(2,1)S(1)} %get-tuple-element.33.kv_up_ref), channel_id=1, source_target_pairs={{0,2},{2,4},{4,6},{6,8},{8,10},{10,12},{12,14},{14,16},{16,18},{18... | collective-permute-start | bytes 393224 | tf_op jit(solution)/shard_map/ppermute | solution.py:47

commit v13 on v12

--- a/solution.py
+++ b/solution.py
@@ -288,17 +288,17 @@
     width, rows = own_ref.shape
     head = lax.axis_index("head")
 
-    def add(c, squares):
-        part = pl.ds(pl.multiple_of(c * chunk, 16), chunk)
+    partial = jnp.zeros((8, rows), F32)
+    for first in range(0, width, chunk):
+        part = slice(first, first + chunk)
         total = own_ref[part, :].astype(F32) + other_ref[part, :].astype(F32)
         sum_s[part, :] = total
         rounded = total.astype(BF16)
         if keep_ref is not None:
             rounded = jnp.where(head == 0, rounded, keep_ref[part, :])
         branch_ref[part, :] = rounded
-        return squares + jnp.sum(total * total, axis=0, keepdims=True)
-
-    squares = lax.fori_loop(0, width // chunk, add, jnp.zeros((1, rows), F32))
+        partial += jnp.sum((total * total).reshape(chunk // 8, 8, rows), axis=0)
+    squares = jnp.sum(partial, axis=0, keepdims=True)
     factor = lax.rsqrt(squares * (1.0 / width) + 1e-05)
     for first in range(0, width, LANES):
         last = min(first + LANES, width)

time: 28.1 us -> 27.6 us (0.982)
  Pallas kernels: 20.5 us -> 20 us
where the time goes in v13:
time: 27.6 us; the launch traced here: 27.5 us
  Pallas kernels  20 us (72%)
  starting transfers between devices  5.66 us (21%)
  between operations  0.91 us (3%)
  waiting for transfers between devices  0.84 us (3%)
    pallas_call x1, Pallas kernels, local(): pl.pallas_call(functools.partial(causal_upper_kernel, chunk=192), out_sha...  7.98 us
    ppermute x2, starting transfers between devices, shifted(): return lax.ppermute(block, axis, [(i, (i + 1) % size) for i in range(size)])  5.52 us
    pallas_call x1, Pallas kernels, local(): pl.pallas_call(functools.partial(project_upper_kernel, chunk=chunk), out_...  4.3 us
    pallas_call x1, Pallas kernels, local(): pl.pallas_call(functools.partial(window_lower_kernel, chunk=chunk), out_s...  3.28 us
    pallas_call x1, Pallas kernels, local(): pl.pallas_call(window_upper_kernel, out_shape=(attn_s, pltpu.VMEM((rows,...  2.25 us
    pallas_call x1, Pallas kernels, local(): pl.pallas_call(functools.partial(norm_upper_kernel, chunk=192), out_shape...  1.09 us
    pallas_call x1, Pallas kernels, local(): pl.pallas_call(pack_kernel, out_shape=jax.ShapeDtypeStruct((half, 2 * kv_...  1.04 us
    ppermute x2, waiting for transfers between devices, shifted(): return lax.ppermute(block, axis, [(i, (i + 1) % size) for i in range(size)])  0.84 us
  transfers between devices with their start and end apart: 4, of which 1 were waited for; matrix products, arithmetic and copies ran while one was open for 0% of the time, Pallas kernels for 69%

profile of v13, /device:TPU:0, one launch (start us, length us, event | category | flops | bytes accessed | tf_op | source)
XLA Modules:
  0.0 27.5 jit_solution(3495245722951416579)
XLA Ops:
  0.6 0.0 copy-start
  0.6 1.0 %pack.1 = bf16[128,512]{1,0:T(8,128)(2,1)S(1)} custom-call(bf16[256,256]{1,0:T(8,128)(2,1)} %k_ref.3, bf16[256,256]{1,0:T(8,128)(2,1)} %v_ref.3), custom_call_target="tpu_custom_call" | custom-call | flops 10000000000 | bytes 1000000 | tf_op jit(solution)/shard_map/pack/pallas_call | solution.py:414
  1.7 3.0 %collective-permute-start = (bf16[128,512]{1,0:T(8,128)(2,1)S(1)}, bf16[128,512]{1,0:T(8,128)(2,1)S(1)}, u32[]{:S(2)}, u32[]{:S(2)}) collective-permute-start(bf16[128,512]{1,0:T(8,128)(2,1)S(1)} %pack.1), channel_id=1, source_target_pairs={{0,2},{2,4},{4,6},{6,8},{8,10},{10,12},{12,14},{14,16},{16,18},{18... | collective-permute-start | bytes 393224 | tf_op jit(solution)/shard_map/ppermute | solution.py:47
  4.7 2.2 %window_upper.1 = (bf16[2048,128]{1,0:T(8,128)(2,1)S(1)}, bf16[256,2048]{1,0:T(8,128)(2,1)S(1)}, bf16[256,256]{1,0:T(8,128)(2,1)S(1)}, bf16[256,256]{1,0:T(8,128...) custom-call(s32[32]{0:T(128)} %lengths_ref.1, ...), custom_call_target="tpu_custom_call" | custom-call | tf_op jit(solution)/shard_map/window_upper/pallas_call | solution.py:428
  6.9 0.0 copy-done
  6.9 4.3 %project_upper.1 = (bf16[2880,128]{1,0:T(8,128)(2,1)S(1)}, bf16[2048,128]{1,0:T(8,128)(2,1)S(1)}) custom-call(bf16[2880,2048]{1,0:T(8,128)(2,1)S(1)} %bitcast.2, bf16[2048,128]{1,0:T(8,128)(2,1)S(1)} %get-tuple-element.25.attn_ref, bf16[256,2048]{1,0:T(8,128)(2,1)S(1)} %get-tuple-element.21.q_ref, bf16[256,256]{1,0:T(8,128)(2,1)S(1)} %get-tuple-element.22.k_ref, ...), custom_call_target="tpu_custom_call" | custom-call | tf_op jit(solution)/shard_map/project_upper/pallas_call | solution.py:449
  11.3 0.1 collective-permute-start.2
  11.3 0.8 %collective-permute-done.halo_ref = bf16[128,512]{1,0:T(8,128)(2,1)S(1)} collective-permute-done((bf16[128,512]{1,0:T(8,128)(2,1)S(1)}, bf16[128,512]{1,0:T(8,128)(2,1)S(1)}, u32[]{:S(2)}, u32[]{:S(2)}) %collective-permute-start) | collective-permute-done | bytes 131104 | tf_op jit(solution)/shard_map/ppermute | solution.py:47
  12.2 0.0 slice-start
  12.2 0.0 slice-start.1
  12.2 0.0 slice-start.2
  12.2 3.3 %window_lower.1 = (bf16[2880,128]{1,0:T(8,128)(2,1)S(1)}, bf16[2880,512]{1,0:T(8,128)(2,1)S(1)}) custom-call(bf16[256,2048]{1,0:T(8,128)(2,1)S(1)} %get-tuple-element.21.q_ref, bf16[256,256]{1,0:T(8,128)(2,1)S(1)} %get-tuple-element.22.k_ref, bf16[256,256]{1,0:T(8,128)(2,1)S(1)} %get-tuple-element.23.v_ref, ...), custom_call_target="tpu_custom_call" | custom-call | tf_op jit(solution)/shard_map/window_lower/pallas_call | solution.py:460
  15.5 0.1 collective-permute-start.1
  15.5 0.0 collective-permute-done.2.other_ref
  15.6 1.1 %norm_upper.1 = (bf16[2880,128]{1,0:T(8,128)(2,1)S(1)}, bf16[128,2880]{1,0:T(8,128)(2,1)S(1)}, bf16[128,512]{1,0:T(8,128)(2,1)S(1)}) custom-call(bf16[2880,128]{1,0:T(8,128)(2,1)S(1)} %get-tuple-element.30.own_ref, bf16[2880,128]{1,0:T(8,128)(2,1)S(1)} %collective-permute-done.2.other_ref, f32[2880]{0:T(1024)S(1)} %get-tuple-element.28.gain_ref, ...), custom_call_target="tpu_custom_call" | custom-call | tf_op jit(solution)/shard_map/norm_upper/pallas_call | solution.py:470
  16.7 2.5 %collective-permute-start.3 = (bf16[128,512]{1,0:T(8,128)(2,1)S(1)}, bf16[128,512]{1,0:T(8,128)(2,1)S(1)}, u32[]{:S(2)}, u32[]{:S(2)}) collective-permute-start(bf16[128,512]{1,0:T(8,128)(2,1)S(1)} %get-tuple-element.33.kv_up_ref), channel_id=1, source_target_pairs={{0,2},{2,4},{4,6},{6,8},{8,10},{10,12},{12,14},{14,16},{16,18},{18... | collective-permute-start | bytes 393224 | tf_op jit(solution)/shard_map/ppermute | solution.py:47
  19.2 0.0 collective-permute-done.1.other_ref
  19.2 0.0 slice-done
  19.2 0.0 slice-done.1
  19.2 0.0 slice-done.2
  19.2 8.0 %causal_upper.1 = (bf16[2880,128]{1,0:T(8,128)(2,1)}, bf16[128,2048]{1,0:T(8,128)(2,1)S(1)}, bf16[128,512]{1,0:T(8,128)(2,1)S(1)}, bf16[256,2048]{1,0:T(8,128)(2,1)}) custom-call(bf16[2880,128]{1,0:T(8,128)(2,1)S(1)} %get-tuple-element.27.own_ref, bf16[2880,128]{1,0:T(8,128)(2,1)S(1)} %collective-permute-done.1.other_ref, ...), custom_call_target="tpu_custom_call" | custom-call | tf_op jit(solution)/shard_map/causal_upper/pallas_call | solution.py:484
  27.2 0.0 collective-permute-done.3.halo_ref
  27.2 0.1 causal_lower.1
  (1 shorter events, 0.0 us)
Async XLA Ops:
  0.6 6.3 %copy-start = (bf16[2048,2880]{0,1:T(8,128)(2,1)S(1)}, bf16[2048,2880]{0,1:T(8,128)(2,1)}, u32[]{:S(2)}) copy-start(bf16[2048,2880]{0,1:T(8,128)(2,1)} %param.12) | copy-start | bytes 35389444
  1.7 10.5 %collective-permute-start = (bf16[128,512]{1,0:T(8,128)(2,1)S(1)}, bf16[128,512]{1,0:T(8,128)(2,1)S(1)}, u32[]{:S(2)}, u32[]{:S(2)}) collective-permute-start(bf16[128,512]{1,0:T(8,128)(2,1)S(1)} %pack.1), channel_id=1, source_target_pairs={{0,2},{2,4},{4,6},{6,8},{8,10},{10,12},{12,14},{14,16},{16,18},{18... | collective-permute-start | bytes 393224 | tf_op jit(solution)/shard_map/ppermute | solution.py:47
  11.3 4.3 %collective-permute-start.2 = (bf16[2880,128]{1,0:T(8,128)(2,1)S(1)}, bf16[2880,128]{1,0:T(8,128)(2,1)S(1)}, u32[]{:S(2)}, u32[]{:S(2)}) collective-permute-start(bf16[2880,128]{1,0:T(8,128)(2,1)S(1)} %get-tuple-element.30.own_ref), channel_id=1, source_target_pairs={{0,1},{1,0},{2,3},{3,2},{4,5},{5,4},{6,7},{7,6},{8,9},{9,8},{10,11... | collective-permute-start | bytes 2211848 | tf_op jit(solution)/shard_map/ppermute | solution.py:52
  12.2 7.0 %slice-start = ((s8[11796480]{0:T(1024)(128)(4,1)}), s8[4194304]{0:T(1024)(128)(4,1)S(1)}, s32[]{:S(2)}) async-start(s8[11796480]{0:T(1024)(128)(4,1)} %bitcast.4), calls=%async_computation | async-start | bytes 8388608
  12.2 7.0 %slice-start.1 = ((s8[11796480]{0:T(1024)(128)(4,1)}), s8[4194304]{0:T(1024)(128)(4,1)S(1)}, s32[]{:S(2)}) async-start(s8[11796480]{0:T(1024)(128)(4,1)} %bitcast.4), calls=%async_computation.1 | async-start | bytes 8388608
  12.2 7.0 %slice-start.2 = ((s8[11796480]{0:T(1024)(128)(4,1)}), s8[3407872]{0:T(1024)(128)(4,1)S(1)}, s32[]{:S(2)}) async-start(s8[11796480]{0:T(1024)(128)(4,1)} %bitcast.4), calls=%async_computation.2 | async-start | bytes 6815744
  15.5 3.7 %collective-permute-start.1 = (bf16[2880,128]{1,0:T(8,128)(2,1)S(1)}, bf16[2880,128]{1,0:T(8,128)(2,1)S(1)}, u32[]{:S(2)}, u32[]{:S(2)}) collective-permute-start(bf16[2880,128]{1,0:T(8,128)(2,1)S(1)} %get-tuple-element.27.own_ref), channel_id=1, source_target_pairs={{0,1},{1,0},{2,3},{3,2},{4,5},{5,4},{6,7},{7,6},{8,9},{9,8},{10,11... | collective-permute-start | bytes 2211848 | tf_op jit(solution)/shard_map/ppermute | solution.py:52
  16.7 10.6 %collective-permute-start.3 = (bf16[128,512]{1,0:T(8,128)(2,1)S(1)}, bf16[128,512]{1,0:T(8,128)(2,1)S(1)}, u32[]{:S(2)}, u32[]{:S(2)}) collective-permute-start(bf16[128,512]{1,0:T(8,128)(2,1)S(1)} %get-tuple-element.33.kv_up_ref), channel_id=1, source_target_pairs={{0,2},{2,4},{4,6},{6,8},{8,10},{10,12},{12,14},{14,16},{16,18},{18... | collective-permute-start | bytes 393224 | tf_op jit(solution)/shard_map/ppermute | solution.py:47

commit v14 on v13

--- a/solution.py
+++ b/solution.py
@@ -77,7 +77,7 @@
 
 
 def stage_keys(keys, keys_ref):
-    scaled = (keys.astype(F32) * HD ** (-0.5)).astype(BF16)
+    scaled = keys * jnp.asarray(HD ** (-0.5), BF16)
     lane = lax.broadcasted_iota(jnp.int32, (keys.shape[0], LANES), 1)
     zero = jnp.zeros((keys.shape[0], LANES), BF16)
     for pair in range(keys.shape[1] // LANES):

time: 27.6 us -> 27.6 us (level)
  no operation moved by 1% of the time
where the time goes in v14:
time: 27.6 us; the launch traced here: 27.4 us
  Pallas kernels  20 us (72%)
  starting transfers between devices  5.66 us (21%)
  between operations  0.91 us (3%)
  waiting for transfers between devices  0.85 us (3%)
    pallas_call x1, Pallas kernels, local(): pl.pallas_call(functools.partial(causal_upper_kernel, chunk=192), out_sha...  7.95 us
    ppermute x2, starting transfers between devices, shifted(): return lax.ppermute(block, axis, [(i, (i + 1) % size) for i in range(size)])  5.52 us
    pallas_call x1, Pallas kernels, local(): pl.pallas_call(functools.partial(project_upper_kernel, chunk=chunk), out_...  4.3 us
    pallas_call x1, Pallas kernels, local(): pl.pallas_call(functools.partial(window_lower_kernel, chunk=chunk), out_s...  3.28 us
    pallas_call x1, Pallas kernels, local(): pl.pallas_call(window_upper_kernel, out_shape=(attn_s, pltpu.VMEM((rows,...  2.25 us
    pallas_call x1, Pallas kernels, local(): pl.pallas_call(functools.partial(norm_upper_kernel, chunk=192), out_shape...  1.09 us
    pallas_call x1, Pallas kernels, local(): pl.pallas_call(pack_kernel, out_shape=jax.ShapeDtypeStruct((half, 2 * kv_...  1.04 us
    ppermute x2, waiting for transfers between devices, shifted(): return lax.ppermute(block, axis, [(i, (i + 1) % size) for i in range(size)])  0.84 us
  transfers between devices with their start and end apart: 4, of which 1 were waited for; matrix products, arithmetic and copies ran while one was open for 0% of the time, Pallas kernels for 69%

profile of v14, /device:TPU:0, one launch (start us, length us, event | category | flops | bytes accessed | tf_op | source)
XLA Modules:
  0.0 27.4 jit_solution(383386751898571245)
XLA Ops:
  0.6 0.0 copy-start
  0.6 1.0 %pack.1 = bf16[128,512]{1,0:T(8,128)(2,1)S(1)} custom-call(bf16[256,256]{1,0:T(8,128)(2,1)} %k_ref.3, bf16[256,256]{1,0:T(8,128)(2,1)} %v_ref.3), custom_call_target="tpu_custom_call" | custom-call | flops 10000000000 | bytes 1000000 | tf_op jit(solution)/shard_map/pack/pallas_call | solution.py:414
  1.7 3.0 %collective-permute-start = (bf16[128,512]{1,0:T(8,128)(2,1)S(1)}, bf16[128,512]{1,0:T(8,128)(2,1)S(1)}, u32[]{:S(2)}, u32[]{:S(2)}) collective-permute-start(bf16[128,512]{1,0:T(8,128)(2,1)S(1)} %pack.1), channel_id=1, source_target_pairs={{0,2},{2,4},{4,6},{6,8},{8,10},{10,12},{12,14},{14,16},{16,18},{18... | collective-permute-start | bytes 393224 | tf_op jit(solution)/shard_map/ppermute | solution.py:47
  4.7 2.2 %window_upper.1 = (bf16[2048,128]{1,0:T(8,128)(2,1)S(1)}, bf16[256,2048]{1,0:T(8,128)(2,1)S(1)}, bf16[256,256]{1,0:T(8,128)(2,1)S(1)}, bf16[256,256]{1,0:T(8,128...) custom-call(s32[32]{0:T(128)} %lengths_ref.1, ...), custom_call_target="tpu_custom_call" | custom-call | tf_op jit(solution)/shard_map/window_upper/pallas_call | solution.py:428
  6.9 0.0 copy-done
  6.9 4.3 %project_upper.1 = (bf16[2880,128]{1,0:T(8,128)(2,1)S(1)}, bf16[2048,128]{1,0:T(8,128)(2,1)S(1)}) custom-call(bf16[2880,2048]{1,0:T(8,128)(2,1)S(1)} %bitcast.2, bf16[2048,128]{1,0:T(8,128)(2,1)S(1)} %get-tuple-element.25.attn_ref, bf16[256,2048]{1,0:T(8,128)(2,1)S(1)} %get-tuple-element.21.q_ref, bf16[256,256]{1,0:T(8,128)(2,1)S(1)} %get-tuple-element.22.k_ref, ...), custom_call_target="tpu_custom_call" | custom-call | tf_op jit(solution)/shard_map/project_upper/pallas_call | solution.py:449
  11.3 0.1 collective-permute-start.2
  11.3 0.8 %collective-permute-done.halo_ref = bf16[128,512]{1,0:T(8,128)(2,1)S(1)} collective-permute-done((bf16[128,512]{1,0:T(8,128)(2,1)S(1)}, bf16[128,512]{1,0:T(8,128)(2,1)S(1)}, u32[]{:S(2)}, u32[]{:S(2)}) %collective-permute-start) | collective-permute-done | bytes 131104 | tf_op jit(solution)/shard_map/ppermute | solution.py:47
  12.2 0.0 slice-start
  12.2 0.0 slice-start.1
  12.2 0.0 slice-start.2
  12.2 3.3 %window_lower.1 = (bf16[2880,128]{1,0:T(8,128)(2,1)S(1)}, bf16[2880,512]{1,0:T(8,128)(2,1)S(1)}) custom-call(bf16[256,2048]{1,0:T(8,128)(2,1)S(1)} %get-tuple-element.21.q_ref, bf16[256,256]{1,0:T(8,128)(2,1)S(1)} %get-tuple-element.22.k_ref, bf16[256,256]{1,0:T(8,128)(2,1)S(1)} %get-tuple-element.23.v_ref, ...), custom_call_target="tpu_custom_call" | custom-call | tf_op jit(solution)/shard_map/window_lower/pallas_call | solution.py:460
  15.5 0.1 collective-permute-start.1
  15.5 0.0 collective-permute-done.2.other_ref
  15.6 1.1 %norm_upper.1 = (bf16[2880,128]{1,0:T(8,128)(2,1)S(1)}, bf16[128,2880]{1,0:T(8,128)(2,1)S(1)}, bf16[128,512]{1,0:T(8,128)(2,1)S(1)}) custom-call(bf16[2880,128]{1,0:T(8,128)(2,1)S(1)} %get-tuple-element.30.own_ref, bf16[2880,128]{1,0:T(8,128)(2,1)S(1)} %collective-permute-done.2.other_ref, f32[2880]{0:T(1024)S(1)} %get-tuple-element.28.gain_ref, ...), custom_call_target="tpu_custom_call" | custom-call | tf_op jit(solution)/shard_map/norm_upper/pallas_call | solution.py:470
  16.7 2.5 %collective-permute-start.3 = (bf16[128,512]{1,0:T(8,128)(2,1)S(1)}, bf16[128,512]{1,0:T(8,128)(2,1)S(1)}, u32[]{:S(2)}, u32[]{:S(2)}) collective-permute-start(bf16[128,512]{1,0:T(8,128)(2,1)S(1)} %get-tuple-element.33.kv_up_ref), channel_id=1, source_target_pairs={{0,2},{2,4},{4,6},{6,8},{8,10},{10,12},{12,14},{14,16},{16,18},{18... | collective-permute-start | bytes 393224 | tf_op jit(solution)/shard_map/ppermute | solution.py:47
  19.2 0.0 collective-permute-done.1.other_ref
  19.2 0.0 slice-done
  19.2 0.0 slice-done.1
  19.2 0.0 slice-done.2
  19.2 8.0 %causal_upper.1 = (bf16[2880,128]{1,0:T(8,128)(2,1)}, bf16[128,2048]{1,0:T(8,128)(2,1)S(1)}, bf16[128,512]{1,0:T(8,128)(2,1)S(1)}, bf16[256,2048]{1,0:T(8,128)(2,1)}) custom-call(bf16[2880,128]{1,0:T(8,128)(2,1)S(1)} %get-tuple-element.27.own_ref, bf16[2880,128]{1,0:T(8,128)(2,1)S(1)} %collective-permute-done.1.other_ref, ...), custom_call_target="tpu_custom_call" | custom-call | tf_op jit(solution)/shard_map/causal_upper/pallas_call | solution.py:484
  27.2 0.0 collective-permute-done.3.halo_ref
  27.2 0.1 causal_lower.1
  (1 shorter events, 0.0 us)
Async XLA Ops:
  0.6 6.3 %copy-start = (bf16[2048,2880]{0,1:T(8,128)(2,1)S(1)}, bf16[2048,2880]{0,1:T(8,128)(2,1)}, u32[]{:S(2)}) copy-start(bf16[2048,2880]{0,1:T(8,128)(2,1)} %param.12) | copy-start | bytes 35389444
  1.7 10.5 %collective-permute-start = (bf16[128,512]{1,0:T(8,128)(2,1)S(1)}, bf16[128,512]{1,0:T(8,128)(2,1)S(1)}, u32[]{:S(2)}, u32[]{:S(2)}) collective-permute-start(bf16[128,512]{1,0:T(8,128)(2,1)S(1)} %pack.1), channel_id=1, source_target_pairs={{0,2},{2,4},{4,6},{6,8},{8,10},{10,12},{12,14},{14,16},{16,18},{18... | collective-permute-start | bytes 393224 | tf_op jit(solution)/shard_map/ppermute | solution.py:47
  11.3 4.3 %collective-permute-start.2 = (bf16[2880,128]{1,0:T(8,128)(2,1)S(1)}, bf16[2880,128]{1,0:T(8,128)(2,1)S(1)}, u32[]{:S(2)}, u32[]{:S(2)}) collective-permute-start(bf16[2880,128]{1,0:T(8,128)(2,1)S(1)} %get-tuple-element.30.own_ref), channel_id=1, source_target_pairs={{0,1},{1,0},{2,3},{3,2},{4,5},{5,4},{6,7},{7,6},{8,9},{9,8},{10,11... | collective-permute-start | bytes 2211848 | tf_op jit(solution)/shard_map/ppermute | solution.py:52
  12.2 7.0 %slice-start = ((s8[11796480]{0:T(1024)(128)(4,1)}), s8[4194304]{0:T(1024)(128)(4,1)S(1)}, s32[]{:S(2)}) async-start(s8[11796480]{0:T(1024)(128)(4,1)} %bitcast.4), calls=%async_computation | async-start | bytes 8388608
  12.2 7.0 %slice-start.1 = ((s8[11796480]{0:T(1024)(128)(4,1)}), s8[4194304]{0:T(1024)(128)(4,1)S(1)}, s32[]{:S(2)}) async-start(s8[11796480]{0:T(1024)(128)(4,1)} %bitcast.4), calls=%async_computation.1 | async-start | bytes 8388608
  12.2 7.0 %slice-start.2 = ((s8[11796480]{0:T(1024)(128)(4,1)}), s8[3407872]{0:T(1024)(128)(4,1)S(1)}, s32[]{:S(2)}) async-start(s8[11796480]{0:T(1024)(128)(4,1)} %bitcast.4), calls=%async_computation.2 | async-start | bytes 6815744
  15.5 3.7 %collective-permute-start.1 = (bf16[2880,128]{1,0:T(8,128)(2,1)S(1)}, bf16[2880,128]{1,0:T(8,128)(2,1)S(1)}, u32[]{:S(2)}, u32[]{:S(2)}) collective-permute-start(bf16[2880,128]{1,0:T(8,128)(2,1)S(1)} %get-tuple-element.27.own_ref), channel_id=1, source_target_pairs={{0,1},{1,0},{2,3},{3,2},{4,5},{5,4},{6,7},{7,6},{8,9},{9,8},{10,11... | collective-permute-start | bytes 2211848 | tf_op jit(solution)/shard_map/ppermute | solution.py:52
  16.7 10.5 %collective-permute-start.3 = (bf16[128,512]{1,0:T(8,128)(2,1)S(1)}, bf16[128,512]{1,0:T(8,128)(2,1)S(1)}, u32[]{:S(2)}, u32[]{:S(2)}) collective-permute-start(bf16[128,512]{1,0:T(8,128)(2,1)S(1)} %get-tuple-element.33.kv_up_ref), channel_id=1, source_target_pairs={{0,2},{2,4},{4,6},{6,8},{8,10},{10,12},{12,14},{14,16},{16,18},{18... | collective-permute-start | bytes 393224 | tf_op jit(solution)/shard_map/ppermute | solution.py:47
